TPU v7x, 32 devices: a whole 2x2x4 slice. The times are simulated.
32 devices in a mesh: fsdp: 8 (over y, x, core), sp: 4 (over z).
Axes of the slice: x: 2, y: 2, z: 4, core: 2. Of those that a mesh axis runs over, the one named last changes fastest.
Arguments:
- residual_in: float32 [8, 2, 1024, 1152], P('fsdp', None, 'sp'), may hold values from -6 to 6
- condition: float32 [8, 2, 1152], P('fsdp'), may hold values from -6 to 6
- text_states: bfloat16 [8, 2, 120, 4096], P('fsdp', None, 'sp'), may hold values from -6 to 6
- slot_item: int32 [8, 2], P('fsdp'), may hold values from 0 to 1, as said below
- cotangent: bfloat16 [8, 2, 1024, 1152], P('fsdp', None, 'sp'), may hold values from -6 to 6
- w_ada: float32 [1152, 6912], P(('fsdp', 'sp')), may hold values from -0.1875 to 0.1875
- w_qkv: float32 [1152, 3456], P(('fsdp', 'sp')), may hold values from -0.1875 to 0.1875
- w_out: float32 [1152, 1152], P(('fsdp', 'sp')), may hold values from -0.75 to 0.75
- w_cross_q: float32 [1152, 1152], P(('fsdp', 'sp')), may hold values from -0.1875 to 0.1875
- w_cross_kv: float32 [4096, 2304], P(('fsdp', 'sp')), may hold values from -0.09375 to 0.09375
- w_cross_out: float32 [1152, 1152], P(('fsdp', 'sp')), may hold values from -0.5 to 0.5
- w_up: float32 [1152, 4608], P(('fsdp', 'sp')), may hold values from -0.1875 to 0.1875
- w_down: float32 [4608, 1152], P(('fsdp', 'sp')), may hold values from -0.09375 to 0.09375
- w_temp_qkv: float32 [1152, 3456], P(('fsdp', 'sp')), may hold values from -0.1875 to 0.1875
- w_temp_out: float32 [1152, 1152], P(('fsdp', 'sp')), may hold values from -0.25 to 0.25
- g_cross: float32 [1152], P(('fsdp', 'sp')), may hold values from 0.5 to 1.5
- g_temp: float32 [1152], P(('fsdp', 'sp')), may hold values from 0.5 to 1.5
- t_gate: float32 [1152], P(('fsdp', 'sp')), may hold values from 0.5 to 1.5
Outputs:
- output: float32 [8, 2, 1024, 1152], P('fsdp', None, 'sp')
- input_grad: float32 [8, 2, 1024, 1152], P('fsdp', None, 'sp')
- grad_w_ada: float32 [1152, 6912], P(('fsdp', 'sp'))
- grad_w_qkv: float32 [1152, 3456], P(('fsdp', 'sp'))
- grad_w_out: float32 [1152, 1152], P(('fsdp', 'sp'))
- grad_w_cross_q: float32 [1152, 1152], P(('fsdp', 'sp'))
- grad_w_cross_kv: float32 [4096, 2304], P(('fsdp', 'sp'))
- grad_w_cross_out: float32 [1152, 1152], P(('fsdp', 'sp'))
- grad_w_up: float32 [1152, 4608], P(('fsdp', 'sp'))
- grad_w_down: float32 [4608, 1152], P(('fsdp', 'sp'))
- grad_w_temp_qkv: float32 [1152, 3456], P(('fsdp', 'sp'))
- grad_w_temp_out: float32 [1152, 1152], P(('fsdp', 'sp'))
- grad_g_cross: float32 [1152], P(('fsdp', 'sp'))
- grad_g_temp: float32 [1152], P(('fsdp', 'sp'))
- grad_t_gate: float32 [1152], P(('fsdp', 'sp'))
Inputs may be any that keep to these rules, and one draw needn't show every extreme that they name: `slot_item`: each group holds either one video whose 2 frames use slot 0's condition and text (all entries 0) or 2 images (entries 0, 1, ...); group 0 holds a video and group 1 images.
All inputs are finite; a program needn't handle non-finite values.
Results may differ from a plain program's by a relative error of at most 0.022.
Values may be sent and summed in bfloat16 or wider, within the bound.
A program may use at most 512 MiB of HBM per device.

v0:
```python
import jax
import jax.numpy as jnp
from jax import lax
from jax.sharding import PartitionSpec as P

HEADS = 16
HEAD_DIM = 72


epsilon = 1e-06
highest = lax.Precision.HIGHEST


def matmul(left, right):
    return jnp.dot(left, right, preferred_element_type=jnp.float32)


def matmul_tn(left, right):
    return lax.dot_general(
        left, right, (((0,), (0,)), ((), ())), preferred_element_type=jnp.float32
    )


def matmul_nt(left, right):
    return lax.dot_general(
        left, right, (((1,), (1,)), ((), ())), preferred_element_type=jnp.float32
    )


def normalize(values):
    centred = values - jnp.mean(values, axis=-1, keepdims=True)
    return centred * lax.rsqrt(jnp.mean(centred * centred, axis=-1, keepdims=True) + epsilon)


def normalize_back(values, grad_out):
    return jax.vjp(normalize, values)[1](grad_out)[0]


def gelu_tanh(values):
    return jax.nn.gelu(values, approximate=True)


def softmax_back(probs, grad_probs):
    return probs * (grad_probs - jnp.sum(grad_probs * probs, axis=-1, keepdims=True))


def temporal_probs(triple, score_scale):
    scores = (
        jnp.einsum(
            "aphd,bphd->phab", triple[:, :, 0], triple[:, :, 1], preferred_element_type=jnp.float32
        )
        * score_scale
    )
    shifted = jnp.exp(scores - jnp.max(scores, axis=-1, keepdims=True))
    return shifted / jnp.sum(shifted, axis=-1, keepdims=True)


def local(
    residual_in,
    condition,
    text_states,
    slot_item,
    cotangent,
    w_ada,
    w_qkv,
    w_out,
    w_cross_q,
    w_cross_kv,
    w_cross_out,
    w_up,
    w_down,
    w_temp_qkv,
    w_temp_out,
    g_cross,
    g_temp,
    t_gate,
):
    slot_count = residual_in.shape[1]
    patch_local = residual_in.shape[2]
    model_width = residual_in.shape[3]
    text_local = text_states.shape[2]
    text_width = text_states.shape[3]
    sp_count = lax.axis_size("sp")
    head_count = HEADS
    head_size = HEAD_DIM
    heads_local = head_count // sp_count
    patch_total = patch_local * sp_count
    text_total = text_local * sp_count
    tok_rows = slot_count * patch_local
    score_scale = head_size ** (-0.5)
    shard_list = [
        w_ada,
        w_qkv,
        w_out,
        w_cross_q,
        w_cross_kv,
        w_cross_out,
        w_up,
        w_down,
        w_temp_qkv,
        w_temp_out,
        g_cross,
        g_temp,
        t_gate,
    ]
    lowered = [weight_shard.astype(jnp.bfloat16) for weight_shard in shard_list]
    gathered = (
        lax.all_gather(lowered[0], ("fsdp", "sp"), axis=0, tiled=True),
        lax.all_gather(lowered[1], ("fsdp", "sp"), axis=0, tiled=True),
        lax.all_gather(lowered[2], ("fsdp", "sp"), axis=0, tiled=True),
        lax.all_gather(lowered[3], ("fsdp", "sp"), axis=0, tiled=True),
        lax.all_gather(lowered[4], ("fsdp", "sp"), axis=0, tiled=True),
        lax.all_gather(lowered[5], ("fsdp", "sp"), axis=0, tiled=True),
        lax.all_gather(lowered[6], ("fsdp", "sp"), axis=0, tiled=True),
        lax.all_gather(lowered[7], ("fsdp", "sp"), axis=0, tiled=True),
        lax.all_gather(lowered[8], ("fsdp", "sp"), axis=0, tiled=True),
        lax.all_gather(lowered[9], ("fsdp", "sp"), axis=0, tiled=True),
        lax.all_gather(lowered[10], ("fsdp", "sp"), axis=0, tiled=True),
        lax.all_gather(lowered[11], ("fsdp", "sp"), axis=0, tiled=True),
        lax.all_gather(lowered[12], ("fsdp", "sp"), axis=0, tiled=True),
    )
    (
        ada_full,
        qkv_full,
        out_full,
        cross_q_full,
        cross_kv_full,
        cross_out_full,
        up_full,
        down_full,
        temp_qkv_full,
        temp_out_full,
        gain_cross_low,
        gain_temp_low,
        temp_gate_low,
    ) = gathered
    gain_cross = gain_cross_low.astype(jnp.float32)
    gain_temp = gain_temp_low.astype(jnp.float32)
    temp_gate = temp_gate_low.astype(jnp.float32)
    chosen = slot_item[0]
    video = chosen[-1] == 0
    cond_used = jnp.take(condition[0], chosen, axis=0)
    text_used = jnp.take(text_states[0], chosen, axis=0)
    silu_cond = jax.nn.silu(cond_used).astype(jnp.bfloat16)
    modulation = matmul(silu_cond, ada_full).reshape(slot_count, 6, 1, model_width)
    shift_one = modulation[:, 0]
    scale_one = modulation[:, 1]
    gate_one = modulation[:, 2]
    shift_two = modulation[:, 3]
    scale_two = modulation[:, 4]
    gate_two = modulation[:, 5]
    resid = residual_in[0]
    normed_one = normalize(resid)
    h_one = (
        (normed_one * (1.0 + scale_one) + shift_one)
        .astype(jnp.bfloat16)
        .reshape(tok_rows, model_width)
    )
    qkv_tok = (
        matmul(h_one, qkv_full)
        .astype(jnp.bfloat16)
        .reshape(slot_count, patch_local, 3, sp_count, heads_local * head_size)
    )
    qkv_heads = lax.all_to_all(qkv_tok, "sp", split_axis=3, concat_axis=1, tiled=True)
    items = (
        qkv_heads.reshape(slot_count, patch_total, 3, heads_local, head_size)
        .transpose(2, 0, 3, 1, 4)
        .reshape(3, slot_count * heads_local, patch_total, head_size)
    )

    def spatial_item(triple):
        query, key_rows, value_rows = triple
        scores = matmul_nt(query, key_rows) * score_scale
        score_max = jnp.max(scores, axis=-1, keepdims=True)
        log_total = score_max + jnp.log(
            jnp.sum(jnp.exp(scores - score_max), axis=-1, keepdims=True)
        )
        probs = jnp.exp(scores - log_total)
        return (
            matmul(probs.astype(jnp.bfloat16), value_rows).astype(jnp.bfloat16),
            log_total[:, 0],
        )

    attended, log_totals = lax.map(spatial_item, (items[0], items[1], items[2]))
    back_layout = (
        attended.reshape(slot_count, heads_local, patch_total, head_size)
        .transpose(0, 2, 1, 3)
        .reshape(slot_count, sp_count, patch_local, 1, heads_local * head_size)
    )
    attn_tok = lax.all_to_all(back_layout, "sp", split_axis=1, concat_axis=3, tiled=True).reshape(
        tok_rows, model_width
    )
    branch_one = matmul(attn_tok, out_full).reshape(slot_count, patch_local, model_width)
    x_one = resid + gate_one * branch_one
    normed_two = normalize(x_one)
    cross_in = (normed_two * gain_cross).astype(jnp.bfloat16).reshape(tok_rows, model_width)
    query_flat = matmul(cross_in, cross_q_full).astype(jnp.bfloat16)
    query_c = query_flat.reshape(slot_count, patch_local, head_count, head_size)
    text_flat = text_used.reshape(slot_count * text_local, text_width)
    kv_part = (
        matmul(text_flat, cross_kv_full)
        .astype(jnp.bfloat16)
        .reshape(slot_count, text_local, 2 * model_width)
    )
    kv_all = lax.all_gather(kv_part, "sp", axis=1, tiled=True)
    key_c = kv_all[:, :, :model_width].reshape(slot_count, text_total, head_count, head_size)
    value_c = kv_all[:, :, model_width:].reshape(slot_count, text_total, head_count, head_size)
    scores_c = (
        jnp.einsum("sqhd,skhd->shqk", query_c, key_c, preferred_element_type=jnp.float32)
        * score_scale
    )
    max_c = jnp.max(scores_c, axis=-1, keepdims=True)
    log_total_c = max_c + jnp.log(jnp.sum(jnp.exp(scores_c - max_c), axis=-1, keepdims=True))
    probs_c = jnp.exp(scores_c - log_total_c)
    cross_out = (
        jnp.einsum(
            "shqk,skhd->sqhd",
            probs_c.astype(jnp.bfloat16),
            value_c,
            preferred_element_type=jnp.float32,
        )
        .astype(jnp.bfloat16)
        .reshape(tok_rows, model_width)
    )
    branch_two = matmul(cross_out, cross_out_full).reshape(slot_count, patch_local, model_width)
    x_two = x_one + branch_two
    normed_three = normalize(x_two)
    h_three = (
        (normed_three * (1.0 + scale_two) + shift_two)
        .astype(jnp.bfloat16)
        .reshape(tok_rows, model_width)
    )
    up_proj = matmul(h_three, up_full)
    activated = gelu_tanh(up_proj).astype(jnp.bfloat16)
    branch_three = matmul(activated, down_full).reshape(slot_count, patch_local, model_width)
    x_three = x_two + gate_two * branch_three

    def temporal_on(x_now):
        temp_in = (normalize(x_now) * gain_temp).astype(jnp.bfloat16).reshape(tok_rows, model_width)
        temp_trip = (
            matmul(temp_in, temp_qkv_full)
            .astype(jnp.bfloat16)
            .reshape(slot_count, patch_local, 3, head_count, head_size)
        )
        probs_t = temporal_probs(temp_trip, score_scale)
        temp_out = (
            jnp.einsum(
                "phab,bphd->aphd",
                probs_t.astype(jnp.bfloat16),
                temp_trip[:, :, 2],
                preferred_element_type=jnp.float32,
            )
            .astype(jnp.bfloat16)
            .reshape(tok_rows, model_width)
        )
        return (matmul(temp_out, temp_out_full), temp_in, temp_trip, temp_out)

    def temporal_off(x_now):
        return (
            jnp.zeros((tok_rows, model_width), jnp.float32),
            jnp.zeros((tok_rows, model_width), jnp.bfloat16),
            jnp.zeros((slot_count, patch_local, 3, head_count, head_size), jnp.bfloat16),
            jnp.zeros((tok_rows, model_width), jnp.bfloat16),
        )

    branch_four, temp_in, temp_trip, temp_out = lax.cond(video, temporal_on, temporal_off, x_three)
    output = x_three + temp_gate * branch_four.reshape(slot_count, patch_local, model_width)
    regathered = (
        lax.all_gather(lowered[0], ("fsdp", "sp"), axis=0, tiled=True),
        lax.all_gather(lowered[1], ("fsdp", "sp"), axis=0, tiled=True),
        lax.all_gather(lowered[2], ("fsdp", "sp"), axis=0, tiled=True),
        lax.all_gather(lowered[3], ("fsdp", "sp"), axis=0, tiled=True),
        lax.all_gather(lowered[4], ("fsdp", "sp"), axis=0, tiled=True),
        lax.all_gather(lowered[5], ("fsdp", "sp"), axis=0, tiled=True),
        lax.all_gather(lowered[6], ("fsdp", "sp"), axis=0, tiled=True),
        lax.all_gather(lowered[7], ("fsdp", "sp"), axis=0, tiled=True),
        lax.all_gather(lowered[8], ("fsdp", "sp"), axis=0, tiled=True),
        lax.all_gather(lowered[9], ("fsdp", "sp"), axis=0, tiled=True),
        lax.all_gather(lowered[10], ("fsdp", "sp"), axis=0, tiled=True),
        lax.all_gather(lowered[11], ("fsdp", "sp"), axis=0, tiled=True),
        lax.all_gather(lowered[12], ("fsdp", "sp"), axis=0, tiled=True),
    )
    (
        ada_back,
        qkv_back,
        out_back,
        cross_q_back,
        cross_kv_back,
        cross_out_back,
        up_back,
        down_back,
        temp_qkv_back,
        temp_out_back,
        gain_cross_back,
        gain_temp_back,
        temp_gate_back,
    ) = regathered
    gain_cross_b = gain_cross_back.astype(jnp.float32)
    gain_temp_b = gain_temp_back.astype(jnp.float32)
    temp_gate_b = temp_gate_back.astype(jnp.float32)
    grad_out = cotangent[0].astype(jnp.float32)
    grad_flat = grad_out.reshape(tok_rows, model_width)

    def temporal_grad_on(operands):
        grad_now, x_now, branch_now, temp_in_now, trip_now, temp_out_now = operands
        grad_tgate = jnp.sum(grad_now * branch_now, axis=0)
        grad_branch = (grad_now * temp_gate_b).astype(jnp.bfloat16)
        grad_wto = matmul_tn(temp_out_now, grad_branch)
        grad_temp_out = (
            matmul_nt(grad_branch, temp_out_back)
            .astype(jnp.bfloat16)
            .reshape(slot_count, patch_local, head_count, head_size)
        )
        probs_t = temporal_probs(trip_now, score_scale)
        grad_probs = jnp.einsum(
            "aphd,bphd->phab", grad_temp_out, trip_now[:, :, 2], preferred_element_type=jnp.float32
        )
        grad_value = jnp.einsum(
            "phab,aphd->bphd",
            probs_t.astype(jnp.bfloat16),
            grad_temp_out,
            preferred_element_type=jnp.float32,
        )
        grad_scores = softmax_back(probs_t, grad_probs).astype(jnp.bfloat16)
        grad_query = (
            jnp.einsum(
                "phab,bphd->aphd",
                grad_scores,
                trip_now[:, :, 1],
                preferred_element_type=jnp.float32,
            )
            * score_scale
        )
        grad_key = (
            jnp.einsum(
                "phab,aphd->bphd",
                grad_scores,
                trip_now[:, :, 0],
                preferred_element_type=jnp.float32,
            )
            * score_scale
        )
        grad_trip = (
            jnp.stack([grad_query, grad_key, grad_value], axis=2)
            .astype(jnp.bfloat16)
            .reshape(tok_rows, 3 * model_width)
        )
        grad_wtq = matmul_tn(temp_in_now, grad_trip)
        grad_temp_in = matmul_nt(grad_trip, temp_qkv_back).reshape(
            slot_count, patch_local, model_width
        )
        grad_gtemp = jnp.sum(grad_temp_in * normalize(x_now), axis=(0, 1))
        grad_x_now = normalize_back(x_now, grad_temp_in * gain_temp_b)
        return (grad_x_now, grad_wtq, grad_wto, grad_gtemp, grad_tgate)

    def temporal_grad_off(operands):
        return (
            jnp.zeros((slot_count, patch_local, model_width), jnp.float32),
            jnp.zeros((model_width, 3 * model_width), jnp.float32),
            jnp.zeros((model_width, model_width), jnp.float32),
            jnp.zeros((model_width,), jnp.float32),
            jnp.zeros((model_width,), jnp.float32),
        )

    extra_three, grad_wtq, grad_wto, grad_gtemp, grad_tgate = lax.cond(
        video,
        temporal_grad_on,
        temporal_grad_off,
        (grad_flat, x_three, branch_four, temp_in, temp_trip, temp_out),
    )
    grad_three = grad_out + extra_three
    grad_gate_two = jnp.sum(grad_three * branch_three, axis=1)
    grad_branch_three = (grad_three * gate_two).astype(jnp.bfloat16).reshape(tok_rows, model_width)
    grad_wdown = matmul_tn(activated, grad_branch_three)
    grad_activated = matmul_nt(grad_branch_three, down_back)
    grad_up = jax.vjp(gelu_tanh, up_proj)[1](grad_activated)[0].astype(jnp.bfloat16)
    grad_wup = matmul_tn(h_three, grad_up)
    grad_h_three = matmul_nt(grad_up, up_back).reshape(slot_count, patch_local, model_width)
    grad_shift_two = jnp.sum(grad_h_three, axis=1)
    grad_scale_two = jnp.sum(grad_h_three * normed_three, axis=1)
    grad_two = grad_three + normalize_back(x_two, grad_h_three * (1.0 + scale_two))
    grad_branch_two = grad_two.astype(jnp.bfloat16).reshape(tok_rows, model_width)
    grad_wco = matmul_tn(cross_out, grad_branch_two)
    grad_cross_out = (
        matmul_nt(grad_branch_two, cross_out_back)
        .astype(jnp.bfloat16)
        .reshape(slot_count, patch_local, head_count, head_size)
    )
    grad_probs_c = jnp.einsum(
        "sqhd,skhd->shqk", grad_cross_out, value_c, preferred_element_type=jnp.float32
    )
    grad_value_c = jnp.einsum(
        "shqk,sqhd->skhd",
        probs_c.astype(jnp.bfloat16),
        grad_cross_out,
        preferred_element_type=jnp.float32,
    )
    grad_scores_c = softmax_back(probs_c, grad_probs_c).astype(jnp.bfloat16)
    grad_query_c = (
        (
            jnp.einsum("shqk,skhd->sqhd", grad_scores_c, key_c, preferred_element_type=jnp.float32)
            * score_scale
        )
        .astype(jnp.bfloat16)
        .reshape(tok_rows, model_width)
    )
    grad_key_c = (
        jnp.einsum("shqk,sqhd->skhd", grad_scores_c, query_c, preferred_element_type=jnp.float32)
        * score_scale
    )
    grad_kv_all = jnp.concatenate(
        [
            grad_key_c.reshape(slot_count, text_total, model_width),
            grad_value_c.reshape(slot_count, text_total, model_width),
        ],
        axis=-1,
    )
    grad_kv_part = lax.psum_scatter(
        grad_kv_all.astype(jnp.bfloat16), "sp", scatter_dimension=1, tiled=True
    ).reshape(slot_count * text_local, 2 * model_width)
    grad_wckv = matmul_tn(text_flat, grad_kv_part)
    grad_wcq = matmul_tn(cross_in, grad_query_c)
    grad_cross_in = matmul_nt(grad_query_c, cross_q_back).reshape(
        slot_count, patch_local, model_width
    )
    grad_gcross = jnp.sum(grad_cross_in * normed_two, axis=(0, 1))
    grad_one = grad_two + normalize_back(x_one, grad_cross_in * gain_cross_b)
    late_sums = (
        lax.psum_scatter(grad_wcq, ("fsdp", "sp"), scatter_dimension=0, tiled=True),
        lax.psum_scatter(grad_wco, ("fsdp", "sp"), scatter_dimension=0, tiled=True),
        lax.psum_scatter(grad_wup, ("fsdp", "sp"), scatter_dimension=0, tiled=True),
        lax.psum_scatter(grad_wdown, ("fsdp", "sp"), scatter_dimension=0, tiled=True),
        lax.psum_scatter(grad_wtq, ("fsdp", "sp"), scatter_dimension=0, tiled=True),
        lax.psum_scatter(grad_wto, ("fsdp", "sp"), scatter_dimension=0, tiled=True),
        lax.psum_scatter(grad_gcross, ("fsdp", "sp"), scatter_dimension=0, tiled=True),
        lax.psum_scatter(grad_gtemp, ("fsdp", "sp"), scatter_dimension=0, tiled=True),
        lax.psum_scatter(grad_tgate, ("fsdp", "sp"), scatter_dimension=0, tiled=True),
    )
    grad_gate_one = jnp.sum(grad_one * branch_one, axis=1)
    grad_branch_one = (grad_one * gate_one).astype(jnp.bfloat16).reshape(tok_rows, model_width)
    grad_wout = matmul_tn(attn_tok, grad_branch_one)
    grad_attn = (
        matmul_nt(grad_branch_one, out_back)
        .astype(jnp.bfloat16)
        .reshape(slot_count, patch_local, sp_count, heads_local * head_size)
    )
    grad_attn_heads = lax.all_to_all(grad_attn, "sp", split_axis=2, concat_axis=1, tiled=True)
    grad_items = (
        grad_attn_heads.reshape(slot_count, patch_total, heads_local, head_size)
        .transpose(0, 2, 1, 3)
        .reshape(slot_count * heads_local, patch_total, head_size)
    )

    def spatial_grad(pack):
        query, key_rows, value_rows, log_total, grad_o = pack
        probs = jnp.exp(matmul_nt(query, key_rows) * score_scale - log_total[:, None])
        grad_probs = matmul_nt(grad_o, value_rows)
        grad_value = matmul_tn(probs.astype(jnp.bfloat16), grad_o)
        grad_scores = softmax_back(probs, grad_probs).astype(jnp.bfloat16)
        grad_query = matmul(grad_scores, key_rows) * score_scale
        grad_key = matmul_tn(grad_scores, query) * score_scale
        return jnp.stack([grad_query, grad_key, grad_value]).astype(jnp.bfloat16)

    grad_triples = lax.map(spatial_grad, (items[0], items[1], items[2], log_totals, grad_items))
    grad_back_layout = (
        grad_triples.reshape(slot_count, heads_local, 3, patch_total, head_size)
        .transpose(0, 3, 2, 1, 4)
        .reshape(slot_count, sp_count, patch_local, 3, 1, heads_local * head_size)
    )
    grad_qkv = lax.all_to_all(
        grad_back_layout, "sp", split_axis=1, concat_axis=4, tiled=True
    ).reshape(tok_rows, 3 * model_width)
    grad_wqkv = matmul_tn(h_one, grad_qkv)
    grad_h_one = matmul_nt(grad_qkv, qkv_back).reshape(slot_count, patch_local, model_width)
    grad_shift_one = jnp.sum(grad_h_one, axis=1)
    grad_scale_one = jnp.sum(grad_h_one * normed_one, axis=1)
    input_grad = grad_one + normalize_back(resid, grad_h_one * (1.0 + scale_one))
    grad_modulation = jnp.stack(
        [
            grad_shift_one,
            grad_scale_one,
            grad_gate_one,
            grad_shift_two,
            grad_scale_two,
            grad_gate_two,
        ],
        axis=1,
    ).reshape(slot_count, 6 * model_width)
    grad_wada = jnp.dot(
        silu_cond.astype(jnp.float32).T,
        grad_modulation,
        precision=highest,
        preferred_element_type=jnp.float32,
    )
    early_sums = (
        lax.psum_scatter(grad_wckv, ("fsdp", "sp"), scatter_dimension=0, tiled=True),
        lax.psum_scatter(grad_wqkv, ("fsdp", "sp"), scatter_dimension=0, tiled=True),
        lax.psum_scatter(grad_wout, ("fsdp", "sp"), scatter_dimension=0, tiled=True),
        lax.psum_scatter(grad_wada, ("fsdp", "sp"), scatter_dimension=0, tiled=True),
    )
    return (
        output.reshape(1, slot_count, patch_local, model_width),
        input_grad.reshape(1, slot_count, patch_local, model_width),
        early_sums[3],
        early_sums[1],
        early_sums[2],
        late_sums[0],
        early_sums[0],
        late_sums[1],
        late_sums[2],
        late_sums[3],
        late_sums[4],
        late_sums[5],
        late_sums[6],
        late_sums[7],
        late_sums[8],
    )


def solution(mesh):
    return jax.shard_map(
        local,
        mesh=mesh,
        in_specs=(
            P("fsdp", None, "sp", None),
            P("fsdp", None, None),
            P("fsdp", None, "sp", None),
            P("fsdp", None),
            P("fsdp", None, "sp", None),
            P(("fsdp", "sp"), None),
            P(("fsdp", "sp"), None),
            P(("fsdp", "sp"), None),
            P(("fsdp", "sp"), None),
            P(("fsdp", "sp"), None),
            P(("fsdp", "sp"), None),
            P(("fsdp", "sp"), None),
            P(("fsdp", "sp"), None),
            P(("fsdp", "sp"), None),
            P(("fsdp", "sp"), None),
            P(("fsdp", "sp")),
            P(("fsdp", "sp")),
            P(("fsdp", "sp")),
        ),
        out_specs=(
            P("fsdp", None, "sp", None),
            P("fsdp", None, "sp", None),
            P(("fsdp", "sp"), None),
            P(("fsdp", "sp"), None),
            P(("fsdp", "sp"), None),
            P(("fsdp", "sp"), None),
            P(("fsdp", "sp"), None),
            P(("fsdp", "sp"), None),
            P(("fsdp", "sp"), None),
            P(("fsdp", "sp"), None),
            P(("fsdp", "sp"), None),
            P(("fsdp", "sp"), None),
            P(("fsdp", "sp")),
            P(("fsdp", "sp")),
            P(("fsdp", "sp")),
        ),
        check_vma=False,
    )
```

profile of v0, /device:TPU:0, one launch (start us, length us, event | category | flops | bytes accessed | tf_op | source)
XLA Modules:
  0.0 5164.4 jit_solution(3316142860472917835)
XLA Ops:
  21.7 72.0 %all-gather.28.cloned.1.call-done = bf16[32,36,3456]{2,1,0:T(8,128)(2,1)} async-done(((bf16[1,36,3456]{2,1,0:T(8,128)(2,1)}), bf16[32,36,3456]{2,1,0:T(8,128)(2,1)}) %all-gather.28.cloned.1.call-update) | async-done | bytes 7962640 | tf_op jit(solution)/shard_map/all_gather | solution.py:109
  106.2 108.8 %all-gather.26.cloned.1.call-done = bf16[32,36,6912]{2,1,0:T(8,128)(2,1)} async-done(((bf16[1,36,6912]{2,1,0:T(8,128)(2,1)}), bf16[32,36,6912]{2,1,0:T(8,128)(2,1)}) %all-gather.26.cloned.1.call-update) | async-done | bytes 15925264 | tf_op jit(solution)/shard_map/all_gather | solution.py:108
  214.9 18.5 reshape.588
  282.1 119.5 %all-gather.20.cloned.1.call-done = bf16[4096,2304]{1,0:T(8,128)(2,1)} async-done(((bf16[128,2304]{1,0:T(8,128)(2,1)}), bf16[4096,2304]{1,0:T(8,128)(2,1)}) %all-gather.20.cloned.1.call-update) | async-done | bytes 18874384 | tf_op jit(solution)/shard_map/all_gather | solution.py:112
  443.9 50.9 while.22
  504.8 54.7 %all-reduce.24 = (bf16[1152]{0:T(1024)(128)(2,1)}, bf16[1152]{0:T(1024)(128)(2,1)}, bf16[1152]{0:T(1024)(128)(2,1)S(1)}) all-reduce(bf16[1152]{0:T(1024)(128)(2,1)S(1)} %dynamic-update-slice, bf16[1152]{0:T(1024)(128)(2,1)S(1)} %dynamic-update-slice.2, ...), channel_id=1, replica_groups=mesh['fsdp'=8,'sp'=4] {'fsdp','sp'}, use_global_device_ids=true, to_apply=%add | all-reduce | flops 3456 | bytes 13824
  578.8 19.4 all-gather.32.cloned.1.call-done
  603.3 55.8 %all-gather.40.cloned.1.call-done = bf16[32,36,1152]{2,1,0:T(8,128)(2,1)} async-done(((bf16[1,36,1152]{2,1,0:T(8,128)(2,1)}), bf16[32,36,1152]{2,1,0:T(8,128)(2,1)}) %all-gather.40.cloned.1.call-update) | async-done | bytes 2654224 | tf_op jit(solution)/shard_map/all_gather | solution.py:117
  664.3 76.5 %all-gather.38.cloned.1.call-done = bf16[32,36,3456]{2,1,0:T(8,128)(2,1)} async-done(((bf16[1,36,3456]{2,1,0:T(8,128)(2,1)}), bf16[32,36,3456]{2,1,0:T(8,128)(2,1)}) %all-gather.38.cloned.1.call-update) | async-done | bytes 7962640 | tf_op jit(solution)/shard_map/all_gather | solution.py:116
  753.3 81.8 %all-gather.36.cloned.1.call-done = bf16[32,36,4608]{2,1,0:T(8,128)(2,1)} async-done(((bf16[1,36,4608]{2,1,0:T(8,128)(2,1)}), bf16[32,36,4608]{2,1,0:T(8,128)(2,1)}) %all-gather.36.cloned.1.call-update) | async-done | bytes 10616848 | tf_op jit(solution)/shard_map/all_gather | solution.py:114
  892.5 62.0 %all-gather.24.cloned.1.call-done = bf16[4608,1152]{1,0:T(8,128)(2,1)} async-done(((bf16[144,1152]{1,0:T(8,128)(2,1)}), bf16[4608,1152]{1,0:T(8,128)(2,1)}) %all-gather.24.cloned.1.call-update) | async-done | bytes 10616848 | tf_op jit(solution)/shard_map/all_gather | solution.py:115
  968.6 101.4 %conditional.2 = (f32[512,1152]{1,0:T(8,128)}, bf16[512,1152]{1,0:T(8,128)(2,1)}, bf16[2,256,3,16,72]{1,0,4,3,2:T(2,128)(2,1)}, bf16[512,1152]{0,1:T(8,128)(2,1)}, f32[2,256,1152]{2,1,0:T(8,128)}) conditional(s32[]{:T(128)} %bitcast.68, () %tuple.33, (f32[2,256,1152]{2,1,0:T(8,128)S(1)}, f32[1152]{0:T(1024)S(1)}, bf16[1152,3456]{1,0:T(8,128)(2,1)}, ...), branch_computations={%region_12.13_spmd, %region_13.18_spmd} | conditional | flops 5447696896 | bytes 69818920 | solution.py:266
  1016.7 17.1 fusion.123
  1070.0 158.8 %conditional.3 = (f32[2,256,1152]{2,1,0:T(8,128)}, f32[1152,3456]{0,1:T(8,128)}, f32[1152,1152]{0,1:T(8,128)}, f32[1152]{0:T(1024)}, f32[1152]{0:T(1024)}) conditional(s32[]{:T(128)} %bitcast.68, () %tuple.35, (bf16[2,256,3,16,72]{1,0,4,3,2:T(2,128)(2,1)}, bf16[1,2,256,1152]{3,2,1,0:T(8,128)(2,1)S(1)}, f32[1152]{0:T(1024)}, ...), branch_computations={%region_18.19_spmd, %region_19.29_spmd} | conditional | flops 10907181056 | bytes 180980928 | solution.py:365
  1070.0 21.0 copy.194
  1091.0 17.0 fusion.124
  1231.0 16.5 fusion.82
  1351.3 17.7 copy.218
  1377.5 18.3 convolution_bitcast_fusion.2
  1401.7 84.2 %while.23 = (s32[]{:T(128)}, bf16[8,3,1024,72]{2,3,1,0:T(8,128)(2,1)}, bf16[8,1024,72]{2,1,0:T(8,128)(2,1)}, bf16[8,1024,72]{2,1,0:T(8,128)(2,1)}, f32[8,1024]{1...) while((s32[]{:T(128)}, ...), condition=%wide.region_36.37_spmd, body=%wide.region_34.36_spmd.sunk | while | flops 769252352 | bytes 34422364 | solution.py:464
  1507.6 852.4 %fusion.119 = (f32[48,3456]{1,0:T(8,128)}, f32[48,1152]{1,0:T(8,128)}) fusion(f32[1152,3456]{1,0:T(8,128)} %copy.218, f32[1152,1152]{1,0:T(8,128)} %copy.219), kind=kCustom, calls=%all-reduce-scatter.10 | all-reduce-scatter fusion | flops 7077889 | bytes 22118400
  2445.9 1088.2 %fusion.118 = (f32[48,3456]{1,0:T(8,128)}, f32[48,1152]{1,0:T(8,128)S(1)}, f32[40,4608]{1,0:T(8,128)}) fusion(f32[1152,3456]{1,0:T(8,128)} %fusion.136, f32[1152,1152]{1,0:T(8,128)} %fusion.139, f32[1152,4608]{1,0:T(8,128)} %fusion.140), kind=kCustom, calls=%all-reduce-scatter.9 | all-reduce-scatter fusion | flops 12976130 | bytes 44089344
  3549.2 17.2 fusion.111
  3596.5 35.8 collective-permute-start.46
  3635.1 1058.0 %fusion.117 = (f32[40,6912]{1,0:T(8,128)}, f32[48,1152]{1,0:T(8,128)}, f32[48,1152]{1,0:T(8,128)}) fusion(f32[1152,6912]{1,0:T(8,128)} %fusion.111, f32[1152,1152]{1,0:T(8,128)} %fusion.137, f32[1152,1152]{1,0:T(8,128)} %fusion.138), kind=kCustom, calls=%all-reduce-scatter.8 | all-reduce-scatter fusion | flops 12386306 | bytes 44015616
  4747.6 17.3 collective-permute-start.24
  4833.0 69.0 %all-reduce.23 = (f32[1152]{0:T(1024)S(1)}, f32[1152]{0:T(1024)S(1)}, f32[1152]{0:T(1024)S(1)}) all-reduce(f32[1152]{0:T(1024)} %get-tuple-element.249, f32[1152]{0:T(1024)} %get-tuple-element.148, f32[1152]{0:T(1024)} %get-tuple-element.149), channel_id=13, replica_groups=mesh['fsdp'=8,'sp'=4] {'fsdp','sp'}, use_global_device_ids=true, to_apply=%region_57.58.clone | all-reduce | flops 3456 | bytes 27648
  4916.5 36.9 concatenate.19
  5034.4 17.9 collective-permute-start.1
  5065.5 36.8 concatenate.14
  5113.9 17.1 concatenate.18
  5133.1 22.2 concatenate.13
  (769 shorter events, 1100.2 us)
Async XLA Ops:
  9.2 205.8 %all-gather.26.cloned.1.call-start = ((), (), s32[]{:S(2)}) async-start(), calls=%async_computation.11 | async-start | bytes 18247680 | tf_op jit(solution)/shard_map/all_gather | solution.py:108
  11.4 390.1 %all-gather.20.cloned.1.call-start = ((), (), s32[]{:S(2)}) async-start(), calls=%async_computation.6 | async-start | bytes 19464192 | tf_op jit(solution)/shard_map/all_gather | solution.py:112
  12.4 550.9 %all-gather.34.cloned.1.call-start = ((), (), s32[]{:S(2)}) async-start(), calls=%async_computation.15 | async-start | bytes 3041280 | tf_op jit(solution)/shard_map/all_gather | solution.py:113
  13.1 560.5 %all-gather.30.cloned.1.call-start = ((), (), s32[]{:S(2)}) async-start(), calls=%async_computation.13 | async-start | bytes 3041280 | tf_op jit(solution)/shard_map/all_gather | solution.py:110
  13.9 584.3 %all-gather.32.cloned.1.call-start = ((), (), s32[]{:S(2)}) async-start(), calls=%async_computation.14 | async-start | bytes 3041280 | tf_op jit(solution)/shard_map/all_gather | solution.py:111
  15.5 643.7 %all-gather.40.cloned.1.call-start = ((), (), s32[]{:S(2)}) async-start(), calls=%async_computation.18 | async-start | bytes 3041280 | tf_op jit(solution)/shard_map/all_gather | solution.py:117
  17.2 723.7 %all-gather.38.cloned.1.call-start = ((), (), s32[]{:S(2)}) async-start(), calls=%async_computation.17 | async-start | bytes 9123840 | tf_op jit(solution)/shard_map/all_gather | solution.py:116
  19.0 816.1 %all-gather.36.cloned.1.call-start = ((), (), s32[]{:S(2)}) async-start(), calls=%async_computation.16 | async-start | bytes 12165120 | tf_op jit(solution)/shard_map/all_gather | solution.py:114
  275.9 140.4 %all-to-all-start = ((bf16[2,256,3,4,288]{1,0,4,2,3:T(2,128)(2,1)}), bf16[2,256,3,4,288]{1,0,4,2,3:T(2,128)(2,1)}, u32[]{:S(2)}, u32[]{:S(2)}) async-start(bf16[2,256,3,4,288]{1,0,4,2,3:T(2,128)(2,1)} %copy.179), calls=%async_computation | async-start | bytes 7077888 | tf_op jit(solution)/shard_map/all_to_all | solution.py:164
  280.8 588.3 %all-gather.22.cloned.1.call-start = ((), (), s32[]{:S(2)}) async-start(), calls=%async_computation.7 | async-start | bytes 1382400 | tf_op jit(solution)/shard_map/all_gather | solution.py:205
  414.2 540.4 %all-gather.24.cloned.1.call-start = ((), (), s32[]{:S(2)}) async-start(), calls=%async_computation.8 | async-start | bytes 10948608 | tf_op jit(solution)/shard_map/all_gather | solution.py:115
  498.7 354.3 %all-to-all-start.1 = ((bf16[2,4,256,1,288]{2,4,0,3,1:T(8,128)(2,1)}), bf16[2,4,256,1,288]{2,4,0,3,1:T(8,128)(2,1)S(1)}, u32[]{:S(2)}, u32[]{:S(2)}) async-start(bf16[2,4,256,1,288]{2,4,0,3,1:T(8,128)(2,1)} %copy.184), calls=%async_computation.1 | async-start | bytes 2359296 | tf_op jit(solution)/shard_map/all_to_all | solution.py:190
  502.3 874.0 %all-reduce.30.cloned.1.call-start = ((), (), s32[]{:S(2)}) async-start(), calls=%async_computation.19 | async-start | bytes 2211840
  1287.8 3869.8 %reduce-scatter.21.cloned.1.call-start = ((), (), s32[]{:S(2)}) async-start(), calls=%async_computation.10 | async-start | bytes 21897216 | tf_op jit(solution)/shard_map/reduce_scatter | solution.py:432
  1334.6 3823.1 %reduce-scatter.19.cloned.1.call-start = ((), (), s32[]{:S(2)}) async-start(), calls=%async_computation.9 | async-start | bytes 38928384 | tf_op jit(solution)/shard_map/reduce_scatter | solution.py:496
  1502.4 915.2 %all-to-all-start.3 = ((bf16[2,4,256,3,1,288]{2,5,3,0,4,1:T(8,128)(2,1)}), bf16[2,4,256,3,1,288]{2,5,3,0,4,1:T(8,128)(2,1)}, u32[]{:S(2)}, u32[]{:S(2)}) async-start(bf16[2,4,256,3,1,288]{2,5,3,0,4,1:T(8,128)(2,1)} %copy.206), calls=%async_computation.3 | async-start | bytes 7077888 | tf_op jit(solution)/shard_map/all_to_all | solution.py:470
  2361.6 1173.7 %collective-permute-start.48 = (f32[48,1152]{1,0:T(8,128)}, f32[48,1152]{1,0:T(8,128)}, u32[]{:S(2)}, u32[]{:S(2)}) collective-permute-start(f32[48,1152]{1,0:T(8,128)} %get-tuple-element.304), channel_id=1, source_target_pairs={{0,1},{1,2},{2,3},{3,4},{4,5},{5,6},{6,7},{7,8},{8,9},{9,10},{10,1... | collective-permute-start | bytes 663560
  2368.8 1167.9 %collective-permute-start.49 = (f32[48,1152]{1,0:T(8,128)}, f32[48,1152]{1,0:T(8,128)}, u32[]{:S(2)}, u32[]{:S(2)}) collective-permute-start(f32[48,1152]{1,0:T(8,128)} %get-tuple-element.304), channel_id=1, source_target_pairs={{0,2},{1,3},{2,4},{3,5},{4,6},{5,7},{6,8},{7,9},{8,10},{9,11},{10,... | collective-permute-start | bytes 663560
  2372.6 1165.4 %collective-permute-start.50 = (f32[48,1152]{1,0:T(8,128)}, f32[48,1152]{1,0:T(8,128)}, u32[]{:S(2)}, u32[]{:S(2)}) collective-permute-start(f32[48,1152]{1,0:T(8,128)} %get-tuple-element.304), channel_id=1, source_target_pairs={{0,3},{1,4},{2,5},{3,6},{4,7},{5,8},{6,9},{7,10},{8,11},{9,12},{10... | collective-permute-start | bytes 663560
  2374.6 1167.9 %collective-permute-start.51 = (f32[48,1152]{1,0:T(8,128)}, f32[48,1152]{1,0:T(8,128)}, u32[]{:S(2)}, u32[]{:S(2)}) collective-permute-start(f32[48,1152]{1,0:T(8,128)} %get-tuple-element.304), channel_id=1, source_target_pairs={{0,4},{1,5},{2,6},{3,7},{4,8},{5,9},{6,10},{7,11},{8,12},{9,13},{1... | collective-permute-start | bytes 663560
  2388.2 1145.9 %collective-permute-start.55 = (f32[36,1152]{1,0:T(8,128)}, f32[36,1152]{1,0:T(8,128)}, u32[]{:S(2)}, u32[]{:S(2)}) collective-permute-start(f32[36,1152]{1,0:T(8,128)} %slice.103), channel_id=1, source_target_pairs={{0,8},{1,9},{2,10},{3,11},{4,12},{5,13},{6,14},{7,15},{8,16},{9,17... | collective-permute-start | bytes 497672
  3567.0 1127.1 %collective-permute-start.43 = (f32[48,3456]{1,0:T(8,128)S(1)}, f32[48,3456]{1,0:T(8,128)}, u32[]{:S(2)}, u32[]{:S(2)}) collective-permute-start(f32[48,3456]{1,0:T(8,128)S(1)} %copy-done.30), channel_id=1, source_target_pairs={{0,4},{1,5},{2,6},{3,7},{4,8},{5,9},{6,10},{7,11},{8,12},{9,13},{1... | collective-permute-start | bytes 1990664
  3575.5 1120.9 %collective-permute-start.44 = (f32[48,3456]{1,0:T(8,128)S(1)}, f32[48,3456]{1,0:T(8,128)}, u32[]{:S(2)}, u32[]{:S(2)}) collective-permute-start(f32[48,3456]{1,0:T(8,128)S(1)} %copy-done.30), channel_id=1, source_target_pairs={{0,5},{1,6},{2,7},{3,8},{4,9},{5,10},{6,11},{7,12},{8,13},{9,14},{... | collective-permute-start | bytes 1990664
  3585.4 1112.3 %collective-permute-start.45 = (f32[48,3456]{1,0:T(8,128)S(1)}, f32[48,3456]{1,0:T(8,128)}, u32[]{:S(2)}, u32[]{:S(2)}) collective-permute-start(f32[48,3456]{1,0:T(8,128)S(1)} %copy-done.30), channel_id=1, source_target_pairs={{0,6},{1,7},{2,8},{3,9},{4,10},{5,11},{6,12},{7,13},{8,14},{9,15},... | collective-permute-start | bytes 1990664
  3596.5 1114.3 %collective-permute-start.46 = (f32[48,3456]{1,0:T(8,128)S(1)}, f32[48,3456]{1,0:T(8,128)}, u32[]{:S(2)}, u32[]{:S(2)}) collective-permute-start(f32[48,3456]{1,0:T(8,128)S(1)} %copy-done.30), channel_id=1, source_target_pairs={{0,7},{1,8},{2,9},{3,10},{4,11},{5,12},{6,13},{7,14},{8,15},{9,16}... | collective-permute-start | bytes 1990664
  3633.2 1085.7 %collective-permute-start.35 = (f32[36,1152]{1,0:T(8,128)}, f32[36,1152]{1,0:T(8,128)}, u32[]{:S(2)}, u32[]{:S(2)}) collective-permute-start(f32[36,1152]{1,0:T(8,128)} %slice.100), channel_id=1, source_target_pairs={{0,8},{1,9},{2,10},{3,11},{4,12},{5,13},{6,14},{7,15},{8,16},{9,17... | collective-permute-start | bytes 497672
  4799.6 112.6 %collective-permute-start.17 = (f32[48,1152]{1,0:T(8,128)}, f32[48,1152]{1,0:T(8,128)}, u32[]{:S(2)}, u32[]{:S(2)}) collective-permute-start(f32[48,1152]{1,0:T(8,128)} %get-tuple-element.293), channel_id=1, source_target_pairs={{0,6},{1,7},{2,8},{3,9},{4,10},{5,11},{6,12},{7,13},{8,14},{9,15},... | collective-permute-start | bytes 663560
  4808.1 156.8 %collective-permute-start.10 = (f32[48,3456]{1,0:T(8,128)}, f32[48,3456]{1,0:T(8,128)}, u32[]{:S(2)}, u32[]{:S(2)}) collective-permute-start(f32[48,3456]{1,0:T(8,128)} %get-tuple-element.298), channel_id=1, source_target_pairs={{0,7},{1,8},{2,9},{3,10},{4,11},{5,12},{6,13},{7,14},{8,15},{9,16}... | collective-permute-start | bytes 1990664
  4814.1 152.9 %collective-permute-start.4 = (f32[48,3456]{1,0:T(8,128)}, f32[48,3456]{1,0:T(8,128)}, u32[]{:S(2)}, u32[]{:S(2)}) collective-permute-start(f32[48,3456]{1,0:T(8,128)} %get-tuple-element.298), channel_id=1, source_target_pairs={{0,1},{1,2},{2,3},{3,4},{4,5},{5,6},{6,7},{7,8},{8,9},{9,10},{10,1... | collective-permute-start | bytes 1990664
  4816.7 152.4 %collective-permute-start.5 = (f32[48,3456]{1,0:T(8,128)}, f32[48,3456]{1,0:T(8,128)}, u32[]{:S(2)}, u32[]{:S(2)}) collective-permute-start(f32[48,3456]{1,0:T(8,128)} %get-tuple-element.298), channel_id=1, source_target_pairs={{0,2},{1,3},{2,4},{3,5},{4,6},{5,7},{6,8},{7,9},{8,10},{9,11},{10,... | collective-permute-start | bytes 1990664
  4825.4 133.7 %collective-permute-start.11 = (f32[36,3456]{1,0:T(8,128)}, f32[36,3456]{1,0:T(8,128)}, u32[]{:S(2)}, u32[]{:S(2)}) collective-permute-start(f32[36,3456]{1,0:T(8,128)} %slice.97), channel_id=1, source_target_pairs={{0,8},{1,9},{2,10},{3,11},{4,12},{5,13},{6,14},{7,15},{8,16},{9,17... | collective-permute-start | bytes 1493000
  5009.8 104.0 %collective-permute-start.38 = (f32[40,4608]{1,0:T(8,128)S(1)}, f32[40,4608]{1,0:T(8,128)}, u32[]{:S(2)}, u32[]{:S(2)}) collective-permute-start(f32[40,4608]{1,0:T(8,128)S(1)} %copy-done.40), channel_id=1, source_target_pairs={{0,3},{1,4},{2,5},{3,6},{4,7},{5,8},{6,9},{7,10},{8,11},{9,12},{10... | collective-permute-start | bytes 2211848
  (185 other events, 14073.1 us)
Sparse Core Ops, SparseCore 0:
  11.5 82.1 all-gather.27
  97.0 117.8 all-gather.25
  218.3 183.2 all-gather.19
  404.8 57.9 all-gather.33
  466.1 61.5 all-gather.29
  531.0 67.0 all-gather.31
  601.5 57.5 all-gather.39
  662.6 78.1 all-gather.37
  744.2 90.8 all-gather.35
  837.1 27.1 all-gather.21
  867.7 86.7 all-gather.23
  1287.9 53.0 all-reduce.29
  1349.1 264.9 reduce-scatter.20
  1621.0 542.9 reduce-scatter.18
where the time goes:
time: 5230 us; the launch traced here: 5160 us
  blocking collectives  3120 us (60%)
  waiting for transfers between devices  607 us (12%)
  local copies, waits for them, and re-layouts  590 us (11%)
  matrix products  412 us (8%)
  starting transfers between devices  322 us (6%)
  other arithmetic  92.5 us (2%)
    unnamed x5, blocking collectives  3120 us
    unnamed x340, local copies, waits for them, and re-layouts  326 us
    unnamed x57, starting transfers between devices  303 us
    all_gather x1, waiting for transfers between devices, local(): lax.all_gather(lowered[4], ('fsdp', 'sp'), axis=0, tiled=True)  120 us
    all_gather x1, waiting for transfers between devices, local(): lax.all_gather(lowered[0], ('fsdp', 'sp'), axis=0, tiled=True)  109 us
    dot_general x26, matrix products, matmul(): return jnp.dot(left, right, preferred_element_type=jnp.float32)  106 us
  transfers between devices with their start and end apart: 74, of which 10 were waited for; matrix products, arithmetic and copies ran while one was open for 72% of the time, Pallas kernels for 0%

commit v1 on v0

v1 whole, which is shorter than its diff:
```python
import functools
import jax, jax.numpy as jnp
from jax import lax
from jax.experimental import pallas as pl
from jax.experimental.pallas import tpu as pltpu
HD=72
F32=jnp.float32; BF=jnp.bfloat16
def nt(a,b): return lax.dot_general(a,b,(((1,),(1,)),((),())),preferred_element_type=F32)
def tn(a,b): return lax.dot_general(a,b,(((0,),(0,)),((),())),preferred_element_type=F32)
def nn(a,b): return jnp.dot(a,b,preferred_element_type=F32)

def spatial_fwd_kernel(heads, scale, qkv, o, st, os):
    T = qkv.shape[0]
    W = heads*HD
    for i in range(3*heads):
        st[i] = jnp.zeros(st.shape[1:], BF)
        st[i, :, :HD] = qkv[:, i*HD:(i+1)*HD]
    tile = 256
    def head(h, _):
        k = st[heads+h]; v = st[2*heads+h]
        def rows(i, _):
            q = st[h, pl.ds(pl.multiple_of(i*tile,tile), tile), :]
            s = nt(q,k)
            m = jnp.max(s,axis=-1,keepdims=True)
            e = jnp.exp((s-m)*scale)
            l = jnp.sum(e,axis=-1,keepdims=True)
            r = nn(e.astype(BF), v)
            os[h, pl.ds(pl.multiple_of(i*tile,tile), tile), :] = (r/l).astype(BF)
            return 0
        lax.fori_loop(0, T//tile, rows, 0)
        return 0
    lax.fori_loop(0, heads, head, 0)
    for h in range(heads):
        o[:, h*HD:(h+1)*HD] = os[h, :, :HD]

def spatial_fwd(qkv, heads, scale):
    T=qkv.shape[0]
    return pl.pallas_call(functools.partial(spatial_fwd_kernel,heads,scale),
        out_shape=jax.ShapeDtypeStruct((T,heads*HD),BF),
        in_specs=[pl.BlockSpec(memory_space=pltpu.VMEM)],
        out_specs=pl.BlockSpec(memory_space=pltpu.VMEM),
        scratch_shapes=[pltpu.VMEM((3*heads,T,128),BF),pltpu.VMEM((heads,T,128),BF)],
        compiler_params=pltpu.CompilerParams(vmem_limit_bytes=48*2**20),
        cost_estimate=pl.CostEstimate(flops=4*heads*T*T*128,bytes_accessed=T*heads*HD*8,transcendentals=heads*T*T),
        name="spatial_fwd")(qkv)

def spatial_bwd_kernel(heads, scale, qkv, go, g, st, gs, acc):
    T = qkv.shape[0]
    for i in range(3*heads):
        st[i] = jnp.zeros(st.shape[1:], BF)
        st[i, :, :HD] = qkv[:, i*HD:(i+1)*HD]
    for h in range(heads):
        gs[h] = jnp.zeros(gs.shape[1:], BF)
        gs[h, :, :HD] = go[:, h*HD:(h+1)*HD]
    tile = 256
    def head(h, _):
        k = st[heads+h]; v = st[2*heads+h]
        acc[...] = jnp.zeros(acc.shape, F32)
        def cols(i, _):
            sl = pl.ds(pl.multiple_of(i*tile,tile), tile)
            q = st[h, sl, :]; gq_in = gs[h, sl, :]
            s = nt(k,q)
            m = jnp.max(s,axis=0,keepdims=True)
            e = jnp.exp((s-m)*scale)
            p = e * (1.0/jnp.sum(e,axis=0,keepdims=True))
            dp = nt(v,gq_in)
            t = dp*p
            d = jnp.sum(t,axis=0,keepdims=True)
            ds = (t-p*d).astype(BF)
            acc[0] += nn(ds,q)
            acc[1] += nn(p.astype(BF),gq_in)
            st[h, sl, :] = (tn(ds,k)*scale).astype(BF)
            return 0
        lax.fori_loop(0, T//tile, cols, 0)
        st[heads+h] = (acc[0]*scale).astype(BF)
        st[2*heads+h] = acc[1].astype(BF)
        return 0
    lax.fori_loop(0, heads, head, 0)
    for i in range(3*heads):
        g[:, i*HD:(i+1)*HD] = st[i, :, :HD]

def spatial_bwd(qkv, go, heads, scale):
    T=qkv.shape[0]
    return pl.pallas_call(functools.partial(spatial_bwd_kernel,heads,scale),
        out_shape=jax.ShapeDtypeStruct((T,3*heads*HD),BF),
        in_specs=[pl.BlockSpec(memory_space=pltpu.VMEM)]*2,
        out_specs=pl.BlockSpec(memory_space=pltpu.VMEM),
        scratch_shapes=[pltpu.VMEM((3*heads,T,128),BF),pltpu.VMEM((heads,T,128),BF),pltpu.VMEM((2,T,128),F32)],
        compiler_params=pltpu.CompilerParams(vmem_limit_bytes=56*2**20),
        cost_estimate=pl.CostEstimate(flops=10*heads*T*T*128,bytes_accessed=T*heads*HD*16,transcendentals=heads*T*T),
        name="spatial_bwd")(qkv, go)

def cross_fwd_kernel(heads, scale, q, kv, o):
    S,T,W = q.shape
    for h in range(heads):
        c = slice(h*HD,(h+1)*HD); cv = slice(W+h*HD, W+(h+1)*HD)
        s = nt(q[0,:,c], kv[0,:,c])
        m = jnp.max(s,axis=-1,keepdims=True)
        e = jnp.exp((s-m)*scale)
        l = jnp.sum(e,axis=-1,keepdims=True)
        o[0,:,c] = (nn(e.astype(BF), kv[0,:,cv])/l).astype(BF)

def cross_fwd(q, kv, heads, scale):
    S,T,W = q.shape; K=kv.shape[1]
    return pl.pallas_call(functools.partial(cross_fwd_kernel,heads,scale),
        grid=(S,),
        out_shape=jax.ShapeDtypeStruct((S,T,W),BF),
        in_specs=[pl.BlockSpec((1,T,W),lambda s:(s,0,0)),pl.BlockSpec((1,K,2*W),lambda s:(s,0,0))],
        out_specs=pl.BlockSpec((1,T,W),lambda s:(s,0,0)),
        compiler_params=pltpu.CompilerParams(vmem_limit_bytes=32*2**20),
        cost_estimate=pl.CostEstimate(flops=4*S*heads*T*K*128,bytes_accessed=S*T*W*4,transcendentals=S*heads*T*K),
        name="cross_fwd")(q,kv)

def cross_bwd_kernel(heads, scale, q, kv, go, gq, gkv):
    S,T,W = q.shape
    for h in range(heads):
        c = slice(h*HD,(h+1)*HD); cv = slice(W+h*HD, W+(h+1)*HD)
        qh=q[0,:,c]; kh=kv[0,:,c]; vh=kv[0,:,cv]; gh=go[0,:,c]
        s = nt(kh,qh)
        m = jnp.max(s,axis=0,keepdims=True)
        e = jnp.exp((s-m)*scale)
        p = e*(1.0/jnp.sum(e,axis=0,keepdims=True))
        dp = nt(vh,gh)
        t = dp*p
        ds = (t-p*jnp.sum(t,axis=0,keepdims=True)).astype(BF)
        gq[0,:,c] = (tn(ds,kh)*scale).astype(BF)
        gkv[0,:,c] = nn(ds,qh)*scale
        gkv[0,:,cv] = nn(p.astype(BF),gh)

def cross_bwd(q, kv, go, heads, scale):
    S,T,W = q.shape; K=kv.shape[1]
    return pl.pallas_call(functools.partial(cross_bwd_kernel,heads,scale),
        grid=(S,),
        out_shape=(jax.ShapeDtypeStruct((S,T,W),BF),jax.ShapeDtypeStruct((S,K,2*W),F32)),
        in_specs=[pl.BlockSpec((1,T,W),lambda s:(s,0,0)),pl.BlockSpec((1,K,2*W),lambda s:(s,0,0)),pl.BlockSpec((1,T,W),lambda s:(s,0,0))],
        out_specs=(pl.BlockSpec((1,T,W),lambda s:(s,0,0)),pl.BlockSpec((1,K,2*W),lambda s:(s,0,0))),
        compiler_params=pltpu.CompilerParams(vmem_limit_bytes=32*2**20),
        cost_estimate=pl.CostEstimate(flops=10*S*heads*T*K*128,bytes_accessed=S*T*W*8,transcendentals=S*heads*T*K),
        name="cross_bwd")(q,kv,go)


HEADS = 16
EPS = 1e-06
HIGHEST = lax.Precision.HIGHEST
BOTH = ("fsdp", "sp")


def normalize(values):
    centred = values - jnp.mean(values, axis=-1, keepdims=True)
    return centred * lax.rsqrt(jnp.mean(centred * centred, axis=-1, keepdims=True) + EPS)


def normalize_back(values, grad_out):
    return jax.vjp(normalize, values)[1](grad_out)[0]


def gelu_tanh(values):
    return jax.nn.gelu(values, approximate=True)


def scatter(grad):
    part = lax.psum_scatter(grad.astype(BF), "fsdp", scatter_dimension=0, tiled=True)
    return lax.psum_scatter(part, "sp", scatter_dimension=0, tiled=True).astype(F32)


class Moves:
    def __init__(self, fsdp, sp, slots):
        self.fsdp, self.sp, self.slots = fsdp, sp, slots
        self.core = lax.axis_index("fsdp") % 2
        self.z = lax.axis_index("sp")
        self.rounds = []
        for r in range(sp):
            pairs = []
            for f in range(fsdp):
                for z in range(sp):
                    t = (z - r) % sp
                    pairs.append((f * sp + z, (f - f % 2 + t % 2) * sp + slots * (f % 2) + t // 2))
            self.rounds.append(pairs)
        self.swap = [(f, f ^ 1) for f in range(fsdp)]

    def out(self, tokens):
        rows = tokens.shape[0] // self.sp
        blocks = tokens.reshape(self.sp, rows, tokens.shape[1])
        got = []
        for r, pairs in enumerate(self.rounds):
            t = (self.z - r) % self.sp
            block = lax.dynamic_index_in_dim(blocks, t, 0, keepdims=False)
            got.append(lax.ppermute(block, BOTH, pairs))
        return jnp.concatenate(got, axis=0)

    def home(self, tokens):
        rows = tokens.shape[0] // self.sp
        out = jnp.zeros((self.sp, rows, tokens.shape[1]), tokens.dtype)
        for r, pairs in enumerate(self.rounds):
            back = lax.ppermute(tokens[r * rows : (r + 1) * rows], BOTH, [(b, a) for a, b in pairs])
            t = (self.z - r) % self.sp
            out = lax.dynamic_update_index_in_dim(out, back, t, 0)
        return out.reshape(tokens.shape)

    def exchange(self, array):
        return lax.ppermute(array, "fsdp", self.swap)


def local(
    residual_in,
    condition,
    text_states,
    slot_item,
    cotangent,
    w_ada,
    w_qkv,
    w_out,
    w_cross_q,
    w_cross_kv,
    w_cross_out,
    w_up,
    w_down,
    w_temp_qkv,
    w_temp_out,
    g_cross,
    g_temp,
    t_gate,
):
    slots, patches, width = residual_in.shape[1:]
    text_local, text_width = text_states.shape[2:]
    sp = lax.axis_size("sp")
    fsdp = lax.axis_size("fsdp")
    f_index, z_index = lax.axis_index("fsdp"), lax.axis_index("sp")
    rows = w_qkv.shape[0]
    tok = slots * patches
    scale = HD ** (-0.5)
    moves = Moves(fsdp, sp, slots)
    core = f_index % 2

    def gather(shard):
        return lax.all_gather(shard.astype(BF), BOTH, axis=0, tiled=True)

    chosen = slot_item[0]
    video = (chosen[-1] == 0).astype(F32)

    cond = condition[0]
    cond_used = jnp.where((chosen == 0)[:, None], cond[0][None], cond[1][None])
    silu_low = jax.nn.silu(cond_used).astype(BF)
    silu_all = lax.all_gather(silu_low, "fsdp", axis=0, tiled=True)
    silu_rows = lax.dynamic_slice_in_dim(silu_all, (f_index * sp + z_index) * rows, rows, 1)
    mod_part = nn(silu_rows, w_ada.astype(BF))
    modulation = lax.psum(
        lax.psum_scatter(mod_part, "fsdp", scatter_dimension=0, tiled=True), "sp"
    ).reshape(slots, 6, 1, width)
    shift_one, scale_one, gate_one, shift_two, scale_two, gate_two = (modulation[:, i] for i in range(6))

    heads_half = HEADS // 2
    half = heads_half * HD
    qkv_full = gather(w_qkv)
    qkv_half = lax.dynamic_index_in_dim(
        qkv_full.reshape(width, 3, 2, half), core, 2, keepdims=False
    ).reshape(width, 3 * half)
    vectors = lax.all_gather(jnp.stack([g_cross, g_temp, t_gate]).astype(BF), BOTH, axis=1, tiled=True).astype(F32)
    gain_cross, gain_temp, temp_gate = vectors[0], vectors[1], vectors[2]
    out_full = gather(w_out)
    cross_q_full = gather(w_cross_q)
    cross_out_full = gather(w_cross_out)
    up_full = gather(w_up)
    down_full = gather(w_down)
    temp_qkv_full = gather(w_temp_qkv)
    temp_out_full = gather(w_temp_out)

    kv_rows = w_cross_kv.shape[0]
    kv_weight = lax.all_gather(w_cross_kv.astype(BF), "fsdp", axis=0, tiled=True)
    text = text_states[0]
    text_used = jnp.where((chosen == 0)[:, None, None], text[0][None], text[1][None])
    text_cut = text_used.reshape(slots * text_local, fsdp, sp, kv_rows)
    text_mine = lax.all_to_all(text_cut, "sp", split_axis=2, concat_axis=0, tiled=True)
    text_mine = text_mine.reshape(sp * slots * text_local, fsdp * kv_rows)
    kv_part = lax.psum_scatter(nn(text_mine, kv_weight), "sp", scatter_dimension=0, tiled=True).astype(BF)
    kv_all = (
        lax.all_gather(kv_part.reshape(1, slots, text_local, 2 * width), "sp", axis=0, tiled=True)
        .transpose(1, 0, 2, 3)
        .reshape(slots, sp * text_local, 2 * width)
    )

    resid = residual_in[0]
    normed_one = normalize(resid)
    h_one = (normed_one * (1.0 + scale_one) + shift_one).astype(BF).reshape(tok, width)
    h_mine = moves.out(h_one)
    h_slot = jnp.concatenate([h_mine, moves.exchange(h_mine)], axis=0)
    qkv = nn(h_slot, qkv_half).astype(BF)
    o_slot = spatial_fwd(qkv, heads_half, scale)
    o_mine = o_slot[:tok]
    o_other = moves.exchange(o_slot[tok:])
    o_full = jnp.where(
        core == 0,
        jnp.concatenate([o_mine, o_other], axis=1),
        jnp.concatenate([o_other, o_mine], axis=1),
    )
    attn_tok = moves.home(o_full)
    branch_one = nn(attn_tok, out_full).reshape(slots, patches, width)
    x_one = resid + gate_one * branch_one

    normed_two = normalize(x_one)
    cross_in = (normed_two * gain_cross).astype(BF).reshape(tok, width)
    query_c = nn(cross_in, cross_q_full).astype(BF).reshape(slots, patches, width)
    cross_out = cross_fwd(query_c, kv_all, HEADS, scale).reshape(tok, width)
    branch_two = nn(cross_out, cross_out_full).reshape(slots, patches, width)
    x_two = x_one + branch_two

    normed_three = normalize(x_two)
    h_three = (normed_three * (1.0 + scale_two) + shift_two).astype(BF).reshape(tok, width)
    up_proj = nn(h_three, up_full)
    activated = gelu_tanh(up_proj).astype(BF)
    branch_three = nn(activated, down_full).reshape(slots, patches, width)
    x_three = x_two + gate_two * branch_three

    normed_four = normalize(x_three)
    temp_in = (normed_four * gain_temp).astype(BF).reshape(tok, width)
    trip = nn(temp_in, temp_qkv_full).astype(BF).reshape(slots, patches, 3, width)
    tq = [trip[a, :, 0].astype(F32) for a in range(slots)]
    tk = [trip[a, :, 1].astype(F32) for a in range(slots)]
    tv = [trip[a, :, 2].astype(F32) for a in range(slots)]
    member = (jnp.arange(width)[:, None] // HD == jnp.arange(HEADS)[None, :]).astype(F32)
    member_low = member.T.astype(BF)

    def per_head(lefts, rights):
        products = jnp.stack([a * b for a in lefts for b in rights])
        return jnp.dot(
            products.reshape(-1, width), member, precision=HIGHEST, preferred_element_type=F32
        ).reshape(slots, slots, patches, HEADS)

    def spread(values):
        return nn(values.astype(BF).reshape(-1, HEADS), member_low).reshape(slots, slots, patches, width)

    probs_t = jax.nn.softmax(per_head(tq, tk) * scale, axis=1)
    probs_wide = spread(probs_t)
    temp_out = jnp.stack(
        [sum(probs_wide[a, b] * tv[b] for b in range(slots)) for a in range(slots)]
    ).astype(BF).reshape(tok, width)
    branch_four = nn(temp_out, temp_out_full).reshape(slots, patches, width)
    output = x_three + (video * temp_gate) * branch_four

    grad_out = cotangent[0].astype(F32)
    grad_tgate = video * jnp.sum(grad_out * branch_four, axis=(0, 1))
    grad_b4 = (grad_out * (video * temp_gate)).astype(BF).reshape(tok, width)
    grad_wto = tn(temp_out, grad_b4)
    grad_to = nt(grad_b4, temp_out_full).astype(BF).astype(F32).reshape(slots, patches, width)
    grad_to = [grad_to[a] for a in range(slots)]
    dp_t = per_head(grad_to, tv)
    ds_t = probs_t * (dp_t - jnp.sum(dp_t * probs_t, axis=1, keepdims=True))
    ds_wide = spread(ds_t)
    pairs = range(slots)
    grad_trip = jnp.stack(
        [
            jnp.stack([scale * sum(ds_wide[a, b] * tk[b] for b in pairs) for a in pairs]),
            jnp.stack([scale * sum(ds_wide[a, b] * tq[a] for a in pairs) for b in pairs]),
            jnp.stack([sum(probs_wide[a, b] * grad_to[a] for a in pairs) for b in pairs]),
        ],
        axis=2,
    ).astype(BF).reshape(tok, 3 * width)
    grad_wtq = tn(temp_in, grad_trip)
    grad_temp_in = nt(grad_trip, temp_qkv_full).reshape(slots, patches, width)
    grad_gtemp = jnp.sum(grad_temp_in * normed_four, axis=(0, 1))
    grad_three = grad_out + normalize_back(x_three, grad_temp_in * gain_temp)

    grad_gate_two = jnp.sum(grad_three * branch_three, axis=1)
    grad_b3 = (grad_three * gate_two).astype(BF).reshape(tok, width)
    grad_wdown = tn(activated, grad_b3)
    grad_act = nt(grad_b3, down_full)
    grad_up = jax.vjp(gelu_tanh, up_proj)[1](grad_act)[0].astype(BF)
    grad_wup = tn(h_three, grad_up)
    grad_h_three = nt(grad_up, up_full).reshape(slots, patches, width)
    grad_shift_two = jnp.sum(grad_h_three, axis=1)
    grad_scale_two = jnp.sum(grad_h_three * normed_three, axis=1)
    grad_two = grad_three + normalize_back(x_two, grad_h_three * (1.0 + scale_two))

    grad_b2 = grad_two.astype(BF).reshape(tok, width)
    grad_wco = tn(cross_out, grad_b2)
    grad_co = nt(grad_b2, cross_out_full).astype(BF).reshape(slots, patches, width)
    grad_qc, grad_kv = cross_bwd(query_c, kv_all, grad_co, HEADS, scale)
    grad_qc = grad_qc.reshape(tok, width)
    grad_kv = (
        grad_kv.reshape(slots, sp, text_local, 2 * width)
        .transpose(1, 0, 2, 3)
        .reshape(sp * slots * text_local, 2 * width)
        .astype(BF)
    )
    grad_kv = lax.all_gather(
        lax.psum_scatter(grad_kv, "sp", scatter_dimension=0, tiled=True), "sp", axis=0, tiled=True
    )
    grad_wckv = tn(text_mine, grad_kv)
    grad_wcq = tn(cross_in, grad_qc)
    grad_cross_in = nt(grad_qc, cross_q_full).reshape(slots, patches, width)
    grad_gcross = jnp.sum(grad_cross_in * normed_two, axis=(0, 1))
    grad_one = grad_two + normalize_back(x_one, grad_cross_in * gain_cross)

    grad_gate_one = jnp.sum(grad_one * branch_one, axis=1)
    grad_b1 = (grad_one * gate_one).astype(BF).reshape(tok, width)
    grad_wout = tn(attn_tok, grad_b1)
    grad_attn = nt(grad_b1, out_full).astype(BF)
    go_mine = moves.out(grad_attn)
    low_half, high_half = go_mine[:, :half], go_mine[:, half:]
    go_other = moves.exchange(jnp.where(core == 0, high_half, low_half))
    go_slot = jnp.concatenate([jnp.where(core == 0, low_half, high_half), go_other], axis=0)
    grad_qkv = spatial_bwd(qkv, go_slot, heads_half, scale)
    grad_wqkv_half = tn(h_slot, grad_qkv).astype(BF)
    gh_slot = nt(grad_qkv, qkv_half)
    gh_mine = (gh_slot[:tok] + moves.exchange(gh_slot[tok:])).astype(BF)
    grad_h_one = moves.home(gh_mine).astype(F32).reshape(slots, patches, width)
    grad_shift_one = jnp.sum(grad_h_one, axis=1)
    grad_scale_one = jnp.sum(grad_h_one * normed_one, axis=1)
    input_grad = grad_one + normalize_back(resid, grad_h_one * (1.0 + scale_one))

    wide = grad_wqkv_half.reshape(width, 3, 1, half)
    zeros = jnp.zeros_like(wide)
    grad_wqkv = jnp.where(
        core == 0, jnp.concatenate([wide, zeros], axis=2), jnp.concatenate([zeros, wide], axis=2)
    ).reshape(width, 3 * width)

    small = jnp.concatenate(
        [
            jnp.stack(
                [
                    grad_shift_one,
                    grad_scale_one,
                    grad_gate_one,
                    grad_shift_two,
                    grad_scale_two,
                    grad_gate_two,
                ],
                axis=1,
            ).reshape(slots * 6, width),
            jnp.stack([grad_gcross, grad_gtemp, grad_tgate]),
        ],
        axis=0,
    )
    small_all = lax.all_gather(small, BOTH, axis=0).reshape(fsdp, sp, slots * 6 + 3, width)
    small_sp = jnp.sum(small_all, axis=1)
    grad_mod = small_sp[:, : slots * 6].reshape(fsdp * slots, 6 * width)
    grad_wada = jnp.dot(silu_rows.astype(F32).T, grad_mod, precision=HIGHEST, preferred_element_type=F32)
    grad_vec = lax.dynamic_slice_in_dim(
        jnp.sum(small_sp[:, slots * 6 :], axis=0), (f_index * sp + z_index) * rows, rows, 1
    )
    grad_wckv = lax.psum_scatter(grad_wckv.astype(BF), "fsdp", scatter_dimension=0, tiled=True).astype(F32)
    return (
        output[None],
        input_grad[None],
        grad_wada,
        scatter(grad_wqkv),
        scatter(grad_wout),
        scatter(grad_wcq),
        grad_wckv,
        scatter(grad_wco),
        scatter(grad_wup),
        scatter(grad_wdown),
        scatter(grad_wtq),
        scatter(grad_wto),
        grad_vec[0],
        grad_vec[1],
        grad_vec[2],
    )


def solution(mesh):
    P = jax.sharding.PartitionSpec
    tokens = P("fsdp", None, "sp", None)
    weight = P(BOTH, None)
    vector = P(BOTH)
    return jax.shard_map(
        local,
        mesh=mesh,
        in_specs=(tokens, P("fsdp", None, None), tokens, P("fsdp", None), tokens)
        + (weight,) * 10
        + (vector,) * 3,
        out_specs=(tokens, tokens) + (weight,) * 10 + (vector,) * 3,
        check_vma=False,
    )
```

time: 5230 us -> 1670 us (0.32); the launches traced: 5160 us -> 1660 us
  blocking collectives: 3120 us -> 303 us
  local copies, waits for them, and re-layouts: 590 us -> 245 us
  starting transfers between devices: 322 us -> 58.4 us
  matrix products: 412 us -> 179 us
  Pallas kernels: 0 us -> 111 us
  waiting for transfers between devices: 607 us -> 664 us
    unnamed x5 -> x2, blocking collectives: 3120 us -> 149 us
    unnamed x57 -> x11, starting transfers between devices: 303 us -> 21.8 us
    all_gather x11 -> x12, waiting for transfers between devices: 596 us -> 341 us  [the longest x8 238 us: gather(): return lax.all_gather(shard.astype(BF), BOTH, axis=0, tiled=True)]
    dot_general x95 -> x32, matrix products: 378 us -> 179 us  [the longest x12 59.9 us: nn(): return jnp.dot(a, b, preferred_element_type=F32)]
    unnamed x340 -> x303, local copies, waits for them, and re-layouts: 326 us -> 134 us
    reduce_scatter x2 -> x9, waiting for transfers between devices: 0.01 us -> 177 us  [the longest x7 108 us: scatter(): lax.psum_scatter(grad.astype(BF), 'fsdp', scatter_dimension=0, tiled=True)]
    all_gather x0 -> x2, blocking collectives: none -> 115 us  [the longest x1 104 us: local(): lax.all_gather(jnp.stack([g_cross, g_temp, t_gate]).astype(BF), BOTH, axi...]
    pallas_call x0 -> x4, Pallas kernels: none -> 111 us  [the longest x1 59.4 us: spatial_bwd(): pl.pallas_call(functools.partial(spatial_bwd_kernel, heads, scale), out_s...]
  transfers between devices with their start and end apart: 74 -> 52, of which waited for: 10 -> 23; matrix products, arithmetic and copies ran while one was open for 72% -> 34% of each run, Pallas kernels for 0% -> 7%
where the time goes in v1:
time: 1670 us; the launch traced here: 1660 us
  waiting for transfers between devices  664 us (40%)
  blocking collectives  303 us (18%)
  local copies, waits for them, and re-layouts  245 us (15%)
  matrix products  179 us (11%)
  Pallas kernels  111 us (7%)
  other arithmetic  76.3 us (5%)
  starting transfers between devices  58.4 us (3%)
  between operations  20.2 us (1%)
    all_gather x8, waiting for transfers between devices, gather(): return lax.all_gather(shard.astype(BF), BOTH, axis=0, tiled=True)  238 us
    unnamed x2, blocking collectives  149 us
    unnamed x303, local copies, waits for them, and re-layouts  134 us
    reduce_scatter x7, waiting for transfers between devices, scatter(): lax.psum_scatter(grad.astype(BF), 'fsdp', scatter_dimension=0, tiled=True)  108 us
    all_gather x1, blocking collectives, local(): lax.all_gather(jnp.stack([g_cross, g_temp, t_gate]).astype(BF), BOTH, axi...  104 us
    unnamed x35, waiting for transfers between devices  77.9 us
    dot_general x12, matrix products, nn(): return jnp.dot(a, b, preferred_element_type=F32)  59.9 us
    pallas_call x1, Pallas kernels, spatial_bwd(): pl.pallas_call(functools.partial(spatial_bwd_kernel, heads, scale), out_s...  59.4 us
  transfers between devices with their start and end apart: 52, of which 23 were waited for; matrix products, arithmetic and copies ran while one was open for 34% of the time, Pallas kernels for 7%

profile of v1, /device:TPU:0, one launch (start us, length us, event | category | flops | bytes accessed | tf_op | source)
XLA Modules:
  0.0 1656.8 jit_solution(11148304334235727383)
XLA Ops:
  28.5 18.9 %all_to_all.15 = bf16[60,8,4,128]{3,1,0,2:T(8,128)(2,1)S(1)} all-to-all(bf16[60,8,4,128]{3,1,0,2:T(8,128)(2,1)S(1)} %copy.145), channel_id=1, replica_groups=mesh['fsdp'=8,'sp'=4] {'sp'}, dimensions={2} | all-to-all | bytes 983040 | tf_op jit(solution)/shard_map/all_to_all | solution.py:273
  55.8 47.5 %fusion = f32[64,2304]{1,0:T(8,128)S(1)} fusion(f32[240,2304]{1,0:T(8,128)S(1)} %fusion.63), kind=kCustom, calls=%all-reduce-scatter | all-reduce-scatter fusion | flops 589825 | bytes 2802176
  117.6 20.3 %psum.7 = f32[2,6,1,1152]{3,1,0,2:T(8,128)S(1)} all-reduce(f32[2,6,1,1152]{3,1,0,2:T(8,128)S(1)} %reshape.689), channel_id=1, replica_groups=mesh['fsdp'=8,'sp'=4] {'sp'}, use_global_device_ids=true, to_apply=%region_1.2 | all-reduce | flops 13824 | bytes 110592 | tf_op jit(solution)/shard_map/psum | solution.py:247
  148.2 104.2 %all-gather.4 = bf16[32,36,3]{1,2,0:T(4,128)(2,1)S(1)} all-gather(bf16[1,36,3]{1,2,0:T(4,128)(2,1)S(1)} %maximum_bitcast_fusion.4), channel_id=1, replica_groups=mesh['fsdp'=8,'sp'=4] {'fsdp','sp'}, dimensions={0}, use_global_device_ids=true | all-gather | bytes 7128 | tf_op jit(solution)/shard_map/all_gather | solution.py:258
  262.5 16.1 reshape.690
  290.1 17.7 %copy.137 = bf16[1152,3,1,576]{0,3,1,2:T(8,128)(2,1)} copy(bf16[1152,3,1,576]{3,2,1,0:T(2,128)(2,1)} %constant_dynamic-slice_fusion.1) | data formatting | bytes 7962624 | tf_op jit(solution)/shard_map/jit(dynamic_index_in_dim)/dynamic_slice | solution.py:255
  315.6 27.3 %spatial_fwd.1 = bf16[1024,576]{1,0:T(8,128)(2,1)S(1)} custom-call(bf16[1024,1728]{1,0:T(8,128)(2,1)S(1)} %convolution_convert_fusion.7.qkv), custom_call_target="tpu_custom_call" | custom-call | flops 4294967296 | bytes 4718592 | tf_op jit(solution)/shard_map/spatial_fwd/pallas_call | solution.py:38
  369.4 19.6 %all-gather.35.cloned.1.call-done = bf16[32,36,1152]{2,1,0:T(8,128)(2,1)} async-done(((bf16[1,36,1152]{2,1,0:T(8,128)(2,1)}), bf16[32,36,1152]{2,1,0:T(8,128)(2,1)}) %all-gather.35.cloned.1.call-update) | async-done | bytes 2654224 | tf_op jit(solution)/shard_map/all_gather | solution.py:236
  399.2 50.8 %all-gather.33.cloned.1.call-done = bf16[32,36,1152]{2,1,0:T(8,128)(2,1)} async-done(((bf16[1,36,1152]{2,1,0:T(8,128)(2,1)}), bf16[32,36,1152]{2,1,0:T(8,128)(2,1)}) %all-gather.33.cloned.1.call-update) | async-done | bytes 2654224 | tf_op jit(solution)/shard_map/all_gather | solution.py:236
  467.7 18.3 %all-gather.27.cloned.1.call-done = bf16[4,2,30,2304]{3,1,2,0:T(2,128)(2,1)} async-done(((bf16[1,2,30,2304]{3,1,2,0:T(2,128)(2,1)}), bf16[4,2,30,2304]{3,1,2,0:T(2,128)(2,1)}) %all-gather.27.cloned.1.call-update) | async-done | bytes 1105936 | tf_op jit(solution)/shard_map/all_gather | solution.py:277
  487.4 79.8 %all-gather.41.cloned.1.call-done = bf16[32,36,3456]{2,1,0:T(8,128)(2,1)} async-done(((bf16[1,36,3456]{2,1,0:T(8,128)(2,1)}), bf16[32,36,3456]{2,1,0:T(8,128)(2,1)}) %all-gather.41.cloned.1.call-update) | async-done | bytes 7962640 | tf_op jit(solution)/shard_map/all_gather | solution.py:236
  567.3 12.5 reshape.757
  579.8 12.4 reshape.742
  601.4 24.7 %collective-permute-done.7 = bf16[128,1152]{1,0:T(8,128)(2,1)S(1)} collective-permute-done((bf16[128,1152]{1,0:T(8,128)(2,1)}, bf16[128,1152]{1,0:T(8,128)(2,1)S(1)}, u32[]{:S(2)}, u32[]{:S(2)}) %collective-permute-start.7) | collective-permute-done | bytes 294944 | tf_op jit(solution)/shard_map/ppermute | solution.py:195
  634.4 14.3 cross_fwd.1
  652.9 24.8 %all-gather.39.cloned.1.call-done = bf16[32,36,4608]{2,1,0:T(8,128)(2,1)} async-done(((bf16[1,36,4608]{2,1,0:T(8,128)(2,1)}), bf16[32,36,4608]{2,1,0:T(8,128)(2,1)}) %all-gather.39.cloned.1.call-update) | async-done | bytes 10616848 | tf_op jit(solution)/shard_map/all_gather | solution.py:236
  677.7 13.9 reshape.740
  703.2 62.8 %all-gather.29.cloned.1.call-done = bf16[4608,1152]{1,0:T(8,128)(2,1)} async-done(((bf16[144,1152]{1,0:T(8,128)(2,1)}), bf16[4608,1152]{1,0:T(8,128)(2,1)}) %all-gather.29.cloned.1.call-update) | async-done | bytes 10616848 | tf_op jit(solution)/shard_map/all_gather | solution.py:236
  766.0 12.9 fusion.103
  857.3 16.7 %fusion.14 = bf16[512,4608]{1,0:T(8,128)(2,1)} fusion(f32[512,4608]{1,0:T(8,128)} %fusion.116, bf16[512,1152]{1,0:T(8,128)(2,1)} %bitcast.459, bf16[4608,1152]{1,0:T(8,128)(2,1)} %all-gather.29.cloned.1.call-done), kind=kOutput, calls=%fused_computation.11 | convolution fusion | flops 5483003904 | bytes 25952256 | tf_op jit(solution)/shard_map/dot_general | solution.py:8
  982.8 18.1 %collective-permute-done.12 = bf16[128,1152]{1,0:T(8,128)(2,1)S(1)} collective-permute-done((bf16[128,1152]{1,0:T(8,128)(2,1)S(1)}, bf16[128,1152]{1,0:T(8,128)(2,1)S(1)}, u32[]{:S(2)}, u32[]{:S(2)}) %collective-permute-start.12) | collective-permute-done | bytes 294944 | tf_op jit(solution)/shard_map/ppermute | solution.py:188
  1007.3 59.4 %spatial_bwd.1 = bf16[1024,1728]{1,0:T(8,128)(2,1)} custom-call(bf16[1024,1728]{1,0:T(8,128)(2,1)} %copy-done.4, bf16[1024,576]{1,0:T(8,128)(2,1)} %pad_maximum_fusion.2.go), custom_call_target="tpu_custom_call" | custom-call | flops 10737418240 | bytes 9437184 | tf_op jit(solution)/shard_map/spatial_bwd/pallas_call | solution.py:84
  1092.2 12.5 convolution_convert_fusion
  1132.6 12.1 collective-permute-done.17
  1155.0 59.4 %reduce-scatter.38.cloned.1.call-done = bf16[144,4608]{1,0:T(8,128)(2,1)} async-done(((bf16[1152,4608]{1,0:T(8,128)(2,1)}), bf16[144,4608]{1,0:T(8,128)(2,1)}) %reduce-scatter.38.cloned.1.call-update) | async-done | bytes 1327120 | tf_op jit(solution)/shard_map/reduce_scatter | solution.py:162
  1214.5 101.1 %fusion.104 = (bf16[48,1152]{1,0:T(8,128)(2,1)}, bf16[48,1152]{1,0:T(8,128)(2,1)}, bf16[64,2304]{1,0:T(8,128)(2,1)S(1)}, bf16[48,1152]{1,0:T(8,128)(2,1)}, bf16[...) fusion(bf16[144,1152]{1,0:T(8,128)(2,1)} %reduce-scatter.30.cloned.1.call-done, ...), kind=kCustom, calls=%all-reduce-scatter.8 | all-reduce-scatter fusion | flops 2875395 | bytes 6193664
  1326.1 48.0 %reduce-scatter.40.cloned.1.call-done = bf16[576,1152]{1,0:T(8,128)(2,1)} async-done(((bf16[4608,1152]{1,0:T(8,128)(2,1)}), bf16[576,1152]{1,0:T(8,128)(2,1)}) %reduce-scatter.40.cloned.1.call-update) | async-done | bytes 1327120 | tf_op jit(solution)/shard_map/reduce_scatter | solution.py:162
  1374.2 32.4 %all-gather.47.cloned.1.call-done = bf16[4,60,2304]{2,1,0:T(8,128)(2,1)} async-done(((bf16[1,60,2304]{2,1,0:T(8,128)(2,1)}), bf16[4,60,2304]{2,1,0:T(8,128)(2,1)}) %all-gather.47.cloned.1.call-update) | async-done | bytes 1105936 | tf_op jit(solution)/shard_map/all_gather | solution.py:385
  1418.4 48.0 %all-gather.45.cloned.1.call-done = f32[32,15,1152]{2,1,0:T(8,128)} async-done(((f32[1,15,1152]{2,1,0:T(8,128)}), f32[32,15,1152]{2,1,0:T(8,128)}) %all-gather.45.cloned.1.call-update) | async-done | bytes 2211856 | tf_op jit(solution)/shard_map/all_gather | solution.py:434
  1483.4 67.7 %all-reduce.26.cloned.1.call-done = bf16[144,3456]{0,1:T(8,128)(2,1)} async-done(((bf16[144,3456]{0,1:T(8,128)(2,1)}), bf16[144,3456]{0,1:T(8,128)(2,1)}) %all-reduce.26.cloned.1.call-update) | async-done | bytes 995344
  1575.8 12.2 reduce-scatter.42.cloned.1.call-done
  1589.9 57.7 %reduce-scatter.34.cloned.1.call-done = bf16[128,2304]{1,0:T(8,128)(2,1)} async-done(((bf16[1024,2304]{1,0:T(8,128)(2,1)}), bf16[128,2304]{1,0:T(8,128)(2,1)}) %reduce-scatter.34.cloned.1.call-update) | async-done | bytes 589840 | tf_op jit(solution)/shard_map/reduce_scatter | solution.py:441
  (610 shorter events, 492.3 us)
Async XLA Ops:
  9.6 107.0 %all-reduce.24.cloned.1.call-start = ((), (), s32[]{:S(2)}) async-start(), calls=%async_computation.33 | async-start | bytes 884736
  21.6 240.8 %all-gather.31.cloned.1.call-start = ((), (), s32[]{:S(2)}) async-start(), calls=%async_computation.23 | async-start | bytes 9123840 | tf_op jit(solution)/shard_map/all_gather | solution.py:236
  22.4 326.3 %all-gather.43.cloned.1.call-start = ((), (), s32[]{:S(2)}) async-start(), calls=%async_computation.29 | async-start | bytes 3041280 | tf_op jit(solution)/shard_map/all_gather | solution.py:236
  23.2 335.9 %all-gather.37.cloned.1.call-start = ((), (), s32[]{:S(2)}) async-start(), calls=%async_computation.26 | async-start | bytes 3041280 | tf_op jit(solution)/shard_map/all_gather | solution.py:236
  23.9 365.0 %all-gather.35.cloned.1.call-start = ((), (), s32[]{:S(2)}) async-start(), calls=%async_computation.25 | async-start | bytes 3041280 | tf_op jit(solution)/shard_map/all_gather | solution.py:236
  24.6 425.3 %all-gather.33.cloned.1.call-start = ((), (), s32[]{:S(2)}) async-start(), calls=%async_computation.24 | async-start | bytes 3041280 | tf_op jit(solution)/shard_map/all_gather | solution.py:236
  25.4 460.7 %all-gather.27.cloned.1.call-start = ((), (), s32[]{:S(2)}) async-start(), calls=%async_computation.12 | async-start | bytes 1382400 | tf_op jit(solution)/shard_map/all_gather | solution.py:277
  108.5 458.7 %all-gather.41.cloned.1.call-start = ((), (), s32[]{:S(2)}) async-start(), calls=%async_computation.28 | async-start | bytes 9123840 | tf_op jit(solution)/shard_map/all_gather | solution.py:236
  110.4 567.3 %all-gather.39.cloned.1.call-start = ((), (), s32[]{:S(2)}) async-start(), calls=%async_computation.27 | async-start | bytes 12165120 | tf_op jit(solution)/shard_map/all_gather | solution.py:236
  111.3 654.7 %all-gather.29.cloned.1.call-start = ((), (), s32[]{:S(2)}) async-start(), calls=%async_computation.13 | async-start | bytes 10948608 | tf_op jit(solution)/shard_map/all_gather | solution.py:236
  113.2 1041.7 %reduce-scatter.46.cloned.1.call-start = ((), (), s32[]{:S(2)}) async-start(), calls=%async_computation.22 | async-start | bytes 2985984 | tf_op jit(solution)/shard_map/reduce_scatter | solution.py:162
  141.5 110.9 %collective-permute-start.3 = (bf16[128,1152]{1,0:T(8,128)(2,1)S(1)}, bf16[128,1152]{1,0:T(8,128)(2,1)S(1)}, u32[]{:S(2)}, u32[]{:S(2)}) collective-permute-start(bf16[128,1152]{1,0:T(8,128)(2,1)S(1)} %get-tuple-element.164), channel_id=1, source_target_pairs={{0,4},{1,1},{2,5},{3,0},{4,6},{5,3},{6,7},{7,2},{8,12},{9,9},{10,1... | collective-permute-start | bytes 884744 | tf_op jit(solution)/shard_map/ppermute | solution.py:188
  143.4 109.0 %collective-permute-start.2 = (bf16[128,1152]{1,0:T(8,128)(2,1)S(1)}, bf16[128,1152]{1,0:T(8,128)(2,1)S(1)}, u32[]{:S(2)}, u32[]{:S(2)}) collective-permute-start(bf16[128,1152]{1,0:T(8,128)(2,1)S(1)} %get-tuple-element.165), channel_id=1, source_target_pairs={{0,1},{1,5},{2,0},{3,4},{4,3},{5,7},{6,2},{7,6},{8,9},{9,13},{10,8... | collective-permute-start | bytes 884744 | tf_op jit(solution)/shard_map/ppermute | solution.py:188
  143.5 108.9 %collective-permute-start.1 = (bf16[128,1152]{1,0:T(8,128)(2,1)S(1)}, bf16[128,1152]{1,0:T(8,128)(2,1)S(1)}, u32[]{:S(2)}, u32[]{:S(2)}) collective-permute-start(bf16[128,1152]{1,0:T(8,128)(2,1)S(1)} %get-tuple-element.166), channel_id=1, source_target_pairs={{0,5},{1,0},{2,4},{3,1},{4,7},{5,2},{6,6},{7,3},{8,13},{9,8},{10,1... | collective-permute-start | bytes 884744 | tf_op jit(solution)/shard_map/ppermute | solution.py:188
  147.4 105.0 %collective-permute-start = (bf16[128,1152]{1,0:T(8,128)(2,1)S(1)}, bf16[128,1152]{1,0:T(8,128)(2,1)S(1)}, u32[]{:S(2)}, u32[]{:S(2)}) collective-permute-start(bf16[128,1152]{1,0:T(8,128)(2,1)S(1)} %get-tuple-element.167), channel_id=1, source_target_pairs={{0,0},{1,4},{2,1},{3,5},{4,2},{5,6},{6,3},{7,7},{8,8},{9,12},{10,9... | collective-permute-start | bytes 884744 | tf_op jit(solution)/shard_map/ppermute | solution.py:188
  346.2 108.9 %collective-permute-start.5 = (bf16[512,576]{0,1:T(8,128)(2,1)}, bf16[512,576]{0,1:T(8,128)(2,1)}, u32[]{:S(2)}, u32[]{:S(2)}) collective-permute-start(bf16[512,576]{0,1:T(8,128)(2,1)} %copy.139), channel_id=1, source_target_pairs={{0,4},{4,0},{8,12},{12,8},{16,20},{20,16},{24,28},{28,24},{1,5},{5... | collective-permute-start | bytes 1769480 | tf_op jit(solution)/shard_map/ppermute | solution.py:201
  460.6 139.7 %collective-permute-start.6 = (bf16[128,1152]{1,0:T(8,128)(2,1)}, bf16[128,1152]{1,0:T(8,128)(2,1)}, u32[]{:S(2)}, u32[]{:S(2)}) collective-permute-start(bf16[128,1152]{1,0:T(8,128)(2,1)} %get-tuple-element.163), channel_id=1, source_target_pairs={{0,0},{4,1},{1,2},{5,3},{2,4},{6,5},{3,6},{7,7},{8,8},{12,9},{9,10... | collective-permute-start | bytes 884744 | tf_op jit(solution)/shard_map/ppermute | solution.py:195
  827.1 327.8 %reduce-scatter.30.cloned.1.call-start = ((), (), s32[]{:S(2)}) async-start(), calls=%async_computation.14 | async-start | bytes 2985984 | tf_op jit(solution)/shard_map/reduce_scatter | solution.py:162
  917.1 237.9 %reduce-scatter.32.cloned.1.call-start = ((), (), s32[]{:S(2)}) async-start(), calls=%async_computation.15 | async-start | bytes 2985984 | tf_op jit(solution)/shard_map/reduce_scatter | solution.py:162
  922.9 232.1 %reduce-scatter.36.cloned.1.call-start = ((), (), s32[]{:S(2)}) async-start(), calls=%async_computation.17 | async-start | bytes 2985984 | tf_op jit(solution)/shard_map/reduce_scatter | solution.py:162
  928.7 226.3 %reduce-scatter.44.cloned.1.call-start = ((), (), s32[]{:S(2)}) async-start(), calls=%async_computation.21 | async-start | bytes 8957952 | tf_op jit(solution)/shard_map/reduce_scatter | solution.py:162
  948.7 265.7 %reduce-scatter.38.cloned.1.call-start = ((), (), s32[]{:S(2)}) async-start(), calls=%async_computation.18 | async-start | bytes 11943936 | tf_op jit(solution)/shard_map/reduce_scatter | solution.py:162
  960.4 363.0 %reduce-scatter.48.cloned.1.call-start = ((), (), s32[]{:S(2)}) async-start(), calls=%async_computation.32 | async-start | bytes 8957952
  1090.8 283.3 %reduce-scatter.40.cloned.1.call-start = ((), (), s32[]{:S(2)}) async-start(), calls=%async_computation.19 | async-start | bytes 11943936 | tf_op jit(solution)/shard_map/reduce_scatter | solution.py:162
  1104.7 301.8 %all-gather.47.cloned.1.call-start = ((), (), s32[]{:S(2)}) async-start(), calls=%async_computation.31 | async-start | bytes 1474560 | tf_op jit(solution)/shard_map/all_gather | solution.py:385
  1322.4 144.0 %all-gather.45.cloned.1.call-start = ((), (), s32[]{:S(2)}) async-start(), calls=%async_computation.30 | async-start | bytes 2433024 | tf_op jit(solution)/shard_map/all_gather | solution.py:434
  1323.3 227.8 %all-reduce.26.cloned.1.call-start = ((), (), s32[]{:S(2)}) async-start(), calls=%async_computation.34 | async-start | bytes 3538944
  1326.0 262.1 %reduce-scatter.42.cloned.1.call-start = ((), (), s32[]{:S(2)}) async-start(), calls=%async_computation.20 | async-start | bytes 1658880 | tf_op jit(solution)/shard_map/reduce_scatter | solution.py:163
  1374.1 273.5 %reduce-scatter.34.cloned.1.call-start = ((), (), s32[]{:S(2)}) async-start(), calls=%async_computation.16 | async-start | bytes 5308416 | tf_op jit(solution)/shard_map/reduce_scatter | solution.py:441
  1472.2 84.6 %collective-permute-start.27 = (bf16[36,1152]{1,0:T(8,128)(2,1)}, bf16[36,1152]{1,0:T(8,128)(2,1)}, u32[]{:S(2)}, u32[]{:S(2)}) collective-permute-start(bf16[36,1152]{1,0:T(8,128)(2,1)} %slice.259), channel_id=1, source_target_pairs={{0,1},{1,2},{2,3},{4,5},{5,6},{6,7},{8,9},{9,10},{10,11},{12,13},{... | collective-permute-start | bytes 248840
  1475.3 86.2 %collective-permute-start.24 = (bf16[36,1152]{1,0:T(8,128)(2,1)S(1)}, bf16[36,1152]{1,0:T(8,128)(2,1)S(1)}, u32[]{:S(2)}, u32[]{:S(2)}) collective-permute-start(bf16[36,1152]{1,0:T(8,128)(2,1)S(1)} %slice.256), channel_id=1, source_target_pairs={{0,1},{1,2},{2,3},{4,5},{5,6},{6,7},{8,9},{9,10},{10,11},{12,13},{... | collective-permute-start | bytes 248840
  1477.4 84.5 %collective-permute-start.22 = (bf16[36,1152]{1,0:T(8,128)(2,1)S(1)}, bf16[36,1152]{1,0:T(8,128)(2,1)S(1)}, u32[]{:S(2)}, u32[]{:S(2)}) collective-permute-start(bf16[36,1152]{1,0:T(8,128)(2,1)S(1)} %slice.254), channel_id=1, source_target_pairs={{0,1},{1,2},{2,3},{4,5},{5,6},{6,7},{8,9},{9,10},{10,11},{12,13},{... | collective-permute-start | bytes 248840
  (145 other events, 3627.8 us)
Sparse Core Ops, SparseCore 0:
  10.5 41.6 all-gather.24
  55.9 54.2 all-reduce.23
  113.5 93.2 all-gather.30
  210.1 56.9 all-gather.42
  270.4 57.6 all-gather.36
  331.3 57.5 all-gather.34
  392.3 57.5 all-gather.32
  451.5 34.4 all-gather.26
  488.9 78.2 all-gather.40
  570.5 107.2 all-gather.38
  680.6 85.4 all-gather.28
  827.3 42.2 reduce-scatter.45
  917.2 43.1 reduce-scatter.29
  963.8 43.7 reduce-scatter.31
  1011.3 43.7 reduce-scatter.35
  1058.5 70.0 reduce-scatter.43
  1132.3 82.1 reduce-scatter.37
  1218.3 70.0 reduce-scatter.47
  1291.9 82.1 reduce-scatter.39
  1376.1 30.4 all-gather.46
  1409.9 56.4 all-gather.44
  1468.8 82.2 all-reduce.25
  1553.5 34.4 reduce-scatter.41
  1591.8 55.8 reduce-scatter.33

commit v2 on v1

--- a/solution.py
+++ b/solution.py
@@ -1,4 +1,5 @@
 import functools
+from types import SimpleNamespace
 import jax, jax.numpy as jnp
 from jax import lax
 from jax.experimental import pallas as pl
@@ -139,10 +140,1517 @@
         name="cross_bwd")(q,kv,go)
 
 
+MESH = pl.DeviceIdType.MESH
+BLOCK = 144
+PIECE = 36
+WIDE = 1152
+
+
+class Place:
+    def __init__(self, sp):
+        self.sp = sp
+        self.f = lax.axis_index("fsdp")
+        self.z = lax.axis_index("sp")
+        self.core = self.f % 2
+        self.x = (self.f // 2) % 2
+        self.y = self.f // 4
+        self.q = self.f // 2
+
+    def flip(self, bit):
+        step = {"core": 1, "x": 2, "y": 4}[bit]
+        here = {"core": self.core, "x": self.x, "y": self.y}[bit]
+        return (self.f + step * (1 - 2 * here), self.z)
+
+    def along(self, r):
+        return (self.f, (self.z + r) % self.sp)
+
+    def peers(self):
+        return [self.flip(b) for b in ("core", "x", "y")] + [self.along(r) for r in range(1, self.sp)]
+
+
+def greet(place):
+    barrier = pltpu.get_barrier_semaphore()
+    peers = place.peers()
+    for peer in peers:
+        pl.semaphore_signal(barrier, inc=1, device_id=peer, device_id_type=MESH)
+    pl.semaphore_wait(barrier, len(peers))
+
+
+def remote(src, dst, send, recv, device):
+    return pltpu.make_async_remote_copy(
+        src_ref=src, dst_ref=dst, send_sem=send, recv_sem=recv, device_id=device, device_id_type=MESH
+    )
+
+
+class Gather:
+    def __init__(self, place, chunks, send, recv):
+        self.place, self.chunks, self.send, self.recv = place, chunks, send, recv
+
+    def region(self, i, f):
+        array, row, rows, columns, _ = self.chunks[i]
+        return array.at[pl.ds(pl.multiple_of(row(f), 16), rows), columns]
+
+    def copy(self, i, event, f, bit):
+        src = self.region(i, f)
+        return remote(src, src, self.send.at[i, event], self.recv.at[i, event], self.place.flip(bit))
+
+    def bits(self, i):
+        return ("x", "y") if self.chunks[i][4] == 0 else ("y", "x")
+
+    def copies(self, i):
+        p = self.place
+        first, second = self.bits(i)
+        f = p.f
+        f_first = p.flip(first)[0]
+        f_second = p.flip(second)[0]
+        f_diagonal = f_first + f_second - f
+        return [
+            self.copy(i, 0, f, first),
+            self.copy(i, 1, f, second),
+            self.copy(i, 2, f_first, second),
+            self.copy(i, 3, f, "core"),
+            self.copy(i, 4, f_first, "core"),
+            self.copy(i, 5, f_second, "core"),
+            self.copy(i, 6, f_diagonal, "core"),
+        ]
+
+    def begin(self, i):
+        c = self.copies(i)
+        for e in (0, 1, 3):
+            c[e].start()
+
+    def middle(self, i):
+        c = self.copies(i)
+        c[0].wait_recv()
+        c[2].start()
+        c[4].start()
+
+    def late(self, i):
+        c = self.copies(i)
+        c[1].wait_recv()
+        c[5].start()
+        c[2].wait_recv()
+        c[6].start()
+
+    def finish(self, i):
+        c = self.copies(i)
+        for e in (3, 4, 5, 6):
+            c[e].wait_recv()
+        for one in c:
+            one.wait_send()
+
+
+def gather_kernel(plan, sp, shards, down_shard, text_shard, *rest):
+    n_out = len({o for o, _ in plan})
+    outs = rest[:n_out]
+    down, text = rest[n_out], rest[n_out + 1]
+    landed, block, send, recv, zsend, zrecv, dsend, drecv, local_sem = rest[n_out + 2 :]
+    p = Place(sp)
+    greet(p)
+    n = len(plan)
+    ahead = 3
+
+    def launch(i):
+        if i < n:
+            for r in range(1, sp):
+                remote(
+                    shards.at[i], landed.at[i, p.z], zsend.at[i, r - 1], zrecv.at[i, r - 1], p.along(r)
+                ).start()
+            landed[i, p.z] = shards[i]
+        elif i == n:
+            for r in range(1, sp):
+                remote(down_shard, down_own, dsend.at[r - 1], drecv.at[p.z], p.along(r)).start()
+
+    rows = down_shard.shape[0]
+    down_own = down.at[pl.ds(pl.multiple_of(p.f * (sp * rows) + p.z * rows, 16), rows), :]
+    for i in range(ahead):
+        launch(i)
+    pltpu.make_async_copy(down_shard, down_own, drecv.at[p.z]).start()
+    trows = text_shard.shape[0]
+    text_own = text.at[pl.ds(pl.multiple_of(p.f * trows, 16), trows), :]
+    text_copy = pltpu.make_async_copy(text_shard, text_own, local_sem.at[2])
+    text_copy.start()
+
+    chunks = [
+        (outs[o], lambda f: f * BLOCK, BLOCK, pl.ds(c, WIDE), k % 2) for k, (o, c) in enumerate(plan)
+    ]
+    chunks += [
+        (down, lambda f, j=j: f * (sp * rows) + j * rows, rows, pl.ds(0, WIDE), (n + j) % 2) for j in range(sp)
+    ]
+    chunks += [(text, lambda f: f * trows, trows, pl.ds(k * WIDE, WIDE), (n + k) % 2) for k in range(2)]
+    g = Gather(p, chunks, send, recv)
+
+    def ready(i):
+        if i < n:
+            for r in range(1, sp):
+                remote(
+                    shards.at[i], landed.at[i, p.z], zsend.at[i, r - 1], zrecv.at[i, r - 1], p.along(r)
+                ).wait_recv()
+            slot = i % 2
+            for zz in range(sp):
+                block[slot, PIECE * zz : PIECE * (zz + 1), :] = landed[i, zz]
+            copy = pltpu.make_async_copy(block.at[slot], g.region(i, p.f), local_sem.at[slot])
+            copy.start()
+            copy.wait()
+        elif i < n + sp:
+            remote(down_shard, down_own, dsend.at[0], drecv.at[i - n], p.along(1)).wait_recv()
+        elif i == n + sp:
+            text_copy.wait()
+
+    total = len(chunks)
+    for t in range(total + 2):
+        if t < total:
+            launch(t + ahead)
+            ready(t)
+            g.begin(t)
+        if 0 <= t - 1 < total:
+            g.middle(t - 1)
+        if 0 <= t - 2 < total:
+            g.late(t - 2)
+    for i in range(total):
+        g.finish(i)
+    for i in range(n):
+        for r in range(1, sp):
+            remote(
+                shards.at[i], landed.at[i, p.z], zsend.at[i, r - 1], zrecv.at[i, r - 1], p.along(r)
+            ).wait_send()
+    for r in range(1, sp):
+        remote(down_shard, down_own, dsend.at[r - 1], drecv.at[p.z], p.along(r)).wait_send()
+
+
+def gather_all(plan, widths, sp, shards, down_shard, text_shard):
+    n = len(plan)
+    total = n + sp + 2
+    any_space = pl.BlockSpec(memory_space=pl.ANY)
+    vmem = pl.BlockSpec(memory_space=pltpu.VMEM)
+    dma = pltpu.SemaphoreType.DMA
+    return pl.pallas_call(
+        functools.partial(gather_kernel, plan, sp),
+        out_shape=[jax.ShapeDtypeStruct((8 * BLOCK, w), BF) for w in widths]
+        + [
+            jax.ShapeDtypeStruct((8 * sp * down_shard.shape[0], WIDE), BF),
+            jax.ShapeDtypeStruct((8 * text_shard.shape[0], 2 * WIDE), BF),
+        ],
+        in_specs=[vmem, any_space, any_space],
+        out_specs=[any_space] * (len(widths) + 2),
+        scratch_shapes=[
+            pltpu.VMEM((n, sp, PIECE, WIDE), BF),
+            pltpu.VMEM((2, BLOCK, WIDE), BF),
+            dma((total, 7)),
+            dma((total, 7)),
+            dma((n, sp - 1)),
+            dma((n, sp - 1)),
+            dma((sp - 1,)),
+            dma((sp,)),
+            dma((3,)),
+        ],
+        compiler_params=pltpu.CompilerParams(
+            collective_id=1, has_side_effects=True, vmem_limit_bytes=48 * 2**20
+        ),
+        name="gather_all",
+    )(shards, down_shard, text_shard)
+
+
+RING = 6
+PIECES, DOWN, TEXT_ROWS, HALVES = range(4)
+DELAY = 2
+
+
+class Reduce:
+    def __init__(self, place, chunks, sems):
+        self.p, self.chunks = place, chunks
+        self.core_send, self.core_recv, self.two_send = sems.core_send, sems.core_recv, sems.two_send
+        self.two_recv, self.one_send, self.one_recv, self.load = sems.two_recv, sems.one_send, sems.one_recv, sems.load
+
+    def slot(self, i):
+        return self.chunks[i].slot
+
+    def before(self, i):
+        same = [k for k in range(i) if self.chunks[k].sums is self.chunks[i].sums and self.slot(k) == self.slot(i)]
+        return same[-1] if same else None
+
+    def after(self, i):
+        return [k for k in range(i + 1, len(self.chunks)) if self.before(k) == i]
+
+    def cross(self, i):
+        c = self.chunks[i]
+        return remote(
+            c.sent(1 - self.p.core), c.arrived, self.core_send.at[i], self.core_recv.at[i], self.p.flip("core")
+        )
+
+    def start(self, i):
+        if self.chunks[i].sent is not None:
+            self.cross(i).start()
+
+    def loads(self, i):
+        c = self.chunks[i]
+        sums = c.sums.at[self.slot(i)]
+        out = []
+        if c.kept is not None:
+            out.append(pltpu.make_async_copy(c.kept(self.p.core), sums, self.load.at[i % 3, 0]))
+            if c.sent is not None:
+                out.append(pltpu.make_async_copy(c.arrived, c.other.at[i % 2], self.load.at[i % 3, 1]))
+        else:
+            out.append(pltpu.make_async_copy(c.arrived, sums, self.load.at[i % 3, 0]))
+        return out
+
+    def prefetch(self, i):
+        k = self.before(i)
+        if k is not None:
+            self.two(k).wait_send()
+            self.one(k).wait_send()
+        if self.chunks[i].sent is not None:
+            self.cross(i).wait_recv()
+        for copy in self.loads(i):
+            copy.start()
+
+    def views(self, i):
+        c, p = self.chunks[i], self.p
+        sums = c.sums
+        s = self.slot(i)
+        if c.order == 0:
+            return ("y", "x", sums.at[s, 1 - p.y], lambda k: (s, p.y, k), 1 - p.x, p.x)
+        return ("x", "y", sums.at[s, :, 1 - p.x], lambda k: (s, k, p.x), 1 - p.y, p.y)
+
+    def two(self, i):
+        first, _, leaving, _, _, _ = self.views(i)
+        return remote(leaving, self.chunks[i].two, self.two_send.at[i], self.two_recv.at[i], self.p.flip(first))
+
+    def one(self, i):
+        _, second, _, at, away, _ = self.views(i)
+        return remote(
+            self.chunks[i].sums.at[at(away)],
+            self.chunks[i].one,
+            self.one_send.at[i],
+            self.one_recv.at[i],
+            self.p.flip(second),
+        )
+
+    def add(self, i):
+        c = self.chunks[i]
+        for copy in self.loads(i):
+            copy.wait()
+        s = self.slot(i)
+        if c.kept is not None and c.sent is not None:
+            rows = c.sums.shape[-2]
+            sums, other = c.sums, c.other
+
+            def tile(t, _):
+                r = pl.ds(pl.multiple_of(t * 16, 16), 16)
+                for a in range(2):
+                    for b in range(2):
+                        sums[s, a, b, r, :] = (
+                            sums[s, a, b, r, :].astype(F32) + other[i % 2, a, b, r, :].astype(F32)
+                        ).astype(BF)
+                return 0
+
+            lax.fori_loop(0, rows // 16, tile, 0)
+        self.two(i).start()
+
+    def second(self, i):
+        c = self.chunks[i]
+        _, _, _, at, away, stay = self.views(i)
+        self.two(i).wait_recv()
+        sums, two = c.sums, c.two
+        rows = sums.shape[-2]
+
+        def fold(k):
+            def tile(t, _):
+                r = pl.ds(pl.multiple_of(t * 16, 16), 16)
+                here = at(k) + (r, slice(None))
+                sums[here] = (sums[here].astype(F32) + two[k, r, :].astype(F32)).astype(BF)
+                return 0
+
+            lax.fori_loop(0, rows // 16, tile, 0)
+
+        fold(away)
+        self.one(i).start()
+        fold(stay)
+
+    def third(self, i, store):
+        c = self.chunks[i]
+        _, _, _, at, _, stay = self.views(i)
+        self.one(i).wait_recv()
+        store(lambda r: c.sums[at(stay) + (r, slice(None))].astype(F32) + c.one[r, :].astype(F32))
+
+    def drain(self, i, total):
+        if self.chunks[i].sent is not None:
+            self.cross(i).wait_send()
+        if not self.after(i):
+            self.two(i).wait_send()
+            self.one(i).wait_send()
+
+
+def along_z(p, sp, source, landing, send, recv):
+    return [
+        remote(source((p.z + r) % sp), landing(r - 1), send(r - 1), recv(r - 1), p.along(r)) for r in range(1, sp)
+    ]
+
+
+class Sums:
+    def __init__(self, sp, plan, down, text, half):
+        self.sp, self.plan, self.down, self.text, self.half = sp, plan, down, text, half
+        self.blocks = len(plan) + (sp if down else 0)
+        self.total = self.blocks + (2 if text else 0) + (2 if half else 0)
+        shape = jax.ShapeDtypeStruct
+        self.results, self.landings, self.scratch = {}, {}, {}
+        block = (BLOCK, WIDE)
+        if self.blocks:
+            self.landings.update(arrived=shape((self.blocks, 2, 2) + block, BF))
+            self.scratch.update(sums=pltpu.VMEM((RING, 2, 2) + block, BF))
+            self.scratch.update(other=pltpu.VMEM((2, 2, 2) + block, BF))
+            self.scratch.update(two=pltpu.VMEM((self.blocks, 2) + block, BF))
+            self.scratch.update(one=pltpu.VMEM((self.blocks,) + block, BF))
+        if plan:
+            n = len(plan)
+            self.results.update(piece=shape((n, PIECE, WIDE), F32))
+            self.scratch.update(pieces=pltpu.VMEM((n, sp, PIECE, WIDE), BF))
+            self.scratch.update(pieces_in=pltpu.VMEM((n, sp - 1, PIECE, WIDE), BF))
+        if down:
+            self.results.update(down=shape(block, F32))
+            self.scratch.update(blocks_d=pltpu.VMEM((sp,) + block, BF))
+            self.scratch.update(blocks_d_in=pltpu.VMEM((sp - 1,) + block, BF))
+        if text:
+            self.results.update(text=shape((2, text, WIDE), F32))
+            self.landings.update(arrived_text=shape((2, 2, 2, text, WIDE), BF))
+            self.scratch.update(sums_t=pltpu.VMEM((2, 2, 2, text, WIDE), BF))
+            self.scratch.update(other_t=pltpu.VMEM((2, 2, 2, text, WIDE), BF))
+            self.scratch.update(two_t=pltpu.VMEM((2, 2, text, WIDE), BF))
+            self.scratch.update(one_t=pltpu.VMEM((2, text, WIDE), BF))
+        if half:
+            self.results.update(half=shape((2, PIECE, half), F32))
+            self.landings.update(arrived_half=shape((2, 2, BLOCK, half), BF))
+            self.scratch.update(sums_h=pltpu.VMEM((2, 2, 2, BLOCK, half), BF))
+            self.scratch.update(two_h=pltpu.VMEM((2, 2, BLOCK, half), BF))
+            self.scratch.update(one_h=pltpu.VMEM((2, BLOCK, half), BF))
+            self.scratch.update(pieces_h=pltpu.VMEM((2, sp, PIECE, half), BF))
+            self.scratch.update(pieces_h_in=pltpu.VMEM((2, sp - 1, PIECE, half), BF))
+        dma = pltpu.SemaphoreType.DMA
+        each = dma((self.total,))
+        self.scratch.update(
+            core_send=each, core_recv=each, two_send=each, two_recv=each, one_send=each, one_recv=each
+        )
+        self.scratch.update(load=dma((3, 2)))
+        self.scratch.update(zsend=dma((self.total, sp - 1)))
+        self.scratch.update(zrecv=dma((self.total, sp - 1)))
+
+    def arrays(self, grads, down=None, text=None, halves=None):
+        out = [g.reshape(2, 2, 2, BLOCK, g.shape[1]) for g in grads]
+        if self.down:
+            out.append(down.reshape(2, 2, 2, self.sp, BLOCK, WIDE))
+        if self.text:
+            out.append(text.reshape(2, 2, 2, self.text, 2 * WIDE))
+        if self.half:
+            out.append(halves.reshape(2, 2, 2, BLOCK, self.half))
+        return out
+
+    def bind(self, place, arrays, refs):
+        arrays = list(arrays)
+        self.p, self.refs = place, refs
+        halves = arrays.pop() if self.half else None
+        text = arrays.pop() if self.text else None
+        down = arrays.pop() if self.down else None
+        chunks = []
+        if self.text:
+            for k in range(2):
+                view = lambda core, k=k: text.at[:, :, core, :, pl.ds(k * WIDE, WIDE)]
+                chunks.append(SimpleNamespace(kept=view, sent=view, kind=TEXT_ROWS, index=k, slot=k))
+                chunks[-1].__dict__.update(sums=refs.sums_t, other=refs.other_t, arrived=refs.arrived_text.at[k])
+                chunks[-1].__dict__.update(two=refs.two_t.at[k], one=refs.one_t.at[k])
+        blocks = []
+        if self.down:
+            for j in range(self.sp):
+                view = lambda core, j=j: down.at[:, :, core, j]
+                blocks.append(SimpleNamespace(kept=view, sent=view, kind=DOWN, index=j))
+        for k, (o, c) in enumerate(self.plan):
+            view = lambda core, o=o, c=c: arrays[o].at[:, :, core, :, pl.ds(c, WIDE)]
+            blocks.append(SimpleNamespace(kept=view, sent=view, kind=PIECES, index=k))
+        for k, c in enumerate(blocks):
+            c.__dict__.update(sums=refs.sums, other=refs.other, arrived=refs.arrived.at[k], slot=k % RING)
+            c.__dict__.update(two=refs.two.at[k], one=refs.one.at[k])
+        chunks, plain = blocks, chunks
+        if self.half:
+            view = lambda core: halves.at[:, :, core]
+            for k in range(2):
+                chunks.append(SimpleNamespace(kept=None if k else view, sent=view if k else None, kind=HALVES, index=k, slot=k))
+                chunks[-1].__dict__.update(sums=refs.sums_h, arrived=refs.arrived_half)
+                chunks[-1].__dict__.update(two=refs.two_h.at[k], one=refs.one_h.at[k])
+        chunks = chunks + plain
+        for k, c in enumerate(chunks):
+            c.order = k % 2
+        self.chunks = chunks
+        self.red = Reduce(place, chunks, refs)
+
+    def sends(self, i):
+        c, refs, p, sp = self.chunks[i], self.refs, self.p, self.sp
+        k = c.index
+        sems = (lambda r: refs.zsend.at[i, r], lambda r: refs.zrecv.at[i, r])
+        if c.kind == PIECES:
+            return along_z(p, sp, lambda z: refs.pieces.at[k, z], lambda r: refs.pieces_in.at[k, r], *sems)
+        if c.kind == HALVES:
+            return along_z(p, sp, lambda z: refs.pieces_h.at[k, z], lambda r: refs.pieces_h_in.at[k, r], *sems)
+        if c.kind == DOWN and k == sp - 1:
+            return along_z(p, sp, lambda z: refs.blocks_d.at[z], lambda r: refs.blocks_d_in.at[r], *sems)
+        return []
+
+    def store(self, i):
+        c, sp = self.chunks[i], self.sp
+        k = c.index
+
+        def cut(target):
+            def inner(value):
+                for z in range(sp):
+                    low = PIECE * z - PIECE * z % 16
+                    high = PIECE * (z + 1)
+                    high += -high % 16
+                    rows = value(pl.ds(low, high - low))
+                    target[k, z] = rows[PIECE * z - low : PIECE * z - low + PIECE].astype(BF)
+
+            return inner
+
+        def tiles(target, rows, kind):
+            def inner(value):
+                def tile(t, _):
+                    r = pl.ds(pl.multiple_of(t * 16, 16), 16)
+                    target[k, r, :] = value(r).astype(kind)
+                    return 0
+
+                lax.fori_loop(0, rows // 16, tile, 0)
+
+            return inner
+
+        if c.kind == PIECES:
+            return cut(self.refs.pieces)
+        if c.kind == HALVES:
+            return cut(self.refs.pieces_h)
+        if c.kind == DOWN:
+            return tiles(self.refs.blocks_d, BLOCK, BF)
+        return tiles(self.refs.text, self.text, F32)
+
+    def last(self, i):
+        c, refs, p, sp = self.chunks[i], self.refs, self.p, self.sp
+        k = c.index
+        for copy in self.sends(i):
+            copy.wait_recv()
+        if c.kind in (PIECES, HALVES):
+            result, mine, others_in = (
+                (refs.piece, refs.pieces, refs.pieces_in)
+                if c.kind == PIECES
+                else (refs.half, refs.pieces_h, refs.pieces_h_in)
+            )
+            result[k] = mine[k, p.z].astype(F32) + sum(others_in[k, r].astype(F32) for r in range(sp - 1))
+        elif c.kind == DOWN and k == sp - 1:
+
+            def tile(t, _):
+                r = pl.ds(pl.multiple_of(t * 16, 16), 16)
+                refs.down[r, :] = refs.blocks_d[p.z, r, :].astype(F32) + sum(
+                    refs.blocks_d_in[a, r, :].astype(F32) for a in range(sp - 1)
+                )
+                return 0
+
+            lax.fori_loop(0, BLOCK // 16, tile, 0)
+
+    ahead = 4
+
+    def begin(self):
+        for i in range(min(self.ahead, self.total)):
+            self.red.start(i)
+        self.red.prefetch(0)
+
+    def step(self, t):
+        red, total = self.red, self.total
+        if t + self.ahead < total:
+            red.start(t + self.ahead)
+        if t + 1 < total:
+            red.prefetch(t + 1)
+        if t < total:
+            red.add(t)
+        if 0 <= t - DELAY < total:
+            red.second(t - DELAY)
+        i = t - 2 * DELAY
+        if 0 <= i < total:
+            red.third(i, self.store(i))
+            for copy in self.sends(i):
+                copy.start()
+        if 0 <= i - 2 < total:
+            self.last(i - 2)
+
+    def steps(self):
+        return [functools.partial(self.step, t) for t in range(self.total + 2 * DELAY + 2)]
+
+    def end(self):
+        for i in range(self.total):
+            self.red.drain(i, self.total)
+            for copy in self.sends(i):
+                copy.wait_send()
+
+
+MOD_ROWS = 16
+START, WAIT_RECV, WAIT_SEND = range(3)
+TILE = 8
+
+
+class Pairs:
+    def __init__(self, p):
+        self.p = p
+
+    def owner(self, t):
+        p = self.p
+        return (p.f - p.core + t % 2, 2 * p.core + t // 2)
+
+    def is_owner(self, t):
+        p = self.p
+        return jnp.logical_and(p.core == t % 2, p.z == 2 * p.core + t // 2)
+
+    def source(self, z):
+        p = self.p
+        return (p.f - p.core + p.z // 2, z)
+
+    def is_source(self, z):
+        p = self.p
+        return jnp.logical_and(p.core == p.z // 2, p.z == z)
+
+    def mine(self):
+        return 2 * (self.p.z % 2) + self.p.core
+
+
+def to_owners(p, blocks, landing, send, recv, do):
+    pairs = Pairs(p)
+    for i in range(4):
+        if do == WAIT_RECV:
+            remote(blocks.at[0], landing.at[i], send.at[0], recv.at[i], pairs.owner(0)).wait_recv()
+            continue
+        far = remote(blocks.at[i], landing.at[p.z], send.at[i], recv.at[p.z], pairs.owner(i))
+        near = pltpu.make_async_copy(blocks.at[i], landing.at[p.z], recv.at[p.z])
+
+        @pl.when(jnp.logical_not(pairs.is_owner(i)))
+        def _():
+            far.start() if do == START else far.wait_send()
+
+        if do == START:
+
+            @pl.when(pairs.is_owner(i))
+            def _():
+                near.start()
+
+
+def to_homes(p, blocks, landing, send, recv, do):
+    pairs = Pairs(p)
+    mine = pairs.mine()
+    for i in range(4):
+        if do == WAIT_RECV:
+            remote(blocks.at[0], landing.at[i], send.at[0], recv.at[i], pairs.source(0)).wait_recv()
+            continue
+        far = remote(blocks.at[i], landing.at[mine], send.at[i], recv.at[mine], pairs.source(i))
+        near = pltpu.make_async_copy(blocks.at[i], landing.at[mine], recv.at[mine])
+
+        @pl.when(jnp.logical_not(pairs.is_source(i)))
+        def _():
+            far.start() if do == START else far.wait_send()
+
+        if do == START:
+
+            @pl.when(pairs.is_source(i))
+            def _():
+                near.start()
+
+
+def others(p):
+    out = []
+    for m in range(1, 8):
+        f = p.f
+        for bit, step, here in ((1, 1, p.core), (2, 2, p.x), (4, 4, p.y)):
+            if m & bit:
+                f = f + step * (1 - 2 * here)
+        out.append((f, p.z))
+    return out
+
+
+def group(p):
+    sib = p.flip("core")[0]
+    return [p.along(r) for r in range(1, p.sp)] + [(sib, (p.z + r) % p.sp) for r in range(1, p.sp)]
+
+
+def greet_list(peers):
+    barrier = pltpu.get_barrier_semaphore()
+    for peer in peers:
+        pl.semaphore_signal(barrier, inc=1, device_id=peer, device_id_type=MESH)
+    pl.semaphore_wait(barrier, len(peers))
+
+
+def front_kernel(
+    sp,
+    shards,
+    ada,
+    silu,
+    vectors,
+    text,
+    resid,
+    full,
+    h_slot,
+    modulation,
+    vectors_all,
+    text_mine,
+    silu_in,
+    landed,
+    block,
+    parts,
+    parts_in,
+    sums_in,
+    vec_own,
+    vec_in,
+    text_in,
+    h_blocks,
+    send,
+    recv,
+    zsend,
+    zrecv,
+    csend,
+    crecv,
+    local_sem,
+    s1,
+    r1,
+    s2,
+    r2,
+    s3,
+    r3,
+    sv1,
+    rv1,
+    sv2,
+    rv2,
+    st,
+    rt,
+    sh,
+    rh,
+    sx,
+    rx,
+):
+    p = Place(sp)
+    near = others(p)
+    greet_list(near + group(p))
+    here = lambda f: full.at[pl.ds(pl.multiple_of(f * BLOCK, 16), BLOCK), :]
+    orders = [1 - p.core, p.core]
+
+    def cond(m):
+        f = near[m][0]
+        return remote(silu.at[f * sp + p.z], silu_in.at[p.f], s1.at[m], r1.at[m], near[m])
+
+    for m in range(7):
+        cond(m).start()
+    silu_in[p.f] = silu[p.f * sp + p.z]
+
+    vec_own[...] = vectors[:TILE, :].astype(F32)
+    vec_in[p.z] = vec_own[...]
+
+    def vec_z(r):
+        return remote(vec_own, vec_in.at[p.z], sv1.at[r - 1], rv1.at[r - 1], p.along(r))
+
+    for r in range(1, sp):
+        vec_z(r).start()
+
+    def spread(k, r):
+        return remote(
+            shards.at[orders[k]], landed.at[orders[k], p.z], zsend.at[k, r - 1], zrecv.at[k, r - 1], p.along(r)
+        )
+
+    for k in range(2):
+        for r in range(1, sp):
+            spread(k, r).start()
+        landed[orders[k], p.z] = shards[orders[k]]
+
+    def text_z(r):
+        z = (p.z + r) % sp
+        return remote(text.at[z], text_in.at[p.z], st.at[r - 1], rt.at[r - 1], p.along(r))
+
+    for r in range(1, sp):
+        text_z(r).start()
+    text_in[p.z] = text[p.z]
+
+    for m in range(7):
+        cond(m).wait_recv()
+    rows = jnp.concatenate([silu_in[f][:2] for f in range(8)], axis=0).astype(BF)
+    slots = 2
+    for j in range(6):
+        res = nn(rows, ada[:, j * WIDE : (j + 1) * WIDE])
+        for f in range(8):
+            parts[f, slots * j : slots * (j + 1), :] = res[slots * f : slots * (f + 1)]
+    for f in range(8):
+        parts[f, 6 * slots :, :] = jnp.zeros((MOD_ROWS - 6 * slots, WIDE), F32)
+
+    def part(m):
+        return remote(parts.at[near[m][0]], parts_in.at[m], s2.at[m], r2.at[m], near[m])
+
+    for m in range(7):
+        part(m).start()
+
+    sibling = p.flip("core")[0]
+
+    def cross():
+        return remote(block.at[0], here(p.f), csend.at[0], crecv.at[0], p.flip("core"))
+
+    def copies(k):
+        f = sibling if k == 0 else p.f
+        first, second = ("x", "y") if k == 0 else ("y", "x")
+        step = p.flip(first)[0] - p.f
+        return [
+            remote(here(g), here(g), send.at[k, e], recv.at[k, e], p.flip(bit))
+            for e, g, bit in ((0, f, first), (1, f, second), (2, f + step, second))
+        ]
+
+    for k in range(2):
+        for r in range(1, sp):
+            spread(k, r).wait_recv()
+        for zz in range(sp):
+            block[k, PIECE * zz : PIECE * (zz + 1), :] = landed[orders[k], zz]
+        if k == 0:
+            cross().start()
+    own = pltpu.make_async_copy(block.at[1], here(p.f), local_sem.at[0])
+    own.start()
+
+    for m in range(7):
+        part(m).wait_recv()
+    parts[p.f] = parts[p.f] + sum(parts_in[m] for m in range(7))
+
+    def total(r):
+        return remote(parts.at[p.f], sums_in.at[r - 1], s3.at[r - 1], r3.at[r - 1], p.along(r))
+
+    for r in range(1, sp):
+        total(r).start()
+    own.wait()
+    for e in (0, 1):
+        copies(1)[e].start()
+    cross().wait_recv()
+    for e in (0, 1):
+        copies(0)[e].start()
+    for r in range(1, sp):
+        vec_z(r).wait_recv()
+
+    def vec_f(m):
+        return remote(vec_in, vectors_all.at[p.f], sv2.at[m], rv2.at[m], near[m])
+
+    for m in range(7):
+        vec_f(m).start()
+    vectors_all[p.f] = vec_in[...]
+    for r in range(1, sp):
+        total(r).wait_recv()
+    modulation[...] = parts[p.f] + sum(sums_in[r] for r in range(sp - 1))
+
+    patches = resid.shape[1]
+    step = 32
+    for s in range(slots):
+        for k in range(2):
+
+            def tile(i, _):
+                r = pl.multiple_of(i * step, step)
+                v = resid[s, pl.ds(k * (patches // 2) + r, step), :]
+                c = v - jnp.mean(v, axis=-1, keepdims=True)
+                n = c * lax.rsqrt(jnp.mean(c * c, axis=-1, keepdims=True) + 1e-06)
+                h = n * (1.0 + modulation[slots + s : slots + s + 1, :]) + modulation[s : s + 1, :]
+                h_blocks[2 * s + k, pl.ds(r, step), :] = h.astype(BF)
+                return 0
+
+            lax.fori_loop(0, patches // 2 // step, tile, 0)
+    to_owners(p, h_blocks, h_slot.at[0], sh, rh, START)
+    for k in (1, 0):
+        copies(k)[0].wait_recv()
+        copies(k)[2].start()
+    for r in range(1, sp):
+        text_z(r).wait_recv()
+    text_rows = text_in.shape[1]
+    for zz in range(sp):
+        text_mine[text_rows * zz : text_rows * (zz + 1), :] = text_in[zz]
+    to_owners(p, h_blocks, h_slot.at[0], sh, rh, WAIT_RECV)
+    swap = remote(h_slot.at[0], h_slot.at[1], sx.at[0], rx.at[0], p.flip("core"))
+    swap.start()
+    for k in range(2):
+        copies(k)[1].wait_recv()
+        copies(k)[2].wait_recv()
+        for e in range(3):
+            copies(k)[e].wait_send()
+        for r in range(1, sp):
+            spread(k, r).wait_send()
+    cross().wait_send()
+    for m in range(7):
+        vec_f(m).wait_recv()
+        vec_f(m).wait_send()
+        part(m).wait_send()
+        cond(m).wait_send()
+    for r in range(1, sp):
+        vec_z(r).wait_send()
+        total(r).wait_send()
+        text_z(r).wait_send()
+    to_owners(p, h_blocks, h_slot.at[0], sh, rh, WAIT_SEND)
+    swap.wait()
+
+
+def front(sp, shards, ada, silu, vectors, text, resid):
+    half = shards.shape[2]
+    patches = resid.shape[1]
+    text_rows, depth = text.shape[1:]
+    dma = pltpu.SemaphoreType.DMA
+    vmem = pl.BlockSpec(memory_space=pltpu.VMEM)
+    any_space = pl.BlockSpec(memory_space=pl.ANY)
+    shape = jax.ShapeDtypeStruct
+    lanes = silu.shape[2]
+    return pl.pallas_call(
+        functools.partial(front_kernel, sp),
+        out_shape=[
+            shape((8 * BLOCK, half), BF),
+            shape((2, 4, patches // 2, WIDE), BF),
+            shape((MOD_ROWS, WIDE), F32),
+            shape((8, sp, TILE, lanes), F32),
+            shape((sp * text_rows, depth), BF),
+            shape((8, TILE, lanes), F32),
+        ],
+        in_specs=[vmem] * 6,
+        out_specs=[any_space] + [vmem] * 5,
+        scratch_shapes=[
+            pltpu.VMEM((2, sp, PIECE, half), BF),
+            pltpu.VMEM((2, BLOCK, half), BF),
+            pltpu.VMEM((8, MOD_ROWS, WIDE), F32),
+            pltpu.VMEM((7, MOD_ROWS, WIDE), F32),
+            pltpu.VMEM((sp - 1, MOD_ROWS, WIDE), F32),
+            pltpu.VMEM((TILE, lanes), F32),
+            pltpu.VMEM((sp, TILE, lanes), F32),
+            pltpu.VMEM((sp, text_rows, depth), BF),
+            pltpu.VMEM((4, patches // 2, WIDE), BF),
+            dma((2, 3)),
+            dma((2, 3)),
+            dma((2, sp - 1)),
+            dma((2, sp - 1)),
+            dma((1,)),
+            dma((1,)),
+            dma((1,)),
+        ]
+        + [dma((7,))] * 4
+        + [dma((sp - 1,))] * 4
+        + [dma((7,))] * 2
+        + [dma((sp - 1,))] * 2
+        + [dma((4,))] * 2
+        + [dma((1,))] * 2,
+        compiler_params=pltpu.CompilerParams(
+            collective_id=4, has_side_effects=True, vmem_limit_bytes=48 * 2**20
+        ),
+        name="front",
+    )(shards, ada, silu, vectors, text, resid)
+
+
+LAG = 2
+FIRST = 5
+PER = 2
+
+
+def interleave(first, per, work, steps):
+    steps = list(steps)
+    for _ in range(first):
+        steps.pop(0)()
+    for k, piece in enumerate(work):
+        piece()
+        if steps and k % per == per - 1:
+            steps.pop(0)()
+    for step in steps:
+        step()
+
+
+class SumAlong:
+    def __init__(self, p, part, landing, out, send, recv, send_again, recv_again):
+        self.p, self.part, self.landing, self.out = p, part, landing, out
+        self.sems = (send, recv, send_again, recv_again)
+
+    def parts(self):
+        send, recv = self.sems[:2]
+        return along_z(
+            self.p,
+            self.p.sp,
+            lambda z: self.part.at[z],
+            lambda r: self.landing.at[r],
+            lambda r: send.at[r],
+            lambda r: recv.at[r],
+        )
+
+    def shares(self):
+        own = self.out.at[self.p.z]
+        send, recv = self.sems[2:]
+        return [
+            remote(own, own, send.at[r - 1], recv.at[r - 1], self.p.along(r)) for r in range(1, self.p.sp)
+        ]
+
+    def start(self):
+        for copy in self.parts():
+            copy.start()
+
+    def sum(self):
+        for copy in self.parts():
+            copy.wait_recv()
+        z = self.p.z
+        for c in range(self.out.shape[2] // WIDE):
+            cols = slice(c * WIDE, (c + 1) * WIDE)
+            self.out[z, :, cols] = (
+                self.part[z, :, cols].astype(F32)
+                + sum(self.landing[r, :, cols].astype(F32) for r in range(self.p.sp - 1))
+            ).astype(BF)
+        for copy in self.shares():
+            copy.start()
+
+    def end(self):
+        for copy in self.parts():
+            copy.wait_send()
+        for copy in self.shares():
+            copy.wait()
+
+
+def attend_kernel(plan, sp, heads, scale, n_out, *refs):
+    shards, down_shard, text_shard, h_slot, qkv_w, text_mine = refs[:6]
+    refs = refs[6:]
+    outs = refs[:n_out]
+    down, text, qkv, attn, kv = refs[n_out : n_out + 5]
+    refs = refs[n_out + 5 :]
+    landed, block, stack, heads_out, o_send, o_recv, o_full, text_w, kv_part, kv_in = refs[:10]
+    send, recv, zsend, zrecv, dsend, drecv, local_sem, osem, hsend, hrecv = refs[10:20]
+    p = Place(sp)
+    along = SumAlong(p, kv_part, kv_in, kv, *refs[20:])
+    greet_list([p.flip(b) for b in ("core", "x", "y")] + group(p))
+    n = len(plan)
+    rows = down_shard.shape[0]
+    trows = text_shard.shape[0]
+    down_own = down.at[pl.ds(pl.multiple_of(p.f * (sp * rows) + p.z * rows, 16), rows), :]
+    text_own = text.at[pl.ds(pl.multiple_of(p.f * trows, 16), trows), :]
+    text_copy = pltpu.make_async_copy(text_shard, text_own, local_sem.at[2])
+    text_copy.start()
+
+    chunks = [(text, lambda f: f * trows, trows, pl.ds(k * WIDE, WIDE), k % 2) for k in range(2)]
+    chunks += [(outs[o], lambda f: f * BLOCK, BLOCK, pl.ds(c, WIDE), k % 2) for k, (o, c) in enumerate(plan)]
+    chunks += [
+        (down, lambda f, j=j: f * (sp * rows) + j * rows, rows, pl.ds(0, WIDE), (n + j) % 2) for j in range(sp)
+    ]
+    total = len(chunks)
+    g = Gather(p, chunks, send, recv)
+
+    def pieces(i):
+        return [
+            remote(shards.at[i], landed.at[i, p.z], zsend.at[i, r - 1], zrecv.at[i, r - 1], p.along(r))
+            for r in range(1, sp)
+        ]
+
+    def down_z(r):
+        return remote(down_shard, down_own, dsend.at[r - 1], drecv.at[p.z], p.along(r))
+
+    def launch(i):
+        if i < n:
+            for copy in pieces(i):
+                copy.start()
+            landed[i, p.z] = shards[i]
+        elif i == n:
+            for r in range(1, sp):
+                down_z(r).start()
+
+    def ready(t):
+        if t == 0:
+            text_copy.wait()
+        i = t - 2
+        if 0 <= i < n:
+            for copy in pieces(i):
+                copy.wait_recv()
+            slot = i % 2
+            for zz in range(sp):
+                block[slot, PIECE * zz : PIECE * (zz + 1), :] = landed[i, zz]
+            copy = pltpu.make_async_copy(block.at[slot], g.region(t, p.f), local_sem.at[slot])
+            copy.start()
+            copy.wait()
+        elif i >= n:
+            remote(down_shard, down_own, dsend.at[0], drecv.at[i - n], p.along(1)).wait_recv()
+
+    ahead = 3
+    pltpu.make_async_copy(down_shard, down_own, drecv.at[p.z]).start()
+    for i in range(ahead):
+        launch(i)
+
+    def step(t):
+        if t < total:
+            if t >= 2:
+                launch(t - 2 + ahead)
+            ready(t)
+            g.begin(t)
+        if 0 <= t - LAG < total:
+            g.middle(t - LAG)
+        if 0 <= t - 2 * LAG < total:
+            g.late(t - 2 * LAG)
+
+    T = qkv.shape[0]
+    half = heads * HD
+    tile = 256
+
+    def project(i):
+        hb = h_slot.shape[2]
+        for b in range(tile // hb):
+            k = i * (tile // hb) + b
+            qkv[hb * k : hb * (k + 1), :] = nn(h_slot[k // 4, k % 4], qkv_w[...]).astype(BF)
+
+    def stage():
+        for i in range(3 * heads):
+            stack[i] = jnp.zeros(stack.shape[1:], BF)
+            stack[i, :, :HD] = qkv[:, i * HD : (i + 1) * HD]
+
+    def head(h):
+        def tile_of(i, _):
+            q = stack[h, pl.ds(pl.multiple_of(i * tile, tile), tile), :]
+            s = nt(q, stack[heads + h])
+            m = jnp.max(s, axis=-1, keepdims=True)
+            e = jnp.exp((s - m) * scale)
+            l = jnp.sum(e, axis=-1, keepdims=True)
+            r = nn(e.astype(BF), stack[2 * heads + h])
+            heads_out[h, pl.ds(pl.multiple_of(i * tile, tile), tile), :] = (r / l).astype(BF)
+            return 0
+
+        lax.fori_loop(0, T // tile, tile_of, 0)
+
+    def o_cross():
+        return remote(o_send, o_recv, osem.at[0], osem.at[1], p.flip("core"))
+
+    def o_out():
+        for h in range(heads):
+            o_send[:, h * HD : (h + 1) * HD] = heads_out[h, T // 2 :, :HD]
+        o_cross().start()
+
+    def o_home():
+        o_cross().wait_recv()
+        hb = T // 8
+        low = p.core == 0
+        for b in range(4):
+            r = slice(hb * b, hb * (b + 1))
+            mine = jnp.concatenate([heads_out[h, r, :HD] for h in range(heads)], axis=1)
+            other = o_recv[r, :]
+            o_full[b, :, :half] = jnp.where(low, mine, other)
+            o_full[b, :, half:] = jnp.where(low, other, mine)
+        to_homes(p, o_full, attn, hsend, hrecv, START)
+
+    text_load = pltpu.make_async_copy(text, text_w, local_sem.at[3])
+
+    def text_start():
+        g.finish(0)
+        g.finish(1)
+        text_load.start()
+
+    krows = kv.shape[1]
+
+    def kv_product():
+        text_load.wait()
+        for c in range(2):
+            cols = slice(c * WIDE, (c + 1) * WIDE)
+            res = nn(text_mine[...], text_w[:, cols])
+            for z in range(sp):
+                kv_part[z, :, cols] = res[krows * z : krows * (z + 1)].astype(BF)
+        along.start()
+
+    work = [functools.partial(project, i) for i in range(T // tile)]
+    work += [text_start, stage]
+    work += [functools.partial(head, h) for h in range(heads)]
+    work.insert(-5, kv_product)
+    work.insert(-2, along.sum)
+    work += [o_out, o_home]
+    interleave(FIRST, PER, work, [functools.partial(step, t) for t in range(total + 2 * LAG)])
+    for i in range(2, total):
+        g.finish(i)
+    for i in range(n):
+        for copy in pieces(i):
+            copy.wait_send()
+    for r in range(1, sp):
+        down_z(r).wait_send()
+    to_homes(p, o_full, attn, hsend, hrecv, WAIT_RECV)
+    to_homes(p, o_full, attn, hsend, hrecv, WAIT_SEND)
+    o_cross().wait_send()
+    along.end()
+
+
+def attend(plan, widths, sp, heads, scale, shards, down_shard, text_shard, h_slot, qkv_w, text_mine):
+    n = len(plan)
+    total = n + sp + 2
+    T = 8 * h_slot.shape[2]
+    half = heads * HD
+    trows = text_shard.shape[0]
+    krows = text_mine.shape[0] // sp
+    any_space = pl.BlockSpec(memory_space=pl.ANY)
+    vmem = pl.BlockSpec(memory_space=pltpu.VMEM)
+    dma = pltpu.SemaphoreType.DMA
+    shape = jax.ShapeDtypeStruct
+    return pl.pallas_call(
+        functools.partial(attend_kernel, plan, sp, heads, scale, len(widths)),
+        out_shape=[shape((8 * BLOCK, w), BF) for w in widths]
+        + [
+            shape((8 * sp * down_shard.shape[0], WIDE), BF),
+            shape((8 * trows, 2 * WIDE), BF),
+            shape((T, 3 * half), BF),
+            shape((4, T // 8, WIDE), BF),
+            shape((sp, krows, 2 * WIDE), BF),
+        ],
+        in_specs=[vmem, any_space, any_space, vmem, vmem, vmem],
+        out_specs=[any_space] * (len(widths) + 2) + [vmem] * 3,
+        scratch_shapes=[
+            pltpu.VMEM((n, sp, PIECE, WIDE), BF),
+            pltpu.VMEM((2, BLOCK, WIDE), BF),
+            pltpu.VMEM((3 * heads, T, 128), BF),
+            pltpu.VMEM((heads, T, 128), BF),
+            pltpu.VMEM((T // 2, half), BF),
+            pltpu.VMEM((T // 2, half), BF),
+            pltpu.VMEM((4, T // 8, WIDE), BF),
+            pltpu.VMEM((8 * trows, 2 * WIDE), BF),
+            pltpu.VMEM((sp, krows, 2 * WIDE), BF),
+            pltpu.VMEM((sp - 1, krows, 2 * WIDE), BF),
+            dma((total, 7)),
+            dma((total, 7)),
+            dma((n, sp - 1)),
+            dma((n, sp - 1)),
+            dma((sp - 1,)),
+            dma((sp,)),
+            dma((4,)),
+            dma((2,)),
+            dma((4,)),
+            dma((4,)),
+            dma((sp - 1,)),
+            dma((sp - 1,)),
+            dma((sp - 1,)),
+            dma((sp - 1,)),
+        ],
+        compiler_params=pltpu.CompilerParams(
+            collective_id=5, has_side_effects=True, vmem_limit_bytes=56 * 2**20
+        ),
+        cost_estimate=pl.CostEstimate(flops=2**34, bytes_accessed=2**28, transcendentals=2**23),
+        name="attend",
+    )(shards, down_shard, text_shard, h_slot, qkv_w, text_mine)
+
+
+def split(refs, *counts):
+    out = []
+    for c in counts:
+        out.append(refs[:c])
+        refs = refs[c:]
+    return out + [refs]
+
+
+def attend_back_kernel(make, sp, heads, scale, *refs):
+    sums = make()
+    n_in = sums.n_in
+    arrays, (go_blocks, qkv, kv_part), results, (g, kv), landings, scratch, rest = split(
+        refs, n_in, 3, len(sums.results), 2, len(sums.landings), len(sums.scratch)
+    )
+    names = SimpleNamespace()
+    for group_names, group_refs in ((sums.results, results), (sums.landings, landings), (sums.scratch, scratch)):
+        names.__dict__.update(zip(group_names, group_refs))
+    go_in, go_away, go_half, part, acc, gsend, grecv, esem, ksend, krecv = rest
+    p = Place(sp)
+    greet_list([p.flip(b) for b in ("core", "x", "y")] + group(p))
+    sums.bind(p, arrays, names)
+    to_owners(p, go_blocks, go_in, gsend, grecv, START)
+    sums.begin()
+    kv[p.z] = kv_part[...]
+
+    def shares():
+        own = kv.at[p.z]
+        return [remote(own, own, ksend.at[r - 1], krecv.at[r - 1], p.along(r)) for r in range(1, sp)]
+
+    T = qkv.shape[0]
+    half = heads * HD
+    rows = T // 8
+
+    def cross():
+        return remote(go_away, go_half.at[1], esem.at[0], esem.at[1], p.flip("core"))
+
+    def cut():
+        to_owners(p, go_blocks, go_in, gsend, grecv, WAIT_RECV)
+        low = p.core == 0
+        for b in range(4):
+            first, other = go_in[b, :, :half], go_in[b, :, half:]
+            go_half[0, b] = jnp.where(low, first, other)
+            go_away[b] = jnp.where(low, other, first)
+        cross().start()
+
+    tile = 256
+
+    def head(h):
+        if h == 0:
+            cross().wait_recv()
+        for k in range(3):
+            c = (k * heads + h) * HD
+            part[k, :, :HD] = qkv[:, c : c + HD]
+        for b in range(8):
+            part[3, rows * b : rows * (b + 1), :HD] = go_half[b // 4, b % 4, :, h * HD : (h + 1) * HD]
+        acc[...] = jnp.zeros(acc.shape, F32)
+
+        def cols(i, _):
+            sl = pl.ds(pl.multiple_of(i * tile, tile), tile)
+            q, go = part[0, sl, :], part[3, sl, :]
+            k, v = part[1], part[2]
+            s = nt(k, q)
+            m = jnp.max(s, axis=0, keepdims=True)
+            e = jnp.exp((s - m) * scale)
+            pr = e * (1.0 / jnp.sum(e, axis=0, keepdims=True))
+            t = nt(v, go) * pr
+            ds = (t - pr * jnp.sum(t, axis=0, keepdims=True)).astype(BF)
+            acc[0] += nn(ds, q)
+            acc[1] += nn(pr.astype(BF), go)
+            part[0, sl, :] = (tn(ds, k) * scale).astype(BF)
+            return 0
+
+        lax.fori_loop(0, T // tile, cols, 0)
+        c = h * HD
+        g[:, c : c + HD] = part[0, :, :HD]
+        c += half
+        g[:, c : c + HD] = (acc[0, :, :HD] * scale).astype(BF)
+        c += half
+        g[:, c : c + HD] = acc[1, :, :HD].astype(BF)
+
+    part[...] = jnp.zeros(part.shape, BF)
+    work = [cut] + [functools.partial(head, h) for h in range(heads)]
+    work.insert(2, lambda: [copy.start() for copy in shares()])
+    interleave(2, 1, work, sums.steps())
+    sums.end()
+    for copy in shares():
+        copy.wait()
+    to_owners(p, go_blocks, go_in, gsend, grecv, WAIT_SEND)
+    cross().wait_send()
+
+
+def attend_back(plan, sp, heads, scale, grads, go_blocks, qkv, kv_part):
+    def make():
+        sums = Sums(sp, plan, False, 0, 0)
+        sums.n_in = len(grads)
+        return sums
+
+    sums = make()
+    T = qkv.shape[0]
+    half = heads * HD
+    any_space = pl.BlockSpec(memory_space=pl.ANY)
+    vmem = pl.BlockSpec(memory_space=pltpu.VMEM)
+    dma = pltpu.SemaphoreType.DMA
+    out = pl.pallas_call(
+        functools.partial(attend_back_kernel, make, sp, heads, scale),
+        out_shape=list(sums.results.values()) + [jax.ShapeDtypeStruct(a, BF) for a in (qkv.shape, (sp,) + kv_part.shape)] + list(sums.landings.values()),
+        in_specs=[any_space] * len(grads) + [vmem] * 3,
+        out_specs=[vmem] * (len(sums.results) + 2) + [any_space] * len(sums.landings),
+        scratch_shapes=list(sums.scratch.values())
+        + [
+            pltpu.VMEM((4, T // 8, WIDE), BF),
+            pltpu.VMEM((4, T // 8, half), BF),
+            pltpu.VMEM((2, 4, T // 8, half), BF),
+            pltpu.VMEM((4, T, 128), BF),
+            pltpu.VMEM((2, T, 128), F32),
+            dma((4,)),
+            dma((4,)),
+            dma((2,)),
+            dma((sp - 1,)),
+            dma((sp - 1,)),
+        ],
+        compiler_params=pltpu.CompilerParams(
+            collective_id=6, has_side_effects=True, vmem_limit_bytes=60 * 2**20
+        ),
+        cost_estimate=pl.CostEstimate(flops=2**35, bytes_accessed=2**28, transcendentals=2**23),
+        name="attend_back",
+    )(*sums.arrays(grads), go_blocks, qkv, kv_part)
+    return out[:3]
+
+
+def finish_kernel(make, sp, *refs):
+    sums = make()
+    arrays, (gh, resid, grad_one, mod, small), results, (out, small_all), landings, scratch, rest = split(
+        refs, sums.n_in, 5, len(sums.results), 2, len(sums.landings), len(sums.scratch)
+    )
+    names = SimpleNamespace()
+    for group_names, group_refs in ((sums.results, results), (sums.landings, landings), (sums.scratch, scratch)):
+        names.__dict__.update(zip(group_names, group_refs))
+    home, gh_in, blocks, mine, mine_in, partial, hsend, hrecv, esem, s1, r1, s2, r2 = rest
+    p = Place(sp)
+    near = others(p)
+    greet_list(near + group(p))
+    sums.bind(p, arrays, names)
+
+    def cross():
+        return remote(gh.at[1], gh_in, esem.at[0], esem.at[1], p.flip("core"))
+
+    cross().start()
+    sums.begin()
+    half_rows = gh.shape[2]
+    slots = resid.shape[0]
+
+    def add():
+        cross().wait_recv()
+        step = 16
+        for b in range(4):
+
+            def tile(i, _):
+                r = pl.ds(pl.multiple_of(i * step, step), step)
+                blocks[b, r, :] = (gh[0, b, r, :] + gh_in[b, r, :]).astype(BF)
+                return 0
+
+            lax.fori_loop(0, half_rows // step, tile, 0)
+        to_homes(p, blocks, home, hsend, hrecv, START)
+
+    def tail():
+        to_homes(p, blocks, home, hsend, hrecv, WAIT_RECV)
+        step = 32
+        partial[...] = jnp.zeros(partial.shape, F32)
+        for b in range(4):
+            s, k = b // 2, b % 2
+
+            def tile(i, _):
+                start = pl.multiple_of(i * step, step)
+                r = pl.ds(k * half_rows + start, step)
+                v = resid[s, r, :]
+                c = v - jnp.mean(v, axis=-1, keepdims=True)
+                inv = lax.rsqrt(jnp.mean(c * c, axis=-1, keepdims=True) + 1e-06)
+                n = c * inv
+                g = home[b, pl.ds(start, step), :].astype(F32)
+                gn = g * n
+                partial[s, 0] += sum(g[8 * j : 8 * j + 8] for j in range(step // 8))
+                partial[s, 1] += sum(gn[8 * j : 8 * j + 8] for j in range(step // 8))
+                d = g * (1.0 + mod[slots + s : slots + s + 1, :])
+                back = d - jnp.mean(d, axis=-1, keepdims=True) - n * jnp.mean(d * n, axis=-1, keepdims=True)
+                out[s, r, :] = grad_one[s, r, :] + back * inv
+                return 0
+
+            lax.fori_loop(0, half_rows // step, tile, 0)
+        mine[...] = small[...]
+        for s in range(slots):
+            for j in range(2):
+                mine[slots * j + s : slots * j + s + 1, :] = jnp.sum(partial[s, j], axis=0, keepdims=True)
+        for copy in along():
+            copy.start()
+
+    def along():
+        return [remote(mine, mine_in.at[r - 1], s1.at[r - 1], r1.at[r - 1], p.along(r)) for r in range(1, sp)]
+
+    def share(m):
+        own = small_all.at[p.f]
+        return remote(own, own, s2.at[m], r2.at[m], near[m])
+
+    def total():
+        for copy in along():
+            copy.wait_recv()
+        small_all[p.f] = mine[...] + sum(mine_in[r] for r in range(sp - 1))
+        for m in range(7):
+            share(m).start()
+
+    idle = lambda: None
+    interleave(1, 1, [add, idle, idle, idle, tail, idle, total], sums.steps())
+    sums.end()
+    for m in range(7):
+        share(m).wait()
+    for copy in along():
+        copy.wait_send()
+    to_homes(p, blocks, home, hsend, hrecv, WAIT_SEND)
+    cross().wait_send()
+
+
+def finish(sp, down, text, halves, gh, resid, grad_one, mod, small):
+    half = halves.shape[1]
+
+    def make():
+        sums = Sums(sp, [], True, text.shape[0] // 8, half)
+        sums.n_in = 3
+        return sums
+
+    sums = make()
+    rows = gh.shape[2]
+    any_space = pl.BlockSpec(memory_space=pl.ANY)
+    vmem = pl.BlockSpec(memory_space=pltpu.VMEM)
+    dma = pltpu.SemaphoreType.DMA
+    shape = jax.ShapeDtypeStruct
+    out = pl.pallas_call(
+        functools.partial(finish_kernel, make, sp),
+        out_shape=list(sums.results.values())
+        + [shape(resid.shape, F32), shape((8,) + small.shape, F32)]
+        + list(sums.landings.values()),
+        in_specs=[any_space] * 3 + [vmem] * 5,
+        out_specs=[vmem] * (len(sums.results) + 2) + [any_space] * len(sums.landings),
+        scratch_shapes=list(sums.scratch.values())
+        + [
+            pltpu.VMEM((4, rows, WIDE), BF),
+            pltpu.VMEM((4, rows, WIDE), F32),
+            pltpu.VMEM((4, rows, WIDE), BF),
+            pltpu.VMEM(small.shape, F32),
+            pltpu.VMEM((sp - 1,) + small.shape, F32),
+            pltpu.VMEM((2, 2, 8, WIDE), F32),
+            dma((4,)),
+            dma((4,)),
+            dma((2,)),
+            dma((sp - 1,)),
+            dma((sp - 1,)),
+            dma((7,)),
+            dma((7,)),
+        ],
+        compiler_params=pltpu.CompilerParams(
+            collective_id=7, has_side_effects=True, vmem_limit_bytes=60 * 2**20
+        ),
+        name="finish",
+    )(*sums.arrays([], down, text, halves), gh, resid, grad_one, mod, small)
+    return out[:5]
+
+
+def temporal_kernel(heads, scale, trip, go, out, g):
+    slots, rows, width = go.shape
+    lanes = lax.broadcasted_iota(jnp.int32, (width, 128), 0) // HD
+    member = (lanes == lax.broadcasted_iota(jnp.int32, (width, 128), 1)).astype(F32).astype(BF)
+    across = lax.broadcasted_iota(jnp.int32, (128, width), 1) // HD
+    member_t = (across == lax.broadcasted_iota(jnp.int32, (128, width), 0)).astype(F32).astype(BF)
+    pairs = [(a, b) for a in range(slots) for b in range(slots)]
+
+    def part(a, k):
+        return trip[a, :, k * width : (k + 1) * width].astype(F32)
+
+    def per_head(x):
+        high = x.astype(BF)
+        return nn(high, member) + nn((x - high.astype(F32)).astype(BF), member)
+
+    def wide(x):
+        return nn(x.astype(BF), member_t)
+
+    s = {(a, b): per_head(part(a, 0) * part(b, 1)) * scale for a, b in pairs}
+    p = {}
+    for a in range(slots):
+        m = functools.reduce(jnp.maximum, [s[a, b] for b in range(slots)])
+        e = [jnp.exp(s[a, b] - m) for b in range(slots)]
+        total = sum(e)
+        for b in range(slots):
+            p[a, b] = e[b] / total
+    pw = {k: wide(v) for k, v in p.items()}
+    d = [go[a].astype(F32) for a in range(slots)]
+    for a in range(slots):
+        out[a] = sum(pw[a, b] * part(b, 2) for b in range(slots)).astype(BF)
+    for b in range(slots):
+        g[b, :, 2 * width :] = sum(pw[a, b] * d[a] for a in range(slots)).astype(BF)
+    dp = {(a, b): per_head(d[a] * part(b, 2)) for a, b in pairs}
+    ds = {}
+    for a in range(slots):
+        mean = sum(dp[a, b] * p[a, b] for b in range(slots))
+        for b in range(slots):
+            ds[a, b] = wide(p[a, b] * (dp[a, b] - mean))
+    for a in range(slots):
+        g[a, :, :width] = (scale * sum(ds[a, b] * part(b, 1) for b in range(slots))).astype(BF)
+        g[a, :, width : 2 * width] = (scale * sum(ds[b, a] * part(b, 0) for b in range(slots))).astype(BF)
+
+
+def temporal(trip, go, heads, scale):
+    slots, patches, width = go.shape
+    rows = 64
+    block = lambda w: pl.BlockSpec((slots, rows, w), lambda i: (0, i, 0))
+    return pl.pallas_call(
+        functools.partial(temporal_kernel, heads, scale),
+        grid=(patches // rows,),
+        out_shape=[jax.ShapeDtypeStruct((slots, patches, w), BF) for w in (width, 3 * width)],
+        in_specs=[block(3 * width), block(width)],
+        out_specs=[block(width), block(3 * width)],
+        compiler_params=pltpu.CompilerParams(vmem_limit_bytes=48 * 2**20),
+        cost_estimate=pl.CostEstimate(flops=2**32, bytes_accessed=2**24, transcendentals=2**16),
+        name="temporal",
+    )(trip, go)
+
+
 HEADS = 16
 EPS = 1e-06
 HIGHEST = lax.Precision.HIGHEST
 BOTH = ("fsdp", "sp")
+PLAN = (
+    [(0, 0), (1, 0), (2, 0)] + [(3, k * WIDE) for k in range(4)] + [(4, k * WIDE) for k in range(3)] + [(5, 0)]
+)
 
 
 def normalize(values):
@@ -161,6 +1669,15 @@
 def scatter(grad):
     part = lax.psum_scatter(grad.astype(BF), "fsdp", scatter_dimension=0, tiled=True)
     return lax.psum_scatter(part, "sp", scatter_dimension=0, tiled=True).astype(F32)
+
+
+def sum_along(parts, sp):
+    z = lax.axis_index("sp")
+    total = lax.dynamic_index_in_dim(parts, z, 0, keepdims=False).astype(F32)
+    for r in range(1, sp):
+        part = lax.dynamic_index_in_dim(parts, (z + r) % sp, 0, keepdims=False)
+        total += lax.ppermute(part, "sp", [(k, (k + r) % sp) for k in range(sp)]).astype(F32)
+    return total.astype(BF)
 
 
 class Moves:
@@ -186,16 +1703,20 @@
             t = (self.z - r) % self.sp
             block = lax.dynamic_index_in_dim(blocks, t, 0, keepdims=False)
             got.append(lax.ppermute(block, BOTH, pairs))
-        return jnp.concatenate(got, axis=0)
+        return jnp.roll(jnp.stack(got), self.mine(), axis=0).reshape(tokens.shape)
 
     def home(self, tokens):
         rows = tokens.shape[0] // self.sp
+        tokens = jnp.roll(tokens.reshape(self.sp, rows, -1), -self.mine(), axis=0).reshape(tokens.shape)
         out = jnp.zeros((self.sp, rows, tokens.shape[1]), tokens.dtype)
         for r, pairs in enumerate(self.rounds):
             back = lax.ppermute(tokens[r * rows : (r + 1) * rows], BOTH, [(b, a) for a, b in pairs])
             t = (self.z - r) % self.sp
             out = lax.dynamic_update_index_in_dim(out, back, t, 0)
         return out.reshape(tokens.shape)
+
+    def mine(self):
+        return 2 * (self.z % 2) + self.core
 
     def exchange(self, array):
         return lax.ppermute(array, "fsdp", self.swap)
@@ -241,59 +1762,107 @@
     cond = condition[0]
     cond_used = jnp.where((chosen == 0)[:, None], cond[0][None], cond[1][None])
     silu_low = jax.nn.silu(cond_used).astype(BF)
-    silu_all = lax.all_gather(silu_low, "fsdp", axis=0, tiled=True)
-    silu_rows = lax.dynamic_slice_in_dim(silu_all, (f_index * sp + z_index) * rows, rows, 1)
-    mod_part = nn(silu_rows, w_ada.astype(BF))
-    modulation = lax.psum(
-        lax.psum_scatter(mod_part, "fsdp", scatter_dimension=0, tiled=True), "sp"
-    ).reshape(slots, 6, 1, width)
-    shift_one, scale_one, gate_one, shift_two, scale_two, gate_two = (modulation[:, i] for i in range(6))
-
+    text = text_states[0]
+    text_used = jnp.where((chosen == 0)[:, None, None], text[0][None], text[1][None])
+    kv_rows = w_cross_kv.shape[0]
+    text_cut = text_used.reshape(slots * text_local, fsdp, sp, kv_rows)
     heads_half = HEADS // 2
     half = heads_half * HD
-    qkv_full = gather(w_qkv)
-    qkv_half = lax.dynamic_index_in_dim(
-        qkv_full.reshape(width, 3, 2, half), core, 2, keepdims=False
-    ).reshape(width, 3 * half)
-    vectors = lax.all_gather(jnp.stack([g_cross, g_temp, t_gate]).astype(BF), BOTH, axis=1, tiled=True).astype(F32)
-    gain_cross, gain_temp, temp_gate = vectors[0], vectors[1], vectors[2]
-    out_full = gather(w_out)
-    cross_q_full = gather(w_cross_q)
-    cross_out_full = gather(w_cross_out)
-    up_full = gather(w_up)
-    down_full = gather(w_down)
-    temp_qkv_full = gather(w_temp_qkv)
-    temp_out_full = gather(w_temp_out)
-
-    kv_rows = w_cross_kv.shape[0]
-    kv_weight = lax.all_gather(w_cross_kv.astype(BF), "fsdp", axis=0, tiled=True)
-    text = text_states[0]
-    text_used = jnp.where((chosen == 0)[:, None, None], text[0][None], text[1][None])
-    text_cut = text_used.reshape(slots * text_local, fsdp, sp, kv_rows)
-    text_mine = lax.all_to_all(text_cut, "sp", split_axis=2, concat_axis=0, tiled=True)
-    text_mine = text_mine.reshape(sp * slots * text_local, fsdp * kv_rows)
-    kv_part = lax.psum_scatter(nn(text_mine, kv_weight), "sp", scatter_dimension=0, tiled=True).astype(BF)
-    kv_all = (
-        lax.all_gather(kv_part.reshape(1, slots, text_local, 2 * width), "sp", axis=0, tiled=True)
-        .transpose(1, 0, 2, 3)
-        .reshape(slots, sp * text_local, 2 * width)
-    )
-
     resid = residual_in[0]
     normed_one = normalize(resid)
-    h_one = (normed_one * (1.0 + scale_one) + shift_one).astype(BF).reshape(tok, width)
-    h_mine = moves.out(h_one)
-    h_slot = jnp.concatenate([h_mine, moves.exchange(h_mine)], axis=0)
-    qkv = nn(h_slot, qkv_half).astype(BF)
-    o_slot = spatial_fwd(qkv, heads_half, scale)
-    o_mine = o_slot[:tok]
-    o_other = moves.exchange(o_slot[tok:])
-    o_full = jnp.where(
-        core == 0,
-        jnp.concatenate([o_mine, o_other], axis=1),
-        jnp.concatenate([o_other, o_mine], axis=1),
-    )
-    attn_tok = moves.home(o_full)
+    small_slice = fsdp == 8 and sp == 4
+    stacked_vectors = jnp.stack([g_cross, g_temp, t_gate]).astype(BF)
+    if small_slice:
+        qkv_shards = w_qkv.astype(BF).reshape(rows, 3, 2, half).transpose(2, 0, 1, 3).reshape(2, rows, 3 * half)
+        silu_blocks = silu_low.astype(F32).reshape(slots, fsdp * sp, rows).transpose(1, 0, 2)
+        qkv_half, h_slot, mod_rows, vectors, text_mine, silu_rows = front(
+            sp,
+            qkv_shards,
+            w_ada.astype(BF),
+            jnp.pad(silu_blocks, ((0, 0), (0, TILE - slots), (0, 0))),
+            jnp.pad(stacked_vectors, ((0, 2 * TILE - 3), (0, 0))),
+            text_cut.transpose(2, 0, 1, 3).reshape(sp, slots * text_local, fsdp * kv_rows),
+            resid,
+        )
+        silu_rows = silu_rows[:, :slots].reshape(fsdp * slots, rows).astype(BF)
+        modulation = mod_rows[: 6 * slots].reshape(6, slots, 1, width)
+        vectors = vectors[:, :, :3].transpose(2, 0, 1, 3).reshape(3, width)
+        low = [w.astype(BF) for w in (w_out, w_cross_q, w_cross_out, w_up, w_temp_qkv, w_temp_out)]
+        shards = jnp.stack([low[o][:, c : c + width] for o, c in PLAN])
+        (
+            out_full,
+            cross_q_full,
+            cross_out_full,
+            up_full,
+            temp_qkv_full,
+            temp_out_full,
+            down_full,
+            _,
+            qkv,
+            attn_tok,
+            kv_all,
+        ) = attend(
+            PLAN,
+            [w.shape[1] for w in low],
+            sp,
+            heads_half,
+            scale,
+            shards,
+            w_down.astype(BF),
+            w_cross_kv.astype(BF),
+            h_slot,
+            qkv_half,
+            text_mine,
+        )
+        h_slot = h_slot.reshape(2 * tok, width)
+        attn_tok = attn_tok.reshape(tok, width)
+        kv_all = (
+            kv_all.reshape(sp, slots, text_local, 2 * width)
+            .transpose(1, 0, 2, 3)
+            .reshape(slots, sp * text_local, 2 * width)
+        )
+        shift_one, scale_one, gate_one, shift_two, scale_two, gate_two = (modulation[i] for i in range(6))
+    else:
+        silu_all = lax.all_gather(silu_low, "fsdp", axis=0, tiled=True)
+        silu_rows = lax.dynamic_slice_in_dim(silu_all, (f_index * sp + z_index) * rows, rows, 1)
+        modulation = lax.psum(
+            lax.psum_scatter(nn(silu_rows, w_ada.astype(BF)), "fsdp", scatter_dimension=0, tiled=True), "sp"
+        ).reshape(slots, 6, 1, width)
+        shift_one, scale_one, gate_one, shift_two, scale_two, gate_two = (modulation[:, i] for i in range(6))
+        vectors = lax.all_gather(stacked_vectors, BOTH, axis=1, tiled=True).astype(F32)
+        qkv_half = lax.dynamic_index_in_dim(
+            gather(w_qkv).reshape(width, 3, 2, half), core, 2, keepdims=False
+        ).reshape(width, 3 * half)
+        out_full = gather(w_out)
+        cross_q_full = gather(w_cross_q)
+        cross_out_full = gather(w_cross_out)
+        up_full = gather(w_up)
+        down_full = gather(w_down)
+        temp_qkv_full = gather(w_temp_qkv)
+        temp_out_full = gather(w_temp_out)
+        kv_weight = lax.all_gather(w_cross_kv.astype(BF), "fsdp", axis=0, tiled=True)
+        text_mine = lax.all_to_all(text_cut, "sp", split_axis=2, concat_axis=0, tiled=True)
+        text_mine = text_mine.reshape(sp * slots * text_local, fsdp * kv_rows)
+        kv_part = lax.psum_scatter(nn(text_mine, kv_weight), "sp", scatter_dimension=0, tiled=True).astype(BF)
+        kv_all = (
+            lax.all_gather(kv_part.reshape(1, slots, text_local, 2 * width), "sp", axis=0, tiled=True)
+            .transpose(1, 0, 2, 3)
+            .reshape(slots, sp * text_local, 2 * width)
+        )
+        h_one = (normed_one * (1.0 + scale_one) + shift_one).astype(BF).reshape(tok, width)
+        h_mine = moves.out(h_one)
+        h_slot = jnp.concatenate([h_mine, moves.exchange(h_mine)], axis=0)
+        qkv = nn(h_slot, qkv_half).astype(BF)
+        o_slot = spatial_fwd(qkv, heads_half, scale)
+        o_mine = o_slot[:tok]
+        o_other = moves.exchange(o_slot[tok:])
+        o_full = jnp.where(
+            core == 0,
+            jnp.concatenate([o_mine, o_other], axis=1),
+            jnp.concatenate([o_other, o_mine], axis=1),
+        )
+        attn_tok = moves.home(o_full)
+    gain_cross, gain_temp, temp_gate = vectors[0], vectors[1], vectors[2]
     branch_one = nn(attn_tok, out_full).reshape(slots, patches, width)
     x_one = resid + gate_one * branch_one
 
@@ -313,48 +1882,18 @@
 
     normed_four = normalize(x_three)
     temp_in = (normed_four * gain_temp).astype(BF).reshape(tok, width)
-    trip = nn(temp_in, temp_qkv_full).astype(BF).reshape(slots, patches, 3, width)
-    tq = [trip[a, :, 0].astype(F32) for a in range(slots)]
-    tk = [trip[a, :, 1].astype(F32) for a in range(slots)]
-    tv = [trip[a, :, 2].astype(F32) for a in range(slots)]
-    member = (jnp.arange(width)[:, None] // HD == jnp.arange(HEADS)[None, :]).astype(F32)
-    member_low = member.T.astype(BF)
-
-    def per_head(lefts, rights):
-        products = jnp.stack([a * b for a in lefts for b in rights])
-        return jnp.dot(
-            products.reshape(-1, width), member, precision=HIGHEST, preferred_element_type=F32
-        ).reshape(slots, slots, patches, HEADS)
-
-    def spread(values):
-        return nn(values.astype(BF).reshape(-1, HEADS), member_low).reshape(slots, slots, patches, width)
-
-    probs_t = jax.nn.softmax(per_head(tq, tk) * scale, axis=1)
-    probs_wide = spread(probs_t)
-    temp_out = jnp.stack(
-        [sum(probs_wide[a, b] * tv[b] for b in range(slots)) for a in range(slots)]
-    ).astype(BF).reshape(tok, width)
+    trip = nn(temp_in, temp_qkv_full).astype(BF).reshape(slots, patches, 3 * width)
+    grad_out = cotangent[0].astype(F32)
+    grad_b4 = (grad_out * (video * temp_gate)).astype(BF).reshape(tok, width)
+    grad_to = nt(grad_b4, temp_out_full).astype(BF).reshape(slots, patches, width)
+    temp_out, grad_trip = temporal(trip, grad_to, HEADS, scale)
+    temp_out = temp_out.reshape(tok, width)
+    grad_trip = grad_trip.reshape(tok, 3 * width)
     branch_four = nn(temp_out, temp_out_full).reshape(slots, patches, width)
     output = x_three + (video * temp_gate) * branch_four
 
-    grad_out = cotangent[0].astype(F32)
     grad_tgate = video * jnp.sum(grad_out * branch_four, axis=(0, 1))
-    grad_b4 = (grad_out * (video * temp_gate)).astype(BF).reshape(tok, width)
     grad_wto = tn(temp_out, grad_b4)
-    grad_to = nt(grad_b4, temp_out_full).astype(BF).astype(F32).reshape(slots, patches, width)
-    grad_to = [grad_to[a] for a in range(slots)]
-    dp_t = per_head(grad_to, tv)
-    ds_t = probs_t * (dp_t - jnp.sum(dp_t * probs_t, axis=1, keepdims=True))
-    ds_wide = spread(ds_t)
-    pairs = range(slots)
-    grad_trip = jnp.stack(
-        [
-            jnp.stack([scale * sum(ds_wide[a, b] * tk[b] for b in pairs) for a in pairs]),
-            jnp.stack([scale * sum(ds_wide[a, b] * tq[a] for a in pairs) for b in pairs]),
-            jnp.stack([sum(probs_wide[a, b] * grad_to[a] for a in pairs) for b in pairs]),
-        ],
-        axis=2,
-    ).astype(BF).reshape(tok, 3 * width)
     grad_wtq = tn(temp_in, grad_trip)
     grad_temp_in = nt(grad_trip, temp_qkv_full).reshape(slots, patches, width)
     grad_gtemp = jnp.sum(grad_temp_in * normed_four, axis=(0, 1))
@@ -382,10 +1921,6 @@
         .reshape(sp * slots * text_local, 2 * width)
         .astype(BF)
     )
-    grad_kv = lax.all_gather(
-        lax.psum_scatter(grad_kv, "sp", scatter_dimension=0, tiled=True), "sp", axis=0, tiled=True
-    )
-    grad_wckv = tn(text_mine, grad_kv)
     grad_wcq = tn(cross_in, grad_qc)
     grad_cross_in = nt(grad_qc, cross_q_full).reshape(slots, patches, width)
     grad_gcross = jnp.sum(grad_cross_in * normed_two, axis=(0, 1))
@@ -395,63 +1930,88 @@
     grad_b1 = (grad_one * gate_one).astype(BF).reshape(tok, width)
     grad_wout = tn(attn_tok, grad_b1)
     grad_attn = nt(grad_b1, out_full).astype(BF)
-    go_mine = moves.out(grad_attn)
-    low_half, high_half = go_mine[:, :half], go_mine[:, half:]
-    go_other = moves.exchange(jnp.where(core == 0, high_half, low_half))
-    go_slot = jnp.concatenate([jnp.where(core == 0, low_half, high_half), go_other], axis=0)
-    grad_qkv = spatial_bwd(qkv, go_slot, heads_half, scale)
+    if small_slice:
+        late = [g.astype(BF) for g in (grad_wout, grad_wcq, grad_wco, grad_wup, grad_wtq, grad_wto)]
+        pieces, grad_qkv, grad_kv = attend_back(
+            PLAN,
+            sp,
+            heads_half,
+            scale,
+            late,
+            grad_attn.reshape(sp, tok // sp, width),
+            qkv,
+            sum_along(grad_kv.reshape(sp, slots * text_local, 2 * width), sp),
+        )
+        grad_kv = grad_kv.reshape(sp * slots * text_local, 2 * width)
+        own = [jnp.concatenate([pieces[k] for k, (o, _) in enumerate(PLAN) if o == i], axis=1) for i in range(len(late))]
+        own_out, own_cq, own_co, own_up, own_tq, own_to = own
+    else:
+        go_mine = moves.out(grad_attn)
+        low_half, high_half = go_mine[:, :half], go_mine[:, half:]
+        go_other = moves.exchange(jnp.where(core == 0, high_half, low_half))
+        go_slot = jnp.concatenate([jnp.where(core == 0, low_half, high_half), go_other], axis=0)
+        grad_qkv = spatial_bwd(qkv, go_slot, heads_half, scale)
+        grad_kv = lax.all_gather(
+            lax.psum_scatter(grad_kv, "sp", scatter_dimension=0, tiled=True), "sp", axis=0, tiled=True
+        )
     grad_wqkv_half = tn(h_slot, grad_qkv).astype(BF)
+    grad_wckv = tn(text_mine, grad_kv)
     gh_slot = nt(grad_qkv, qkv_half)
-    gh_mine = (gh_slot[:tok] + moves.exchange(gh_slot[tok:])).astype(BF)
-    grad_h_one = moves.home(gh_mine).astype(F32).reshape(slots, patches, width)
-    grad_shift_one = jnp.sum(grad_h_one, axis=1)
-    grad_scale_one = jnp.sum(grad_h_one * normed_one, axis=1)
-    input_grad = grad_one + normalize_back(resid, grad_h_one * (1.0 + scale_one))
-
-    wide = grad_wqkv_half.reshape(width, 3, 1, half)
-    zeros = jnp.zeros_like(wide)
-    grad_wqkv = jnp.where(
-        core == 0, jnp.concatenate([wide, zeros], axis=2), jnp.concatenate([zeros, wide], axis=2)
-    ).reshape(width, 3 * width)
-
-    small = jnp.concatenate(
-        [
-            jnp.stack(
-                [
-                    grad_shift_one,
-                    grad_scale_one,
-                    grad_gate_one,
-                    grad_shift_two,
-                    grad_scale_two,
-                    grad_gate_two,
-                ],
-                axis=1,
-            ).reshape(slots * 6, width),
-            jnp.stack([grad_gcross, grad_gtemp, grad_tgate]),
-        ],
-        axis=0,
-    )
-    small_all = lax.all_gather(small, BOTH, axis=0).reshape(fsdp, sp, slots * 6 + 3, width)
-    small_sp = jnp.sum(small_all, axis=1)
-    grad_mod = small_sp[:, : slots * 6].reshape(fsdp * slots, 6 * width)
+    known = [grad_gate_one, grad_shift_two, grad_scale_two, grad_gate_two]
+    known_vectors = [grad_gcross, grad_gtemp, grad_tgate]
+    if small_slice:
+        zero = jnp.zeros((slots, width), F32)
+        own_down, own_text, own_half, input_grad, small_sp = finish(
+            sp,
+            grad_wdown.astype(BF),
+            grad_wckv.astype(BF),
+            grad_wqkv_half,
+            gh_slot.reshape(2, sp, tok // sp, width),
+            resid,
+            grad_one,
+            mod_rows,
+            jnp.concatenate([zero, zero] + known + [jnp.stack(known_vectors + [zero[0]])], axis=0),
+        )
+        own_text = own_text.transpose(1, 0, 2).reshape(kv_rows, 2 * width)
+        own_half = jnp.where(core == 0, own_half, own_half[::-1])
+        own_qkv = own_half.reshape(2, rows, 3, half).transpose(1, 2, 0, 3).reshape(rows, 3 * width)
+    else:
+        grad_h_one = moves.home((gh_slot[:tok] + moves.exchange(gh_slot[tok:])).astype(BF))
+        grad_h_one = grad_h_one.astype(F32).reshape(slots, patches, width)
+        input_grad = grad_one + normalize_back(resid, grad_h_one * (1.0 + scale_one))
+        new = [jnp.sum(grad_h_one, axis=1), jnp.sum(grad_h_one * normed_one, axis=1)]
+        small = jnp.concatenate(new + known + [jnp.stack(known_vectors)], axis=0)
+        small_sp = jnp.sum(
+            lax.all_gather(small, BOTH, axis=0).reshape(fsdp, sp, slots * 6 + 3, width), axis=1
+        )
+    grad_mod = small_sp[:, : slots * 6].reshape(fsdp, 6, slots, width).transpose(0, 2, 1, 3)
+    grad_mod = grad_mod.reshape(fsdp * slots, 6 * width)
     grad_wada = jnp.dot(silu_rows.astype(F32).T, grad_mod, precision=HIGHEST, preferred_element_type=F32)
     grad_vec = lax.dynamic_slice_in_dim(
-        jnp.sum(small_sp[:, slots * 6 :], axis=0), (f_index * sp + z_index) * rows, rows, 1
+        jnp.sum(small_sp[:, slots * 6 : slots * 6 + 3], axis=0), (f_index * sp + z_index) * rows, rows, 1
     )
-    grad_wckv = lax.psum_scatter(grad_wckv.astype(BF), "fsdp", scatter_dimension=0, tiled=True).astype(F32)
+    if not small_slice:
+        wide = grad_wqkv_half.reshape(width, 3, 1, half)
+        zeros = jnp.zeros_like(wide)
+        grad_wqkv = jnp.where(
+            core == 0, jnp.concatenate([wide, zeros], axis=2), jnp.concatenate([zeros, wide], axis=2)
+        ).reshape(width, 3 * width)
+        own_qkv, own_out, own_cq, own_co = scatter(grad_wqkv), scatter(grad_wout), scatter(grad_wcq), scatter(grad_wco)
+        own_up, own_down, own_tq, own_to = scatter(grad_wup), scatter(grad_wdown), scatter(grad_wtq), scatter(grad_wto)
+        own_text = lax.psum_scatter(grad_wckv.astype(BF), "fsdp", scatter_dimension=0, tiled=True).astype(F32)
     return (
         output[None],
         input_grad[None],
         grad_wada,
-        scatter(grad_wqkv),
-        scatter(grad_wout),
-        scatter(grad_wcq),
-        grad_wckv,
-        scatter(grad_wco),
-        scatter(grad_wup),
-        scatter(grad_wdown),
-        scatter(grad_wtq),
-        scatter(grad_wto),
+        own_qkv,
+        own_out,
+        own_cq,
+        own_text,
+        own_co,
+        own_up,
+        own_down,
+        own_tq,
+        own_to,
         grad_vec[0],
         grad_vec[1],
         grad_vec[2],

time: 1670 us -> 905 us (0.54)
  waiting for transfers between devices: 664 us -> 0.01 us
  Pallas kernels: 111 us -> 642 us
  blocking collectives: 303 us -> 0 us
  local copies, waits for them, and re-layouts: 245 us -> 47.1 us
  other arithmetic: 76.3 us -> 35.2 us
  starting transfers between devices: 58.4 us -> 21.8 us
  matrix products: 179 us -> 150 us
  between operations: 20.2 us -> 2.91 us
    pallas_call x2 -> x5, Pallas kernels: 86.7 us -> 618 us  [the longest x1 225 us: attend(): pl.pallas_call(functools.partial(attend_kernel, plan, sp, heads, scale, l...]
    all_gather x12 -> x0, waiting for transfers between devices: 341 us -> none  [the longest x8 238 us: gather(): return lax.all_gather(shard.astype(BF), BOTH, axis=0, tiled=True)]
    reduce_scatter x9 -> x0, waiting for transfers between devices: 177 us -> none  [the longest x7 108 us: scatter(): lax.psum_scatter(grad.astype(BF), 'fsdp', scatter_dimension=0, tiled=True)]
    unnamed x2 -> x0, blocking collectives: 149 us -> none
    unnamed x303 -> x192, local copies, waits for them, and re-layouts: 134 us -> 18 us
    all_gather x2 -> x0, blocking collectives: 115 us -> none  [the longest x1 104 us: local(): lax.all_gather(jnp.stack([g_cross, g_temp, t_gate]).astype(BF), BOTH, axi...]
    unnamed x35 -> x0, waiting for transfers between devices: 77.9 us -> none
    ppermute x20 -> x3, waiting for transfers between devices: 67.1 us -> 0.01 us  [sum_along(): lax.ppermute(part, 'sp', [(k, (k + r) % sp) for k in range(sp)]).astype(F32)]
  transfers between devices with their start and end apart: 52 -> 3, of which waited for: 23 -> 0; matrix products, arithmetic and copies ran while one was open for 34% -> 6% of each run, Pallas kernels for 7% -> 0%
where the time goes in v2:
time: 905 us; the launch traced here: 899 us
  Pallas kernels  642 us (71%)
  matrix products  150 us (17%)
  local copies, waits for them, and re-layouts  47.1 us (5%)
  other arithmetic  35.2 us (4%)
  starting transfers between devices  21.8 us (2%)
    pallas_call x1, Pallas kernels, attend(): pl.pallas_call(functools.partial(attend_kernel, plan, sp, heads, scale, l...  225 us
    pallas_call x1, Pallas kernels, attend_back(): pl.pallas_call(functools.partial(attend_back_kernel, make, sp, heads, sca...  164 us
    pallas_call x1, Pallas kernels, finish(): pl.pallas_call(functools.partial(finish_kernel, make, sp), out_shape=list...  142 us
    pallas_call x1, Pallas kernels, front(): pl.pallas_call(functools.partial(front_kernel, sp), out_shape=[shape((8 *...  78.3 us
    dot_general x8, matrix products, nt(): lax.dot_general(a, b, (((1,), (1,)), ((), ())), preferred_element_type=F32)  57.1 us
    dot_general x9, matrix products, tn(): lax.dot_general(a, b, (((0,), (0,)), ((), ())), preferred_element_type=F32)  51.5 us
    dot_general x7, matrix products, nn(): return jnp.dot(a, b, preferred_element_type=F32)  39.9 us
    ppermute x3, starting transfers between devices, sum_along(): lax.ppermute(part, 'sp', [(k, (k + r) % sp) for k in range(sp)]).astype(F32)  21.8 us
  transfers between devices with their start and end apart: 3, of which 0 were waited for; matrix products, arithmetic and copies ran while one was open for 6% of the time, Pallas kernels for 0%

profile of v2, /device:TPU:0, one launch (start us, length us, event | category | flops | bytes accessed | tf_op | source)
XLA Modules:
  0.0 899.3 jit_solution(2138818532484924798)
XLA Ops:
  16.1 78.3 %front.1 = (bf16[1152,1728]{1,0:T(8,128)(2,1)}, bf16[2,4,128,1152]{3,2,1,0:T(8,128)(2,1)S(1)}, f32[16,1152]{1,0:T(8,128)S(1)}, f32[8,4,8,36]{3,2,1,0:T(8,128)S(1...) custom-call(bf16[2,36,1728]{2,1,0:T(8,128)(2,1)S(1)} %copy.92.shards, ...), custom_call_target="tpu_custom_call" | custom-call | tf_op jit(solution)/shard_map/front/pallas_call | solution.py:995
  98.1 225.4 %attend.1 = (bf16[1152,1152]{1,0:T(8,128)(2,1)}, bf16[1152,1152]{1,0:T(8,128)(2,1)}, bf16[1152,1152]{1,0:T(8,128)(2,1)}, bf16[1152,4608]{1,0:T(8,128)(2,1)}, bf1...) custom-call(bf16[11,36,1152]{2,1,0:T(8,128)(2,1)} %copy-done.74, ...), custom_call_target="tpu_custom_call" | custom-call | flops 17179869184 | bytes 268435456 | tf_op jit(solution)/shard_map/attend/pallas_call | solution.py:1276
  327.9 3.3 fusion.53
  336.1 14.2 %cross_fwd.1 = bf16[2,256,1152]{2,1,0:T(8,128)(2,1)S(1)} custom-call(bf16[2,256,1152]{2,1,0:T(8,128)(2,1)S(1)} %bitcast.262, bf16[2,120,2304]{2,1,0:T(8,128)(2,1)S(1)} %copy.96.kv), custom_call_target="tpu_custom_call" | custom-call | flops 503316480 | bytes 2359296 | tf_op jit(solution)/shard_map/cross_fwd/pallas_call | solution.py:106
  353.4 8.7 fusion.59
  362.0 12.7 %fusion.51 = f32[512,1152]{1,0:T(8,128)S(1)} fusion(bf16[4608,1152]{1,0:T(8,128)(2,1)} %get-tuple-element.54, f32[512,4608]{1,0:T(8,128)} %fusion.59), kind=kOutput, calls=%fused_computation.169 | convolution fusion | flops 5457051648 | bytes 22413312 | tf_op jit(solution)/shard_map/dot_general | solution.py:11
  379.7 6.4 convolution_convert_fusion.4
  386.2 8.9 temporal.1
  395.1 9.6 %multiply_reduce_fusion.6 = (f32[2,256]{1,0:T(2,128)S(1)}, f32[2,256,1152]{2,1,0:T(8,128)S(1)}) fusion(f32[2,256,1152]{2,1,0:T(8,128)S(1)} %get-tuple-element.133, f32[1152]{0:T(1024)S(1)} %mul.339, f32[2,256]{1,0:T(2,128)S(1)} %broadcast_multiply_fusion.1, bf16[2,256,3456]{2,1,0:T(8,128)(2,1)S(1)} %get-tuple-element.58, ...), kind=kOutput, calls=%fused_computation.61 | convolution fusion | flops 4079222272 | bytes 16228864 | tf_op jit(solution)/shard_map/dot_general | solution.py:9
  406.8 5.0 fusion.21
  411.9 17.2 %fusion.7 = bf16[512,4608]{1,0:T(8,128)(2,1)} fusion(f32[512,4608]{1,0:T(8,128)} %fusion.59, bf16[512,1152]{1,0:T(8,128)(2,1)S(1)} %bitcast.294, bf16[4608,1152]{1,0:T(8,128)(2,1)} %get-tuple-element.54), kind=kOutput, calls=%fused_computation.12 | convolution fusion | flops 5483003904 | bytes 25952256 | tf_op jit(solution)/shard_map/dot_general | solution.py:9
  429.1 9.7 %fusion.60 = f32[512,1152]{1,0:T(8,128)S(1)} fusion(bf16[512,4608]{1,0:T(8,128)(2,1)} %fusion.7, bf16[1152,4608]{1,0:T(8,128)(2,1)} %get-tuple-element.53), kind=kOutput, calls=%fused_computation.176 | convolution fusion | flops 5435817984 | bytes 17694720 | tf_op jit(solution)/shard_map/dot_general | solution.py:9
  445.6 4.0 fusion.26
  451.5 10.0 %cross_bwd.1 = (bf16[2,256,1152]{2,1,0:T(8,128)(2,1)S(1)}, f32[2,120,2304]{2,1,0:T(8,128)S(1)}) custom-call(bf16[2,256,1152]{2,1,0:T(8,128)(2,1)S(1)} %bitcast.263, bf16[2,120,2304]{2,1,0:T(8,128)(2,1)S(1)} %copy.96.kv, bf16[2,256,1152]{2,1,0:T(8,128)(2,1)S(1)} %bitcast.266), custom_call_target="tpu_custom_call" | custom-call | flops 1258291200 | bytes 4718592 | tf_op jit(solution)/shard_map/cross_bwd/pallas_call | solution.py:133
  465.4 10.2 %collective-permute-start = (bf16[60,2304]{1,0:T(8,128)(2,1)S(1)}, bf16[60,2304]{1,0:T(8,128)(2,1)}, u32[]{:S(2)}, u32[]{:S(2)}) collective-permute-start(bf16[60,2304]{1,0:T(8,128)(2,1)S(1)} %bitcast.299), channel_id=1, source_target_pairs={{0,1},{1,2},{2,3},{3,0},{4,5},{5,6},{6,7},{7,4},{8,9},{9,10},{10,1... | collective-permute-start | bytes 829448 | tf_op jit(solution)/shard_map/ppermute | solution.py:1679
  476.3 11.6 %collective-permute-start.1 = (bf16[60,2304]{1,0:T(8,128)(2,1)}, bf16[60,2304]{1,0:T(8,128)(2,1)}, u32[]{:S(2)}, u32[]{:S(2)}) collective-permute-start(bf16[60,2304]{1,0:T(8,128)(2,1)} %bitcast.259), channel_id=1, source_target_pairs={{0,2},{1,3},{2,0},{3,1},{4,6},{5,7},{6,4},{7,5},{8,10},{9,11},{10,... | collective-permute-start | bytes 829448 | tf_op jit(solution)/shard_map/ppermute | solution.py:1679
  488.7 12.7 %convolution_convert_fusion.1 = bf16[4608,1152]{1,0:T(8,128)(2,1)} fusion(bf16[512,1152]{1,0:T(8,128)(2,1)} %bitcast.295, f32[512,4608]{1,0:T(8,128)} %fusion.59), kind=kOutput, calls=%fused_computation.1 | convolution fusion | flops 5462360064 | bytes 21233664 | tf_op jit(solution)/shard_map/dot_general | solution.py:10
  501.4 3.3 fusion.12
  504.8 3.4 multiply_reduce_fusion.4
  508.2 3.3 fusion.10
  511.5 3.2 fusion.11
  514.7 8.8 convolution_convert_fusion
  523.5 6.6 fusion
  533.9 3.9 multiply_reduce_fusion.3
  540.5 2.9 convolution_convert_fusion.6
  544.7 3.2 convolution_convert_fusion.3
  549.9 163.6 %attend_back.1 = (f32[11,36,1152]{2,1,0:T(8,128)}, bf16[1024,1728]{1,0:T(8,128)(2,1)}, bf16[4,60,2304]{2,1,0:T(8,128)(2,1)}, bf16[11,2,2,144,1152]{4,3,2,1,0:T(8,128)(2,1)}) custom-call(bf16[2,2,2,144,1152]{4,3,2,1,0:T(8,128)(2,1)} %bitcast.307, bf16[2,2,2,144,1152]{4,3,2,1,0:T(8,128)(2,1)} %bitcast.305, bf16[2,2,2,144,1152]{4,3,2,1,0:T(8,128)(2,1)} %bitcast.306, ...), custom_call_target="tpu_custom_call" | custom-call | flops 34359738368 | bytes 268435456 | tf_op jit(solution)/shard_map/attend_back/pallas_call | solution.py:1425
  715.4 10.6 %fusion.61 = f32[1024,1152]{1,0:T(8,128)} fusion(bf16[1024,1728]{1,0:T(8,128)(2,1)} %get-tuple-element.63, bf16[1152,1728]{1,0:T(8,128)(2,1)} %get-tuple-element.45.refs_4_), kind=kOutput, calls=%fused_computation.177 | convolution fusion | flops 4076863488 | bytes 12238848 | tf_op jit(solution)/shard_map/dot_general | solution.py:9
  726.0 6.6 convolution_convert_fusion.2
  732.6 6.6 copy.105
  740.5 3.7 convolution_convert_fusion.5
  744.2 141.7 %finish.1 = (f32[144,1152]{1,0:T(8,128)}, f32[2,128,1152]{2,1,0:T(8,128)}, f32[2,36,1728]{2,1,0:T(8,128)}, f32[2,256,1152]{2,1,0:T(8,128)}, f32[8,16,1152]{2,1,0...) custom-call(bf16[2,2,2,4,144,1152]{5,4,3,2,1,0:T(8,128)(2,1)} %bitca, ...), custom_call_target="tpu_custom_call" | custom-call | tf_op jit(solution)/shard_map/finish/pallas_call | solution.py:1557
  (302 shorter events, 77.0 us)
Async XLA Ops:
  0.6 7.7 copy-start.49
  16.0 81.1 %copy-start.55 = (f32[36,1152]{1,0:T(8,128)S(1)}, f32[36,1152]{1,0:T(8,128)}, u32[]{:S(2)}) copy-start(f32[36,1152]{1,0:T(8,128)} %param.32) | copy-start | bytes 497668
  96.6 227.0 %copy-start.4 = (f32[16,1152]{1,0:T(8,128)}, f32[16,1152]{1,0:T(8,128)S(1)}, u32[]{:S(2)}) copy-start(f32[16,1152]{1,0:T(8,128)S(1)} %get-tuple-element.43.refs_6_) | copy-start | bytes 221188
  97.1 234.5 %copy-start.58 = (f32[1152]{0:T(1024)}, f32[1152]{0:T(1024)S(1)}, u32[]{:S(2)}) copy-start(f32[1152]{0:T(1024)S(1)} %mul.318) | copy-start | bytes 13828
  97.1 229.7 %copy-start.56 = (f32[2,1152]{1,0:T(2,128)}, f32[2,1152]{1,0:T(2,128)S(1)}, u32[]{:S(2)}) copy-start(f32[2,1152]{1,0:T(2,128)S(1)} %get-tuple-element.160) | copy-start | bytes 27652
  331.2 19.2 %copy-start.13 = (f32[2,256,1152]{2,1,0:T(8,128)}, f32[2,256,1152]{2,1,0:T(8,128)S(1)}, u32[]{:S(2)}) copy-start(f32[2,256,1152]{2,1,0:T(8,128)S(1)} %get-tuple-element.135) | copy-start | bytes 7077892
  334.2 19.1 %slice-start.2 = ((s8[10616832]{0:T(1024)(128)(4,1)}), s8[2228224]{0:T(1024)(128)(4,1)S(1)}, s32[]{:S(2)}) async-start(s8[10616832]{0:T(1024)(128)(4,1)} %bitcast.311), calls=%async_computation.2 | async-start | bytes 4456448
  336.1 14.3 %copy-start.79 = (bf16[1152,1152]{1,0:T(8,128)(2,1)S(1)}, bf16[1152,1152]{1,0:T(8,128)(2,1)}, u32[]{:S(2)}) copy-start(bf16[1152,1152]{1,0:T(8,128)(2,1)} %get-tuple-element.52) | copy-start | bytes 7962628
  336.1 17.2 %slice-start.3 = ((s8[10616832]{0:T(1024)(128)(4,1)}), s8[4194304]{0:T(1024)(128)(4,1)S(1)}, s32[]{:S(2)}) async-start(s8[10616832]{0:T(1024)(128)(4,1)} %bitcast.311), calls=%async_computation.3 | async-start | bytes 8388608
  352.4 88.0 %copy-start.11 = (f32[2,256,1152]{2,1,0:T(8,128)}, f32[2,256,1152]{2,1,0:T(8,128)S(1)}, u32[]{:S(2)}) copy-start(f32[2,256,1152]{2,1,0:T(8,128)S(1)} %get-tuple-element.166) | copy-start | bytes 7077892
  353.3 8.7 copy-start.39
  379.4 6.7 copy-start.41
  395.1 9.6 %copy-start.9 = (bf16[2,256,3456]{2,1,0:T(8,128)(2,1)}, bf16[2,256,3456]{2,1,0:T(8,128)(2,1)S(1)}, u32[]{:S(2)}) copy-start(bf16[2,256,3456]{2,1,0:T(8,128)(2,1)S(1)} %get-tuple-element.58) | copy-start | bytes 10616836
  411.8 17.3 %copy-start.18 = (f32[2,256,1152]{2,1,0:T(8,128)}, f32[2,256,1152]{2,1,0:T(8,128)S(1)}, u32[]{:S(2)}) copy-start(f32[2,256,1152]{2,1,0:T(8,128)S(1)} %get-tuple-element.139) | copy-start | bytes 7077892
  411.9 17.2 %copy-start.43 = (bf16[2,256,1152]{2,1,0:T(8,128)(2,1)}, bf16[2,256,1152]{2,1,0:T(8,128)(2,1)S(1)}, u32[]{:S(2)}) copy-start(bf16[2,256,1152]{2,1,0:T(8,128)(2,1)S(1)} %multiply_convert_fusion.2) | copy-start | bytes 3538948
  440.5 5.1 copy-start.65
  465.4 82.6 %collective-permute-start = (bf16[60,2304]{1,0:T(8,128)(2,1)S(1)}, bf16[60,2304]{1,0:T(8,128)(2,1)}, u32[]{:S(2)}, u32[]{:S(2)}) collective-permute-start(bf16[60,2304]{1,0:T(8,128)(2,1)S(1)} %bitcast.299), channel_id=1, source_target_pairs={{0,1},{1,2},{2,3},{3,0},{4,5},{5,6},{6,7},{7,4},{8,9},{9,10},{10,1... | collective-permute-start | bytes 829448 | tf_op jit(solution)/shard_map/ppermute | solution.py:1679
  476.3 71.6 %collective-permute-start.1 = (bf16[60,2304]{1,0:T(8,128)(2,1)}, bf16[60,2304]{1,0:T(8,128)(2,1)}, u32[]{:S(2)}, u32[]{:S(2)}) collective-permute-start(bf16[60,2304]{1,0:T(8,128)(2,1)} %bitcast.259), channel_id=1, source_target_pairs={{0,2},{1,3},{2,0},{3,1},{4,6},{5,7},{6,4},{7,5},{8,10},{9,11},{10,... | collective-permute-start | bytes 829448 | tf_op jit(solution)/shard_map/ppermute | solution.py:1679
  488.6 59.3 %collective-permute-start.2 = (bf16[60,2304]{1,0:T(8,128)(2,1)}, bf16[60,2304]{1,0:T(8,128)(2,1)}, u32[]{:S(2)}, u32[]{:S(2)}) collective-permute-start(bf16[60,2304]{1,0:T(8,128)(2,1)} %bitcast.258), channel_id=1, source_target_pairs={{0,3},{1,0},{2,1},{3,2},{4,7},{5,4},{6,5},{7,6},{8,11},{9,8},{10,9... | collective-permute-start | bytes 829448 | tf_op jit(solution)/shard_map/ppermute | solution.py:1679
  488.7 12.7 %copy-start.23 = (bf16[1,2,256,1152]{3,2,1,0:T(8,128)(2,1)S(1)}, bf16[1,2,256,1152]{3,2,1,0:T(8,128)(2,1)}, u32[]{:S(2)}) copy-start(bf16[1,2,256,1152]{3,2,1,0:T(8,128)(2,1)} %param.22) | copy-start | bytes 3538948
  508.2 6.5 slice-start
  514.7 8.8 copy-start.10
  514.7 8.8 copy-start.42
  523.5 7.3 copy-start.64
  523.5 7.3 copy-start.70
  523.5 7.3 copy-start.15
  523.5 7.3 copy-start.68
  533.9 5.4 copy-start.57
  540.5 4.2 copy-start.32
  715.4 10.6 %copy-start.6 = (bf16[2,4,128,1152]{3,2,1,0:T(8,128)(2,1)S(1)}, bf16[2,4,128,1152]{3,2,1,0:T(8,128)(2,1)}, u32[]{:S(2)}) copy-start(bf16[2,4,128,1152]{3,2,1,0:T(8,128)(2,1)} %copy-done.5) | copy-start | bytes 7077892
  715.4 10.6 %copy-start.81 = (bf16[1024,1728]{1,0:T(8,128)(2,1)S(1)}, bf16[1024,1728]{1,0:T(8,128)(2,1)}, u32[]{:S(2)}) copy-start(bf16[1024,1728]{1,0:T(8,128)(2,1)} %get-tuple-element.63) | copy-start | bytes 10616836
  732.6 6.6 copy-start.29
  (60 other events, 147.7 us)

commit v3 on v2

--- a/solution.py
+++ b/solution.py
@@ -497,7 +497,7 @@
         block = (BLOCK, WIDE)
         if self.blocks:
             self.landings.update(arrived=shape((self.blocks, 2, 2) + block, BF))
-            self.scratch.update(sums=pltpu.VMEM((RING, 2, 2) + block, BF))
+            self.scratch.update(sums=pltpu.VMEM((min(RING, self.blocks), 2, 2) + block, BF))
             self.scratch.update(other=pltpu.VMEM((2, 2, 2) + block, BF))
             self.scratch.update(two=pltpu.VMEM((self.blocks, 2) + block, BF))
             self.scratch.update(one=pltpu.VMEM((self.blocks,) + block, BF))
@@ -566,7 +566,7 @@
             view = lambda core, o=o, c=c: arrays[o].at[:, :, core, :, pl.ds(c, WIDE)]
             blocks.append(SimpleNamespace(kept=view, sent=view, kind=PIECES, index=k))
         for k, c in enumerate(blocks):
-            c.__dict__.update(sums=refs.sums, other=refs.other, arrived=refs.arrived.at[k], slot=k % RING)
+            c.__dict__.update(sums=refs.sums, other=refs.other, arrived=refs.arrived.at[k], slot=k % min(RING, self.blocks))
             c.__dict__.update(two=refs.two.at[k], one=refs.one.at[k])
         chunks, plain = blocks, chunks
         if self.half:
@@ -714,9 +714,9 @@
         return 2 * (self.p.z % 2) + self.p.core
 
 
-def to_owners(p, blocks, landing, send, recv, do):
+def to_owners(p, blocks, landing, send, recv, do, only=range(4)):
     pairs = Pairs(p)
-    for i in range(4):
+    for i in only:
         if do == WAIT_RECV:
             remote(blocks.at[0], landing.at[i], send.at[0], recv.at[i], pairs.owner(0)).wait_recv()
             continue
@@ -950,7 +950,7 @@
                 return 0
 
             lax.fori_loop(0, patches // 2 // step, tile, 0)
-    to_owners(p, h_blocks, h_slot.at[0], sh, rh, START)
+            to_owners(p, h_blocks, h_slot.at[0], sh, rh, START, [2 * s + k])
     for k in (1, 0):
         copies(k)[0].wait_recv()
         copies(k)[2].start()
@@ -959,9 +959,13 @@
     text_rows = text_in.shape[1]
     for zz in range(sp):
         text_mine[text_rows * zz : text_rows * (zz + 1), :] = text_in[zz]
-    to_owners(p, h_blocks, h_slot.at[0], sh, rh, WAIT_RECV)
-    swap = remote(h_slot.at[0], h_slot.at[1], sx.at[0], rx.at[0], p.flip("core"))
-    swap.start()
+
+    def swap(z):
+        return remote(h_slot.at[0, z], h_slot.at[1, z], sx.at[z], rx.at[z], p.flip("core"))
+
+    for z in range(sp):
+        to_owners(p, h_blocks, h_slot.at[0], sh, rh, WAIT_RECV, [z])
+        swap(z).start()
     for k in range(2):
         copies(k)[1].wait_recv()
         copies(k)[2].wait_recv()
@@ -980,7 +984,8 @@
         total(r).wait_send()
         text_z(r).wait_send()
     to_owners(p, h_blocks, h_slot.at[0], sh, rh, WAIT_SEND)
-    swap.wait()
+    for z in range(sp):
+        swap(z).wait()
 
 
 def front(sp, shards, ada, silu, vectors, text, resid):
@@ -1026,8 +1031,7 @@
         + [dma((sp - 1,))] * 4
         + [dma((7,))] * 2
         + [dma((sp - 1,))] * 2
-        + [dma((4,))] * 2
-        + [dma((1,))] * 2,
+        + [dma((4,))] * 4,
         compiler_params=pltpu.CompilerParams(
             collective_id=4, has_side_effects=True, vmem_limit_bytes=48 * 2**20
         ),
@@ -1035,8 +1039,8 @@
     )(shards, ada, silu, vectors, text, resid)
 
 
-LAG = 2
-FIRST = 5
+LAG = 3
+FIRST = 8
 PER = 2
 
 
@@ -1100,15 +1104,15 @@
 
 
 def attend_kernel(plan, sp, heads, scale, n_out, *refs):
-    shards, down_shard, text_shard, h_slot, qkv_w, text_mine = refs[:6]
-    refs = refs[6:]
+    shards, down_shard, text_shard, h_slot, qkv_w, text_mine, resid, mod, gain = refs[:9]
+    refs = refs[9:]
     outs = refs[:n_out]
-    down, text, qkv, attn, kv = refs[n_out : n_out + 5]
-    refs = refs[n_out + 5 :]
-    landed, block, stack, heads_out, o_send, o_recv, o_full, text_w, kv_part, kv_in = refs[:10]
-    send, recv, zsend, zrecv, dsend, drecv, local_sem, osem, hsend, hrecv = refs[10:20]
+    down, text, qkv, attn, kv_all, branch, cross_in, query, cross, x_two = refs[n_out : n_out + 10]
+    refs = refs[n_out + 10 :]
+    landed, block, stack, heads_out, o_send, o_recv, o_full, text_w, kv_part, kv_in, kv, weights, x_one = refs[:13]
+    send, recv, zsend, zrecv, dsend, drecv, local_sem, osem, hsend, hrecv, wsem = refs[13:24]
     p = Place(sp)
-    along = SumAlong(p, kv_part, kv_in, kv, *refs[20:])
+    along = SumAlong(p, kv_part, kv_in, kv, *refs[24:])
     greet_list([p.flip(b) for b in ("core", "x", "y")] + group(p))
     n = len(plan)
     rows = down_shard.shape[0]
@@ -1160,7 +1164,7 @@
         elif i >= n:
             remote(down_shard, down_own, dsend.at[0], drecv.at[i - n], p.along(1)).wait_recv()
 
-    ahead = 3
+    ahead = 6
     pltpu.make_async_copy(down_shard, down_own, drecv.at[p.z]).start()
     for i in range(ahead):
         launch(i)
@@ -1231,7 +1235,7 @@
         g.finish(1)
         text_load.start()
 
-    krows = kv.shape[1]
+    krows = kv_part.shape[1]
 
     def kv_product():
         text_load.wait()
@@ -1242,33 +1246,87 @@
                 kv_part[z, :, cols] = res[krows * z : krows * (z + 1)].astype(BF)
         along.start()
 
+    slots, patches = resid.shape[:2]
+    hb = T // 8
+    loads = [pltpu.make_async_copy(outs[o], weights.at[o % 2], wsem.at[o]) for o in range(3)]
+
+    def weights_start():
+        for o in range(2):
+            g.finish(2 + o)
+            loads[o].start()
+
+    def after(b):
+        if b == 0:
+            to_homes(p, o_full, attn, hsend, hrecv, WAIT_RECV)
+            loads[0].wait()
+            loads[1].wait()
+        s, r = b // 2, slice(hb * (b % 2), hb * (b % 2 + 1))
+        out = nn(attn[b], weights[0])
+        branch[s, r, :] = out
+        v = resid[s, r, :] + mod[2 * slots + s : 2 * slots + s + 1, :] * out
+        x_one[s, r, :] = v
+        c = v - jnp.mean(v, axis=-1, keepdims=True)
+        n = c * lax.rsqrt(jnp.mean(c * c, axis=-1, keepdims=True) + 1e-06)
+        low = (n * gain[:1, :]).astype(BF)
+        cross_in[s, r, :] = low
+        query[s, r, :] = nn(low, weights[1]).astype(BF)
+
+    def text_end():
+        g.finish(4)
+        loads[2].start()
+        along.end()
+        count = kv_all.shape[1] // sp
+        for s in range(slots):
+            for z in range(sp):
+                kv_all[s, count * z : count * (z + 1), :] = kv[z, count * s : count * (s + 1), :]
+
+    def cross_attention(s):
+        for h in range(2 * heads):
+            c = slice(h * HD, (h + 1) * HD)
+            cv = slice(WIDE + h * HD, WIDE + (h + 1) * HD)
+            scores = nt(query[s, :, c], kv_all[s, :, c])
+            m = jnp.max(scores, axis=-1, keepdims=True)
+            e = jnp.exp((scores - m) * scale)
+            l = jnp.sum(e, axis=-1, keepdims=True)
+            cross[s, :, c] = (nn(e.astype(BF), kv_all[s, :, cv]) / l).astype(BF)
+
+    def cross_project(s):
+        if s == 0:
+            loads[2].wait()
+        for k in range(patches // hb):
+            r = slice(hb * k, hb * (k + 1))
+            x_two[s, r, :] = x_one[s, r, :] + nn(cross[s, r, :], weights[0])
+
     work = [functools.partial(project, i) for i in range(T // tile)]
     work += [text_start, stage]
     work += [functools.partial(head, h) for h in range(heads)]
     work.insert(-5, kv_product)
     work.insert(-2, along.sum)
-    work += [o_out, o_home]
+    idle = lambda: None
+    work += [o_out, o_home, weights_start, idle, idle, idle]
+    work += [functools.partial(after, b) for b in range(4)]
+    work += [text_end, functools.partial(cross_attention, 0), functools.partial(cross_attention, 1)]
+    work += [functools.partial(cross_project, s) for s in range(slots)]
     interleave(FIRST, PER, work, [functools.partial(step, t) for t in range(total + 2 * LAG)])
-    for i in range(2, total):
+    for i in range(5, total):
         g.finish(i)
     for i in range(n):
         for copy in pieces(i):
             copy.wait_send()
     for r in range(1, sp):
         down_z(r).wait_send()
-    to_homes(p, o_full, attn, hsend, hrecv, WAIT_RECV)
     to_homes(p, o_full, attn, hsend, hrecv, WAIT_SEND)
     o_cross().wait_send()
-    along.end()
-
-
-def attend(plan, widths, sp, heads, scale, shards, down_shard, text_shard, h_slot, qkv_w, text_mine):
+
+
+def attend(plan, widths, sp, heads, scale, shards, down_shard, text_shard, h_slot, qkv_w, text_mine, resid, mod, gain):
     n = len(plan)
     total = n + sp + 2
     T = 8 * h_slot.shape[2]
     half = heads * HD
     trows = text_shard.shape[0]
     krows = text_mine.shape[0] // sp
+    slots = resid.shape[0]
     any_space = pl.BlockSpec(memory_space=pl.ANY)
     vmem = pl.BlockSpec(memory_space=pltpu.VMEM)
     dma = pltpu.SemaphoreType.DMA
@@ -1281,10 +1339,15 @@
             shape((8 * trows, 2 * WIDE), BF),
             shape((T, 3 * half), BF),
             shape((4, T // 8, WIDE), BF),
-            shape((sp, krows, 2 * WIDE), BF),
+            shape((slots, sp * krows // slots, 2 * WIDE), BF),
+            shape(resid.shape, F32),
+            shape(resid.shape, BF),
+            shape(resid.shape, BF),
+            shape(resid.shape, BF),
+            shape(resid.shape, F32),
         ],
-        in_specs=[vmem, any_space, any_space, vmem, vmem, vmem],
-        out_specs=[any_space] * (len(widths) + 2) + [vmem] * 3,
+        in_specs=[vmem, any_space, any_space, vmem, vmem, vmem, vmem, vmem, vmem],
+        out_specs=[any_space] * (len(widths) + 2) + [vmem] * 8,
         scratch_shapes=[
             pltpu.VMEM((n, sp, PIECE, WIDE), BF),
             pltpu.VMEM((2, BLOCK, WIDE), BF),
@@ -1296,6 +1359,9 @@
             pltpu.VMEM((8 * trows, 2 * WIDE), BF),
             pltpu.VMEM((sp, krows, 2 * WIDE), BF),
             pltpu.VMEM((sp - 1, krows, 2 * WIDE), BF),
+            pltpu.VMEM((sp, krows, 2 * WIDE), BF),
+            pltpu.VMEM((2, WIDE, WIDE), BF),
+            pltpu.VMEM(resid.shape, F32),
             dma((total, 7)),
             dma((total, 7)),
             dma((n, sp - 1)),
@@ -1306,17 +1372,18 @@
             dma((2,)),
             dma((4,)),
             dma((4,)),
+            dma((3,)),
             dma((sp - 1,)),
             dma((sp - 1,)),
             dma((sp - 1,)),
             dma((sp - 1,)),
         ],
         compiler_params=pltpu.CompilerParams(
-            collective_id=5, has_side_effects=True, vmem_limit_bytes=56 * 2**20
+            collective_id=5, has_side_effects=True, vmem_limit_bytes=60 * 2**20
         ),
         cost_estimate=pl.CostEstimate(flops=2**34, bytes_accessed=2**28, transcendentals=2**23),
         name="attend",
-    )(shards, down_shard, text_shard, h_slot, qkv_w, text_mine)
+    )(shards, down_shard, text_shard, h_slot, qkv_w, text_mine, resid, mod, gain)
 
 
 def split(refs, *counts):
@@ -1330,8 +1397,8 @@
 def attend_back_kernel(make, sp, heads, scale, *refs):
     sums = make()
     n_in = sums.n_in
-    arrays, (go_blocks, qkv, kv_part), results, (g, kv), landings, scratch, rest = split(
-        refs, n_in, 3, len(sums.results), 2, len(sums.landings), len(sums.scratch)
+    arrays, (go_blocks, qkv, kv_part, h_slot), results, (g, kv, gw), landings, scratch, rest = split(
+        refs, n_in, 4, len(sums.results), 3, len(sums.landings), len(sums.scratch)
     )
     names = SimpleNamespace()
     for group_names, group_refs in ((sums.results, results), (sums.landings, landings), (sums.scratch, scratch)):
@@ -1399,8 +1466,13 @@
         c += half
         g[:, c : c + HD] = acc[1, :, :HD].astype(BF)
 
+    def weights(c):
+        cols = slice(c, min(c + 512, g.shape[1]))
+        gw[:, cols] = tn(h_slot[...], g[:, cols]).astype(BF)
+
     part[...] = jnp.zeros(part.shape, BF)
     work = [cut] + [functools.partial(head, h) for h in range(heads)]
+    work += [functools.partial(weights, c) for c in range(0, g.shape[1], 512)]
     work.insert(2, lambda: [copy.start() for copy in shares()])
     interleave(2, 1, work, sums.steps())
     sums.end()
@@ -1410,7 +1482,7 @@
     cross().wait_send()
 
 
-def attend_back(plan, sp, heads, scale, grads, go_blocks, qkv, kv_part):
+def attend_back(plan, sp, heads, scale, grads, go_blocks, qkv, kv_part, h_slot):
     def make():
         sums = Sums(sp, plan, False, 0, 0)
         sums.n_in = len(grads)
@@ -1424,9 +1496,9 @@
     dma = pltpu.SemaphoreType.DMA
     out = pl.pallas_call(
         functools.partial(attend_back_kernel, make, sp, heads, scale),
-        out_shape=list(sums.results.values()) + [jax.ShapeDtypeStruct(a, BF) for a in (qkv.shape, (sp,) + kv_part.shape)] + list(sums.landings.values()),
-        in_specs=[any_space] * len(grads) + [vmem] * 3,
-        out_specs=[vmem] * (len(sums.results) + 2) + [any_space] * len(sums.landings),
+        out_shape=list(sums.results.values()) + [jax.ShapeDtypeStruct(a, BF) for a in (qkv.shape, (sp,) + kv_part.shape, (WIDE, qkv.shape[1]))] + list(sums.landings.values()),
+        in_specs=[any_space] * len(grads) + [vmem] * 4,
+        out_specs=[vmem] * (len(sums.results) + 3) + [any_space] * len(sums.landings),
         scratch_shapes=list(sums.scratch.values())
         + [
             pltpu.VMEM((4, T // 8, WIDE), BF),
@@ -1441,23 +1513,23 @@
             dma((sp - 1,)),
         ],
         compiler_params=pltpu.CompilerParams(
-            collective_id=6, has_side_effects=True, vmem_limit_bytes=60 * 2**20
+            collective_id=6, has_side_effects=True, vmem_limit_bytes=62 * 2**20
         ),
         cost_estimate=pl.CostEstimate(flops=2**35, bytes_accessed=2**28, transcendentals=2**23),
         name="attend_back",
-    )(*sums.arrays(grads), go_blocks, qkv, kv_part)
-    return out[:3]
+    )(*sums.arrays(grads), go_blocks, qkv, kv_part, h_slot)
+    return out[:4]
 
 
 def finish_kernel(make, sp, *refs):
     sums = make()
-    arrays, (gh, resid, grad_one, mod, small), results, (out, small_all), landings, scratch, rest = split(
-        refs, sums.n_in, 5, len(sums.results), 2, len(sums.landings), len(sums.scratch)
+    arrays, (g, qkv_w, resid, grad_one, mod, small), results, (out, small_all), landings, scratch, rest = split(
+        refs, sums.n_in, 6, len(sums.results), 2, len(sums.landings), len(sums.scratch)
     )
     names = SimpleNamespace()
     for group_names, group_refs in ((sums.results, results), (sums.landings, landings), (sums.scratch, scratch)):
         names.__dict__.update(zip(group_names, group_refs))
-    home, gh_in, blocks, mine, mine_in, partial, hsend, hrecv, esem, s1, r1, s2, r2 = rest
+    home, gh, gh_in, blocks, mine, mine_in, partial, hsend, hrecv, esem, s1, r1, s2, r2 = rest
     p = Place(sp)
     near = others(p)
     greet_list(near + group(p))
@@ -1466,9 +1538,16 @@
     def cross():
         return remote(gh.at[1], gh_in, esem.at[0], esem.at[1], p.flip("core"))
 
-    cross().start()
     sums.begin()
     half_rows = gh.shape[2]
+
+    def back(k):
+        for b in range(4):
+            first = (4 * k + b) * half_rows
+            gh[k, b] = nt(g[first : first + half_rows, :], qkv_w[...])
+        if k == 1:
+            cross().start()
+
     slots = resid.shape[0]
 
     def add():
@@ -1530,7 +1609,8 @@
             share(m).start()
 
     idle = lambda: None
-    interleave(1, 1, [add, idle, idle, idle, tail, idle, total], sums.steps())
+    work = [functools.partial(back, 1), functools.partial(back, 0), add, idle, idle, idle, tail, idle, total]
+    interleave(1, 1, work, sums.steps())
     sums.end()
     for m in range(7):
         share(m).wait()
@@ -1540,7 +1620,7 @@
     cross().wait_send()
 
 
-def finish(sp, down, text, halves, gh, resid, grad_one, mod, small):
+def finish(sp, down, text, halves, g, qkv_w, resid, grad_one, mod, small):
     half = halves.shape[1]
 
     def make():
@@ -1549,7 +1629,7 @@
         return sums
 
     sums = make()
-    rows = gh.shape[2]
+    rows = g.shape[0] // 8
     any_space = pl.BlockSpec(memory_space=pl.ANY)
     vmem = pl.BlockSpec(memory_space=pltpu.VMEM)
     dma = pltpu.SemaphoreType.DMA
@@ -1559,11 +1639,12 @@
         out_shape=list(sums.results.values())
         + [shape(resid.shape, F32), shape((8,) + small.shape, F32)]
         + list(sums.landings.values()),
-        in_specs=[any_space] * 3 + [vmem] * 5,
+        in_specs=[any_space] * 3 + [vmem] * 6,
         out_specs=[vmem] * (len(sums.results) + 2) + [any_space] * len(sums.landings),
         scratch_shapes=list(sums.scratch.values())
         + [
             pltpu.VMEM((4, rows, WIDE), BF),
+            pltpu.VMEM((2, 4, rows, WIDE), F32),
             pltpu.VMEM((4, rows, WIDE), F32),
             pltpu.VMEM((4, rows, WIDE), BF),
             pltpu.VMEM(small.shape, F32),
@@ -1578,10 +1659,10 @@
             dma((7,)),
         ],
         compiler_params=pltpu.CompilerParams(
-            collective_id=7, has_side_effects=True, vmem_limit_bytes=60 * 2**20
+            collective_id=7, has_side_effects=True, vmem_limit_bytes=62 * 2**20
         ),
         name="finish",
-    )(*sums.arrays([], down, text, halves), gh, resid, grad_one, mod, small)
+    )(*sums.arrays([], down, text, halves), g, qkv_w, resid, grad_one, mod, small)
     return out[:5]
 
 
@@ -1801,6 +1882,11 @@
             qkv,
             attn_tok,
             kv_all,
+            branch_one,
+            cross_in,
+            query_c,
+            cross_out,
+            x_two,
         ) = attend(
             PLAN,
             [w.shape[1] for w in low],
@@ -1813,14 +1899,12 @@
             h_slot,
             qkv_half,
             text_mine,
+            resid,
+            mod_rows,
+            jnp.broadcast_to(vectors[:1], (TILE, width)),
         )
         h_slot = h_slot.reshape(2 * tok, width)
         attn_tok = attn_tok.reshape(tok, width)
-        kv_all = (
-            kv_all.reshape(sp, slots, text_local, 2 * width)
-            .transpose(1, 0, 2, 3)
-            .reshape(slots, sp * text_local, 2 * width)
-        )
         shift_one, scale_one, gate_one, shift_two, scale_two, gate_two = (modulation[i] for i in range(6))
     else:
         silu_all = lax.all_gather(silu_low, "fsdp", axis=0, tiled=True)
@@ -1863,15 +1947,18 @@
         )
         attn_tok = moves.home(o_full)
     gain_cross, gain_temp, temp_gate = vectors[0], vectors[1], vectors[2]
-    branch_one = nn(attn_tok, out_full).reshape(slots, patches, width)
-    x_one = resid + gate_one * branch_one
-
-    normed_two = normalize(x_one)
-    cross_in = (normed_two * gain_cross).astype(BF).reshape(tok, width)
-    query_c = nn(cross_in, cross_q_full).astype(BF).reshape(slots, patches, width)
-    cross_out = cross_fwd(query_c, kv_all, HEADS, scale).reshape(tok, width)
-    branch_two = nn(cross_out, cross_out_full).reshape(slots, patches, width)
-    x_two = x_one + branch_two
+    if small_slice:
+        x_one = resid + gate_one * branch_one
+        normed_two = normalize(x_one)
+        cross_in, cross_out = cross_in.reshape(tok, width), cross_out.reshape(tok, width)
+    else:
+        branch_one = nn(attn_tok, out_full).reshape(slots, patches, width)
+        x_one = resid + gate_one * branch_one
+        normed_two = normalize(x_one)
+        cross_in = (normed_two * gain_cross).astype(BF).reshape(tok, width)
+        query_c = nn(cross_in, cross_q_full).astype(BF).reshape(slots, patches, width)
+        cross_out = cross_fwd(query_c, kv_all, HEADS, scale).reshape(tok, width)
+        x_two = x_one + nn(cross_out, cross_out_full).reshape(slots, patches, width)
 
     normed_three = normalize(x_two)
     h_three = (normed_three * (1.0 + scale_two) + shift_two).astype(BF).reshape(tok, width)
@@ -1932,7 +2019,7 @@
     grad_attn = nt(grad_b1, out_full).astype(BF)
     if small_slice:
         late = [g.astype(BF) for g in (grad_wout, grad_wcq, grad_wco, grad_wup, grad_wtq, grad_wto)]
-        pieces, grad_qkv, grad_kv = attend_back(
+        pieces, grad_qkv, grad_kv, grad_wqkv_half = attend_back(
             PLAN,
             sp,
             heads_half,
@@ -1941,6 +2028,7 @@
             grad_attn.reshape(sp, tok // sp, width),
             qkv,
             sum_along(grad_kv.reshape(sp, slots * text_local, 2 * width), sp),
+            h_slot,
         )
         grad_kv = grad_kv.reshape(sp * slots * text_local, 2 * width)
         own = [jnp.concatenate([pieces[k] for k, (o, _) in enumerate(PLAN) if o == i], axis=1) for i in range(len(late))]
@@ -1954,9 +2042,8 @@
         grad_kv = lax.all_gather(
             lax.psum_scatter(grad_kv, "sp", scatter_dimension=0, tiled=True), "sp", axis=0, tiled=True
         )
-    grad_wqkv_half = tn(h_slot, grad_qkv).astype(BF)
+        grad_wqkv_half = tn(h_slot, grad_qkv).astype(BF)
     grad_wckv = tn(text_mine, grad_kv)
-    gh_slot = nt(grad_qkv, qkv_half)
     known = [grad_gate_one, grad_shift_two, grad_scale_two, grad_gate_two]
     known_vectors = [grad_gcross, grad_gtemp, grad_tgate]
     if small_slice:
@@ -1966,7 +2053,8 @@
             grad_wdown.astype(BF),
             grad_wckv.astype(BF),
             grad_wqkv_half,
-            gh_slot.reshape(2, sp, tok // sp, width),
+            grad_qkv,
+            qkv_half,
             resid,
             grad_one,
             mod_rows,
@@ -1976,6 +2064,7 @@
         own_half = jnp.where(core == 0, own_half, own_half[::-1])
         own_qkv = own_half.reshape(2, rows, 3, half).transpose(1, 2, 0, 3).reshape(rows, 3 * width)
     else:
+        gh_slot = nt(grad_qkv, qkv_half)
         grad_h_one = moves.home((gh_slot[:tok] + moves.exchange(gh_slot[tok:])).astype(BF))
         grad_h_one = grad_h_one.astype(F32).reshape(slots, patches, width)
         input_grad = grad_one + normalize_back(resid, grad_h_one * (1.0 + scale_one))

time: 905 us -> 841 us (0.929)
  matrix products: 150 us -> 122 us
  starting transfers between devices: 21.8 us -> 6.58 us
  local copies, waits for them, and re-layouts: 47.1 us -> 35.6 us
    ppermute x3, starting transfers between devices: 21.8 us -> 6.58 us  [sum_along(): lax.ppermute(part, 'sp', [(k, (k + r) % sp) for k in range(sp)]).astype(F32)]
    pallas_call x1 -> x0, Pallas kernels: 14.2 us -> none  [cross_fwd(): pl.pallas_call(functools.partial(cross_fwd_kernel, heads, scale), grid=(S...]
    dot_general x8 -> x7, matrix products: 57.1 us -> 45.9 us  [nt(): lax.dot_general(a, b, (((1,), (1,)), ((), ())), preferred_element_type=F32)]
    dot_general x9 -> x8, matrix products: 51.5 us -> 41.8 us  [tn(): lax.dot_general(a, b, (((0,), (0,)), ((), ())), preferred_element_type=F32)]
    dot_general x7 -> x4, matrix products: 39.9 us -> 32.6 us  [nn(): return jnp.dot(a, b, preferred_element_type=F32)]
where the time goes in v3:
time: 841 us; the launch traced here: 836 us
  Pallas kernels  637 us (76%)
  matrix products  122 us (15%)
  local copies, waits for them, and re-layouts  35.6 us (4%)
  other arithmetic  31.6 us (4%)
    pallas_call x1, Pallas kernels, attend(): pl.pallas_call(functools.partial(attend_kernel, plan, sp, heads, scale, l...  234 us
    pallas_call x1, Pallas kernels, attend_back(): pl.pallas_call(functools.partial(attend_back_kernel, make, sp, heads, sca...  167 us
    pallas_call x1, Pallas kernels, finish(): pl.pallas_call(functools.partial(finish_kernel, make, sp), out_shape=list...  140 us
    pallas_call x1, Pallas kernels, front(): pl.pallas_call(functools.partial(front_kernel, sp), out_shape=[shape((8 *...  76.1 us
    dot_general x7, matrix products, nt(): lax.dot_general(a, b, (((1,), (1,)), ((), ())), preferred_element_type=F32)  45.9 us
    dot_general x8, matrix products, tn(): lax.dot_general(a, b, (((0,), (0,)), ((), ())), preferred_element_type=F32)  41.8 us
    dot_general x4, matrix products, nn(): return jnp.dot(a, b, preferred_element_type=F32)  32.6 us
  transfers between devices with their start and end apart: 3, of which 0 were waited for; matrix products, arithmetic and copies ran while one was open for 6% of the time, Pallas kernels for 0%

profile of v3, /device:TPU:0, one launch (start us, length us, event | category | flops | bytes accessed | tf_op | source)
XLA Modules:
  0.0 835.9 jit_solution(15281041610446115501)
XLA Ops:
  2.5 2.3 fusion.51
  8.4 76.1 %front.1 = (bf16[1152,1728]{1,0:T(8,128)(2,1)}, bf16[2,4,128,1152]{3,2,1,0:T(8,128)(2,1)S(1)}, f32[16,1152]{1,0:T(8,128)S(1)}, f32[8,4,8,36]{3,2,1,0:T(8,128)S(1...) custom-call(bf16[2,36,1728]{2,1,0:T(8,128)(2,1)S(1)} %copy.80.shards, ...), custom_call_target="tpu_custom_call" | custom-call | tf_op jit(solution)/shard_map/front/pallas_call | solution.py:1000
  91.4 234.4 %attend.1 = (bf16[1152,1152]{1,0:T(8,128)(2,1)}, bf16[1152,1152]{1,0:T(8,128)(2,1)}, bf16[1152,1152]{1,0:T(8,128)(2,1)}, bf16[1152,4608]{1,0:T(8,128)(2,1)}, bf1...) custom-call(bf16[11,36,1152]{2,1,0:T(8,128)(2,1)} %copy-done.61, ...), custom_call_target="tpu_custom_call" | custom-call | flops 17179869184 | bytes 268435456 | tf_op jit(solution)/shard_map/attend/pallas_call | solution.py:1334
  325.8 2.0 reduce_sum.175
  329.1 9.8 %fusion.55 = f32[512,4608]{1,0:T(8,128)S(1)} fusion(bf16[512,1152]{1,0:T(8,128)(2,1)S(1)} %bitcast.258, bf16[1152,4608]{1,0:T(8,128)(2,1)} %get-tuple-element.55), kind=kOutput, calls=%fused_computation.167 | convolution fusion | flops 5435817984 | bytes 21233664 | tf_op jit(solution)/shard_map/dot_general | solution.py:11
  338.9 8.0 fusion.48
  350.4 2.0 multiply_convert_fusion.3
  352.5 10.4 %convolution_convert_fusion.3 = bf16[512,3456]{1,0:T(8,128)(2,1)} fusion(bf16[512,1152]{1,0:T(8,128)(2,1)S(1)} %bitcast.260, bf16[1152,3456]{1,0:T(8,128)(2,1)} %get-tuple-element.57), kind=kOutput, calls=%fused_computation.23 | convolution fusion | flops 4078632960 | bytes 12681216 | tf_op jit(solution)/shard_map/dot_general | solution.py:11
  365.0 9.1 %temporal.1 = (bf16[2,256,1152]{2,1,0:T(8,128)(2,1)S(1)}, bf16[2,256,3456]{2,1,0:T(8,128)(2,1)S(1)}) custom-call(bf16[2,256,3456]{2,1,0:T(8,128)(2,1)} %bitcast.272, bf16[2,256,1152]{2,1,0:T(8,128)(2,1)S(1)} %bitcast.238), custom_call_target="tpu_custom_call" | custom-call | flops 4294967296 | bytes 16777216 | tf_op jit(solution)/shard_map/temporal/pallas_call | solution.py:1716
  374.1 9.6 %multiply_reduce_fusion.7 = (f32[2,256]{1,0:T(2,128)S(1)}, f32[2,256,1152]{2,1,0:T(8,128)S(1)}) fusion(f32[2,256,1152]{2,1,0:T(8,128)S(1)} %copy-done.12, f32[1152]{0:T(1024)S(1)} %mul.323, f32[2,256]{1,0:T(2,128)S(1)} %broadcast_multiply_fusion.2, bf16[2,256,3456]{2,1,0:T(8,128)(2,1)S(1)} %get-tuple-element.60, bf16[1152,3456]{1,0:T(8,128)(2,1)} %get-tuple-element.57), kind=kOutput, calls=%fused_computation.57 | convolution fusion | flops 4079222272 | bytes 16228864 | tf_op jit(solution)/shard_map/dot_general | solution.py:9
  385.3 4.4 fusion.18
  391.2 15.0 %fusion.7 = bf16[512,4608]{1,0:T(8,128)(2,1)S(1)} fusion(f32[512,4608]{1,0:T(8,128)} %copy-done.68, bf16[512,1152]{1,0:T(8,128)(2,1)S(1)} %bitcast.261, bf16[4608,1152]{1,0:T(8,128)(2,1)} %get-tuple-element.56), kind=kOutput, calls=%fused_computation.12 | convolution fusion | flops 5483003904 | bytes 25952256 | tf_op jit(solution)/shard_map/dot_general | solution.py:9
  406.2 10.8 %fusion.56 = f32[512,1152]{1,0:T(8,128)S(1)} fusion(bf16[512,4608]{1,0:T(8,128)(2,1)S(1)} %fusion.7, bf16[1152,4608]{1,0:T(8,128)(2,1)} %get-tuple-element.55), kind=kOutput, calls=%fused_computation.168 | convolution fusion | flops 5435817984 | bytes 17694720 | tf_op jit(solution)/shard_map/dot_general | solution.py:9
  422.4 4.0 fusion.23
  428.5 10.0 %cross_bwd.1 = (bf16[2,256,1152]{2,1,0:T(8,128)(2,1)S(1)}, f32[2,120,2304]{2,1,0:T(8,128)S(1)}) custom-call(bf16[2,256,1152]{2,1,0:T(8,128)(2,1)S(1)} %copy-done.4, bf16[2,120,2304]{2,1,0:T(8,128)(2,1)S(1)} %copy-done.5, bf16[2,256,1152]{2,1,0:T(8,128)(2,1)S(1)} %bitcast.237), custom_call_target="tpu_custom_call" | custom-call | flops 1258291200 | bytes 4718592 | tf_op jit(solution)/shard_map/cross_bwd/pallas_call | solution.py:133
  440.0 3.1 constant_dynamic-slice_fusion.4
  443.1 4.1 collective-permute-start
  449.8 6.9 fusion
  456.7 8.3 convolution_convert_fusion
  465.1 3.2 fusion.12
  468.3 10.1 %convolution_convert_fusion.1 = bf16[4608,1152]{1,0:T(8,128)(2,1)} fusion(bf16[512,1152]{1,0:T(8,128)(2,1)S(1)} %bitcast.262, f32[512,4608]{1,0:T(8,128)S(1)} %bitcast.282), kind=kOutput, calls=%fused_computation.1 | convolution fusion | flops 5462360064 | bytes 21233664 | tf_op jit(solution)/shard_map/dot_general | solution.py:10
  478.5 2.9 fusion.49
  481.7 2.0 multiply_reduce_fusion.5
  490.4 3.2 fusion.11
  493.6 3.2 fusion.10
  496.9 4.7 convolution_convert_fusion.5
  503.0 3.2 convolution_convert_fusion.2
  506.2 2.0 fusion.26.refs_8_
  508.2 167.4 %attend_back.1 = (f32[11,36,1152]{2,1,0:T(8,128)}, bf16[1024,1728]{1,0:T(8,128)(2,1)}, bf16[4,60,2304]{2,1,0:T(8,128)(2,1)}, bf16[1152,1728]{1,0:T(8,128)(2,1)}, bf16[11,2,2,144,1152]{4,3,2,1,0:T(8,128)(2,1)}) custom-call(bf16[2,2,2,144,1152]{4,3,2,1,0:T(8,128)(2,1)} %bitcast.276, bf16[2,2,2,144,1152]{4,3,2,1,0:T(8,128)(2,1)} %bitcast.275, ...), custom_call_target="tpu_custom_call" | custom-call | flops 34359738368 | bytes 268435456 | tf_op jit(solution)/shard_map/attend_back/pallas_call | solution.py:1497
  675.7 2.8 slice_bitcast_fusion
  678.8 3.5 convolution_convert_fusion.4
  682.3 140.2 %finish.1 = (f32[144,1152]{1,0:T(8,128)}, f32[2,128,1152]{2,1,0:T(8,128)}, f32[2,36,1728]{2,1,0:T(8,128)}, f32[2,256,1152]{2,1,0:T(8,128)}, f32[8,16,1152]{2,1,0...) custom-call(bf16[2,2,2,4,144,1152]{5,4,3,2,1,0:T(8,128)(2,1)} %bitca, ...), custom_call_target="tpu_custom_call" | custom-call | tf_op jit(solution)/shard_map/finish/pallas_call | solution.py:1637
  (274 shorter events, 54.1 us)
Async XLA Ops:
  8.3 79.4 %copy-start.38 = (f32[36,4608]{1,0:T(8,128)S(1)}, f32[36,4608]{1,0:T(8,128)}, u32[]{:S(2)}) copy-start(f32[36,4608]{1,0:T(8,128)} %param.29) | copy-start | bytes 1990660
  8.3 79.5 %copy-start.48 = (f32[36,1152]{1,0:T(8,128)S(1)}, f32[36,1152]{1,0:T(8,128)}, u32[]{:S(2)}) copy-start(f32[36,1152]{1,0:T(8,128)} %param.25) | copy-start | bytes 497668
  8.4 79.5 %copy-start.49 = (f32[36,1152]{1,0:T(8,128)S(1)}, f32[36,1152]{1,0:T(8,128)}, u32[]{:S(2)}) copy-start(f32[36,1152]{1,0:T(8,128)} %param.26) | copy-start | bytes 497668
  8.4 79.5 %copy-start.50 = (f32[36,1152]{1,0:T(8,128)S(1)}, f32[36,1152]{1,0:T(8,128)}, u32[]{:S(2)}) copy-start(f32[36,1152]{1,0:T(8,128)} %param.28) | copy-start | bytes 497668
  328.6 10.3 %slice-start.5 = ((s8[10616832]{0:T(1024)(128)(4,1)}), s8[4194304]{0:T(1024)(128)(4,1)S(1)}, s32[]{:S(2)}) async-start(s8[10616832]{0:T(1024)(128)(4,1)} %bitcast.283), calls=%async_computation.5 | async-start | bytes 8388608
  329.0 9.8 %copy-start.31 = (bf16[2,256,1152]{2,1,0:T(8,128)(2,1)}, bf16[2,256,1152]{2,1,0:T(8,128)(2,1)S(1)}, u32[]{:S(2)}) copy-start(bf16[2,256,1152]{2,1,0:T(8,128)(2,1)S(1)} %add_convert_fusion) | copy-start | bytes 3538948
  329.1 9.8 %slice-start.6 = ((s8[10616832]{0:T(1024)(128)(4,1)}), s8[4194304]{0:T(1024)(128)(4,1)S(1)}, s32[]{:S(2)}) async-start(s8[10616832]{0:T(1024)(128)(4,1)} %bitcast.283), calls=%async_computation.6 | async-start | bytes 8388608
  329.1 9.8 %slice-start.7 = ((s8[10616832]{0:T(1024)(128)(4,1)}), s8[2228224]{0:T(1024)(128)(4,1)S(1)}, s32[]{:S(2)}) async-start(s8[10616832]{0:T(1024)(128)(4,1)} %bitcast.283), calls=%async_computation.7 | async-start | bytes 4456448
  338.9 8.0 copy-start.68
  352.4 10.4 %copy-start.33 = (bf16[2,256,1152]{2,1,0:T(8,128)(2,1)}, bf16[2,256,1152]{2,1,0:T(8,128)(2,1)S(1)}, u32[]{:S(2)}) copy-start(bf16[2,256,1152]{2,1,0:T(8,128)(2,1)S(1)} %multiply_convert_fusion.3) | copy-start | bytes 3538948
  352.5 10.4 %copy-start.21 = (bf16[1,2,256,1152]{3,2,1,0:T(8,128)(2,1)S(1)}, bf16[1,2,256,1152]{3,2,1,0:T(8,128)(2,1)}, u32[]{:S(2)}) copy-start(bf16[1,2,256,1152]{3,2,1,0:T(8,128)(2,1)} %param.22) | copy-start | bytes 3538948
  352.5 10.6 %copy-start.23 = (bf16[1152,1152]{1,0:T(8,128)(2,1)S(1)}, bf16[1152,1152]{1,0:T(8,128)(2,1)}, u32[]{:S(2)}) copy-start(bf16[1152,1152]{1,0:T(8,128)(2,1)} %get-tuple-element.58) | copy-start | bytes 7962628
  365.0 9.1 %copy-start.12 = (f32[2,256,1152]{2,1,0:T(8,128)S(1)}, f32[2,256,1152]{2,1,0:T(8,128)}, u32[]{:S(2)}) copy-start(f32[2,256,1152]{2,1,0:T(8,128)} %copy-done.11) | copy-start | bytes 7077892
  374.1 9.6 %copy-start.6 = (bf16[2,256,3456]{2,1,0:T(8,128)(2,1)}, bf16[2,256,3456]{2,1,0:T(8,128)(2,1)S(1)}, u32[]{:S(2)}) copy-start(bf16[2,256,3456]{2,1,0:T(8,128)(2,1)S(1)} %get-tuple-element.60) | copy-start | bytes 10616836
  389.9 16.3 %copy-start.35 = (bf16[2,256,1152]{2,1,0:T(8,128)(2,1)}, bf16[2,256,1152]{2,1,0:T(8,128)(2,1)S(1)}, u32[]{:S(2)}) copy-start(bf16[2,256,1152]{2,1,0:T(8,128)(2,1)S(1)} %multiply_convert_fusion.2) | copy-start | bytes 3538948
  406.2 10.8 %copy-start.67 = (bf16[512,4608]{1,0:T(8,128)(2,1)}, bf16[512,4608]{1,0:T(8,128)(2,1)S(1)}, u32[]{:S(2)}) copy-start(bf16[512,4608]{1,0:T(8,128)(2,1)S(1)} %fusion.7) | copy-start | bytes 14155780
  406.2 10.8 %copy-start.9 = (f32[2,256,1152]{2,1,0:T(8,128)S(1)}, f32[2,256,1152]{2,1,0:T(8,128)}, u32[]{:S(2)}) copy-start(f32[2,256,1152]{2,1,0:T(8,128)} %get-tuple-element.54) | copy-start | bytes 7077892
  439.9 9.8 %copy-start.7 = (bf16[2,256,3456]{2,1,0:T(8,128)(2,1)S(1)}, bf16[2,256,3456]{2,1,0:T(8,128)(2,1)}, u32[]{:S(2)}) copy-start(bf16[2,256,3456]{2,1,0:T(8,128)(2,1)} %copy-done.6) | copy-start | bytes 10616836
  443.0 6.7 copy-start.34
  443.1 63.1 %collective-permute-start = (bf16[60,2304]{1,0:T(8,128)(2,1)S(1)}, bf16[60,2304]{1,0:T(8,128)(2,1)}, u32[]{:S(2)}, u32[]{:S(2)}) collective-permute-start(bf16[60,2304]{1,0:T(8,128)(2,1)S(1)} %bitcast.266), channel_id=1, source_target_pairs={{0,1},{1,2},{2,3},{3,0},{4,5},{5,6},{6,7},{7,4},{8,9},{9,10},{10,1... | collective-permute-start | bytes 829448 | tf_op jit(solution)/shard_map/ppermute | solution.py:1760
  447.2 59.0 %collective-permute-start.1 = (bf16[60,2304]{1,0:T(8,128)(2,1)S(1)}, bf16[60,2304]{1,0:T(8,128)(2,1)}, u32[]{:S(2)}, u32[]{:S(2)}) collective-permute-start(bf16[60,2304]{1,0:T(8,128)(2,1)S(1)} %bitcast.267), channel_id=1, source_target_pairs={{0,2},{1,3},{2,0},{3,1},{4,6},{5,7},{6,4},{7,5},{8,10},{9,11},{10,... | collective-permute-start | bytes 829448 | tf_op jit(solution)/shard_map/ppermute | solution.py:1760
  448.6 8.1 slice-start
  448.6 8.1 copy-start.32
  448.6 8.1 slice-start.1
  448.6 57.6 %collective-permute-start.2 = (bf16[60,2304]{1,0:T(8,128)(2,1)S(1)}, bf16[60,2304]{1,0:T(8,128)(2,1)}, u32[]{:S(2)}, u32[]{:S(2)}) collective-permute-start(bf16[60,2304]{1,0:T(8,128)(2,1)S(1)} %bitcast.268), channel_id=1, source_target_pairs={{0,3},{1,0},{2,1},{3,2},{4,7},{5,4},{6,5},{7,6},{8,11},{9,8},{10,9... | collective-permute-start | bytes 829448 | tf_op jit(solution)/shard_map/ppermute | solution.py:1760
  456.7 8.4 %copy-start.22 = (bf16[1,2,256,1152]{3,2,1,0:T(8,128)(2,1)S(1)}, bf16[1,2,256,1152]{3,2,1,0:T(8,128)(2,1)}, u32[]{:S(2)}) copy-start(bf16[1,2,256,1152]{3,2,1,0:T(8,128)(2,1)} %param.22) | copy-start | bytes 3538948
  456.7 11.6 %slice-start.2 = ((s8[9437184]{0:T(1024)(128)(4,1)}), s8[1048576]{0:T(1024)(128)(4,1)S(1)}, s32[]{:S(2)}) async-start(s8[9437184]{0:T(1024)(128)(4,1)} %bitcast.281), calls=%async_computation.2 | async-start | bytes 2097152
  456.7 11.6 %slice-start.3 = ((s8[9437184]{0:T(1024)(128)(4,1)}), s8[4194304]{0:T(1024)(128)(4,1)S(1)}, s32[]{:S(2)}) async-start(s8[9437184]{0:T(1024)(128)(4,1)} %bitcast.281), calls=%async_computation.3 | async-start | bytes 8388608
  468.3 10.2 %copy-start.54 = (f32[2,1152]{1,0:T(2,128)S(1)}, f32[2,1152]{1,0:T(2,128)}, u32[]{:S(2)}) copy-start(f32[2,1152]{1,0:T(2,128)} %get-tuple-element.171) | copy-start | bytes 27652
  487.9 5.7 copy-start.17
  496.9 4.8 copy-start.55
  496.9 6.1 copy-start.65
  (51 other events, 121.9 us)

commit v4 on v3

--- a/solution.py
+++ b/solution.py
@@ -789,9 +789,10 @@
     full,
     h_slot,
     modulation,
-    vectors_all,
+    vector_rows,
     text_mine,
     silu_in,
+    vectors_all,
     landed,
     block,
     parts,
@@ -979,6 +980,7 @@
         vec_f(m).wait_send()
         part(m).wait_send()
         cond(m).wait_send()
+    vector_rows[...] = jnp.concatenate([vectors_all[f, z] for f in range(8) for z in range(sp)], axis=1)
     for r in range(1, sp):
         vec_z(r).wait_send()
         total(r).wait_send()
@@ -1003,13 +1005,14 @@
             shape((8 * BLOCK, half), BF),
             shape((2, 4, patches // 2, WIDE), BF),
             shape((MOD_ROWS, WIDE), F32),
-            shape((8, sp, TILE, lanes), F32),
+            shape((TILE, 8 * sp * lanes), F32),
             shape((sp * text_rows, depth), BF),
             shape((8, TILE, lanes), F32),
         ],
         in_specs=[vmem] * 6,
         out_specs=[any_space] + [vmem] * 5,
         scratch_shapes=[
+            pltpu.VMEM((8, sp, TILE, lanes), F32),
             pltpu.VMEM((2, sp, PIECE, half), BF),
             pltpu.VMEM((2, BLOCK, half), BF),
             pltpu.VMEM((8, MOD_ROWS, WIDE), F32),
@@ -1867,7 +1870,6 @@
         )
         silu_rows = silu_rows[:, :slots].reshape(fsdp * slots, rows).astype(BF)
         modulation = mod_rows[: 6 * slots].reshape(6, slots, 1, width)
-        vectors = vectors[:, :, :3].transpose(2, 0, 1, 3).reshape(3, width)
         low = [w.astype(BF) for w in (w_out, w_cross_q, w_cross_out, w_up, w_temp_qkv, w_temp_out)]
         shards = jnp.stack([low[o][:, c : c + width] for o, c in PLAN])
         (
@@ -1901,7 +1903,7 @@
             text_mine,
             resid,
             mod_rows,
-            jnp.broadcast_to(vectors[:1], (TILE, width)),
+            vectors,
         )
         h_slot = h_slot.reshape(2 * tok, width)
         attn_tok = attn_tok.reshape(tok, width)

time: 841 us -> 847 us (level)
  no operation moved by 1% of the time
where the time goes in v4:
time: 847 us; the launch traced here: 841 us
  Pallas kernels  636 us (75%)
  matrix products  129 us (15%)
  local copies, waits for them, and re-layouts  35.2 us (4%)
  other arithmetic  31.2 us (4%)
    pallas_call x1, Pallas kernels, attend(): pl.pallas_call(functools.partial(attend_kernel, plan, sp, heads, scale, l...  234 us
    pallas_call x1, Pallas kernels, attend_back(): pl.pallas_call(functools.partial(attend_back_kernel, make, sp, heads, sca...  167 us
    pallas_call x1, Pallas kernels, finish(): pl.pallas_call(functools.partial(finish_kernel, make, sp), out_shape=list...  140 us
    pallas_call x1, Pallas kernels, front(): pl.pallas_call(functools.partial(front_kernel, sp), out_shape=[shape((8 *...  76.1 us
    dot_general x7, matrix products, nt(): lax.dot_general(a, b, (((1,), (1,)), ((), ())), preferred_element_type=F32)  45.8 us
    dot_general x8, matrix products, tn(): lax.dot_general(a, b, (((0,), (0,)), ((), ())), preferred_element_type=F32)  41.9 us
    dot_general x4, matrix products, nn(): return jnp.dot(a, b, preferred_element_type=F32)  39.6 us
  transfers between devices with their start and end apart: 3, of which 0 were waited for; matrix products, arithmetic and copies ran while one was open for 6% of the time, Pallas kernels for 0%

profile of v4, /device:TPU:0, one launch (start us, length us, event | category | flops | bytes accessed | tf_op | source)
XLA Modules:
  0.0 841.3 jit_solution(14700097713698394398)
XLA Ops:
  2.5 2.3 fusion.50
  12.6 76.1 %front.1 = (bf16[1152,1728]{1,0:T(8,128)(2,1)}, bf16[2,4,128,1152]{3,2,1,0:T(8,128)(2,1)S(1)}, f32[16,1152]{1,0:T(8,128)S(1)}, f32[8,1152]{1,0:T(8,128)S(1)}, bf...) custom-call(bf16[2,36,1728]{2,1,0:T(8,128)(2,1)S(1)} %copy.80.shards, ...), custom_call_target="tpu_custom_call" | custom-call | tf_op jit(solution)/shard_map/front/pallas_call | solution.py:1002
  93.0 234.4 %attend.1 = (bf16[1152,1152]{1,0:T(8,128)(2,1)}, bf16[1152,1152]{1,0:T(8,128)(2,1)}, bf16[1152,1152]{1,0:T(8,128)(2,1)}, bf16[1152,4608]{1,0:T(8,128)(2,1)}, bf1...) custom-call(bf16[11,36,1152]{2,1,0:T(8,128)(2,1)} %copy-done.58, ...), custom_call_target="tpu_custom_call" | custom-call | flops 17179869184 | bytes 268435456 | tf_op jit(solution)/shard_map/attend/pallas_call | solution.py:1337
  327.4 2.0 reduce_sum.175
  330.7 9.5 %fusion.54 = f32[512,4608]{1,0:T(8,128)S(1)} fusion(bf16[512,1152]{1,0:T(8,128)(2,1)S(1)} %bitcast.256, bf16[1152,4608]{1,0:T(8,128)(2,1)} %get-tuple-element.55), kind=kOutput, calls=%fused_computation.165 | convolution fusion | flops 5435817984 | bytes 21233664 | tf_op jit(solution)/shard_map/dot_general | solution.py:11
  340.2 15.4 %fusion.47 = f32[512,1152]{1,0:T(8,128)S(1)} fusion(bf16[4608,1152]{1,0:T(8,128)(2,1)} %get-tuple-element.56, f32[512,4608]{1,0:T(8,128)S(1)} %fusion.54), kind=kOutput, calls=%fused_computation.160 | convolution fusion | flops 5457051648 | bytes 22413312 | tf_op jit(solution)/shard_map/dot_general | solution.py:11
  358.3 10.3 %convolution_convert_fusion.3 = bf16[512,3456]{1,0:T(8,128)(2,1)} fusion(bf16[512,1152]{1,0:T(8,128)(2,1)S(1)} %bitcast.258, bf16[1152,3456]{1,0:T(8,128)(2,1)} %get-tuple-element.57), kind=kOutput, calls=%fused_computation.23 | convolution fusion | flops 4078632960 | bytes 12681216 | tf_op jit(solution)/shard_map/dot_general | solution.py:11
  370.7 8.9 %temporal.1 = (bf16[2,256,1152]{2,1,0:T(8,128)(2,1)S(1)}, bf16[2,256,3456]{2,1,0:T(8,128)(2,1)S(1)}) custom-call(bf16[2,256,3456]{2,1,0:T(8,128)(2,1)} %bitcast.270, bf16[2,256,1152]{2,1,0:T(8,128)(2,1)S(1)} %bitcast.236), custom_call_target="tpu_custom_call" | custom-call | flops 4294967296 | bytes 16777216 | tf_op jit(solution)/shard_map/temporal/pallas_call | solution.py:1719
  379.7 9.5 %multiply_reduce_fusion.7 = (f32[2,256]{1,0:T(2,128)S(1)}, f32[2,256,1152]{2,1,0:T(8,128)S(1)}) fusion(f32[2,256,1152]{2,1,0:T(8,128)S(1)} %get-tuple-element.149, f32[1152]{0:T(1024)S(1)} %get-tuple-element.138, f32[2,256]{1,0:T(2,128)S(1)} %broadcast_multiply_fusion.2, bf16[2,256,3456]{2,1,0:T(8,128)(2,1)S(1)} %get-tuple-element.60, ...), kind=kOutput, calls=%fused_computation.57 | convolution fusion | flops 4079222272 | bytes 16228864 | tf_op jit(solution)/shard_map/dot_general | solution.py:9
  391.0 4.4 fusion.18
  396.8 15.0 %fusion.7 = bf16[512,4608]{1,0:T(8,128)(2,1)S(1)} fusion(f32[512,4608]{1,0:T(8,128)} %copy-done.65, bf16[512,1152]{1,0:T(8,128)(2,1)S(1)} %bitcast.259, bf16[4608,1152]{1,0:T(8,128)(2,1)} %get-tuple-element.56), kind=kOutput, calls=%fused_computation.12 | convolution fusion | flops 5483003904 | bytes 25952256 | tf_op jit(solution)/shard_map/dot_general | solution.py:9
  411.8 10.8 %fusion.55 = f32[512,1152]{1,0:T(8,128)S(1)} fusion(bf16[512,4608]{1,0:T(8,128)(2,1)S(1)} %fusion.7, bf16[1152,4608]{1,0:T(8,128)(2,1)} %get-tuple-element.55), kind=kOutput, calls=%fused_computation.166 | convolution fusion | flops 5435817984 | bytes 17694720 | tf_op jit(solution)/shard_map/dot_general | solution.py:9
  424.2 2.0 add_add_fusion.1
  428.1 4.0 fusion.23
  434.2 10.0 %cross_bwd.1 = (bf16[2,256,1152]{2,1,0:T(8,128)(2,1)S(1)}, f32[2,120,2304]{2,1,0:T(8,128)S(1)}) custom-call(bf16[2,256,1152]{2,1,0:T(8,128)(2,1)S(1)} %copy-done.5, bf16[2,120,2304]{2,1,0:T(8,128)(2,1)S(1)} %copy-done.6, bf16[2,256,1152]{2,1,0:T(8,128)(2,1)S(1)} %bitcast.235), custom_call_target="tpu_custom_call" | custom-call | flops 1258291200 | bytes 4718592 | tf_op jit(solution)/shard_map/cross_bwd/pallas_call | solution.py:133
  445.6 3.1 constant_dynamic-slice_fusion.4
  448.8 4.0 collective-permute-start
  455.4 6.9 fusion
  462.3 8.3 convolution_convert_fusion
  470.7 3.2 fusion.12
  473.9 10.2 %convolution_convert_fusion.1 = bf16[4608,1152]{1,0:T(8,128)(2,1)} fusion(bf16[512,1152]{1,0:T(8,128)(2,1)S(1)} %bitcast.260, f32[512,4608]{1,0:T(8,128)S(1)} %bitcast.280), kind=kOutput, calls=%fused_computation.1 | convolution fusion | flops 5462360064 | bytes 21233664 | tf_op jit(solution)/shard_map/dot_general | solution.py:10
  484.2 2.9 fusion.48
  487.4 2.0 multiply_reduce_fusion.5
  496.1 3.2 fusion.11
  499.3 3.3 fusion.10
  502.7 4.7 convolution_convert_fusion.5
  508.7 3.2 convolution_convert_fusion.2
  512.0 2.0 fusion.26.refs_8_
  513.9 167.1 %attend_back.1 = (f32[11,36,1152]{2,1,0:T(8,128)}, bf16[1024,1728]{1,0:T(8,128)(2,1)}, bf16[4,60,2304]{2,1,0:T(8,128)(2,1)}, bf16[1152,1728]{1,0:T(8,128)(2,1)}, bf16[11,2,2,144,1152]{4,3,2,1,0:T(8,128)(2,1)}) custom-call(bf16[2,2,2,144,1152]{4,3,2,1,0:T(8,128)(2,1)} %bitcast.274, bf16[2,2,2,144,1152]{4,3,2,1,0:T(8,128)(2,1)} %bitcast.273, ...), custom_call_target="tpu_custom_call" | custom-call | flops 34359738368 | bytes 268435456 | tf_op jit(solution)/shard_map/attend_back/pallas_call | solution.py:1500
  681.1 2.8 slice_bitcast_fusion
  684.2 3.6 convolution_convert_fusion.4
  687.8 140.0 %finish.1 = (f32[144,1152]{1,0:T(8,128)}, f32[2,128,1152]{2,1,0:T(8,128)}, f32[2,36,1728]{2,1,0:T(8,128)}, f32[2,256,1152]{2,1,0:T(8,128)}, f32[8,16,1152]{2,1,0...) custom-call(bf16[2,2,2,4,144,1152]{5,4,3,2,1,0:T(8,128)(2,1)} %bitca, ...), custom_call_target="tpu_custom_call" | custom-call | tf_op jit(solution)/shard_map/finish/pallas_call | solution.py:1640
  (256 shorter events, 53.2 us)
Async XLA Ops:
  11.8 80.3 %copy-start.48 = (f32[36,1152]{1,0:T(8,128)S(1)}, f32[36,1152]{1,0:T(8,128)}, u32[]{:S(2)}) copy-start(f32[36,1152]{1,0:T(8,128)} %param.32) | copy-start | bytes 497668
  330.7 9.5 %copy-start.29 = (bf16[2,256,1152]{2,1,0:T(8,128)(2,1)}, bf16[2,256,1152]{2,1,0:T(8,128)(2,1)S(1)}, u32[]{:S(2)}) copy-start(bf16[2,256,1152]{2,1,0:T(8,128)(2,1)S(1)} %add_convert_fusion) | copy-start | bytes 3538948
  340.2 15.4 %copy-start.65 = (f32[512,4608]{1,0:T(8,128)}, f32[512,4608]{1,0:T(8,128)S(1)}, u32[]{:S(2)}) copy-start(f32[512,4608]{1,0:T(8,128)S(1)} %fusion.54) | copy-start | bytes 28311556
  358.3 10.3 %copy-start.31 = (bf16[2,256,1152]{2,1,0:T(8,128)(2,1)}, bf16[2,256,1152]{2,1,0:T(8,128)(2,1)S(1)}, u32[]{:S(2)}) copy-start(bf16[2,256,1152]{2,1,0:T(8,128)(2,1)S(1)} %multiply_convert_fusion.3) | copy-start | bytes 3538948
  358.3 10.3 %copy-start.18 = (bf16[1,2,256,1152]{3,2,1,0:T(8,128)(2,1)S(1)}, bf16[1,2,256,1152]{3,2,1,0:T(8,128)(2,1)}, u32[]{:S(2)}) copy-start(bf16[1,2,256,1152]{3,2,1,0:T(8,128)(2,1)} %param.22) | copy-start | bytes 3538948
  358.3 10.5 %copy-start.20 = (bf16[1152,1152]{1,0:T(8,128)(2,1)S(1)}, bf16[1152,1152]{1,0:T(8,128)(2,1)}, u32[]{:S(2)}) copy-start(bf16[1152,1152]{1,0:T(8,128)(2,1)} %get-tuple-element.58) | copy-start | bytes 7962628
  379.6 9.6 %copy-start.7 = (bf16[2,256,3456]{2,1,0:T(8,128)(2,1)}, bf16[2,256,3456]{2,1,0:T(8,128)(2,1)S(1)}, u32[]{:S(2)}) copy-start(bf16[2,256,3456]{2,1,0:T(8,128)(2,1)S(1)} %get-tuple-element.60) | copy-start | bytes 10616836
  395.5 16.3 %copy-start.33 = (bf16[2,256,1152]{2,1,0:T(8,128)(2,1)}, bf16[2,256,1152]{2,1,0:T(8,128)(2,1)S(1)}, u32[]{:S(2)}) copy-start(bf16[2,256,1152]{2,1,0:T(8,128)(2,1)S(1)} %multiply_convert_fusion.2) | copy-start | bytes 3538948
  411.8 10.8 %copy-start.64 = (bf16[512,4608]{1,0:T(8,128)(2,1)}, bf16[512,4608]{1,0:T(8,128)(2,1)S(1)}, u32[]{:S(2)}) copy-start(bf16[512,4608]{1,0:T(8,128)(2,1)S(1)} %fusion.7) | copy-start | bytes 14155780
  411.8 10.8 %copy-start.10 = (f32[2,256,1152]{2,1,0:T(8,128)S(1)}, f32[2,256,1152]{2,1,0:T(8,128)}, u32[]{:S(2)}) copy-start(f32[2,256,1152]{2,1,0:T(8,128)} %get-tuple-element.54) | copy-start | bytes 7077892
  424.2 3.9 copy-start.53
  428.1 4.0 copy-start.55
  428.1 4.0 copy-start.68
  445.6 9.8 %copy-start.8 = (bf16[2,256,3456]{2,1,0:T(8,128)(2,1)S(1)}, bf16[2,256,3456]{2,1,0:T(8,128)(2,1)}, u32[]{:S(2)}) copy-start(bf16[2,256,3456]{2,1,0:T(8,128)(2,1)} %copy-done.7) | copy-start | bytes 10616836
  448.7 6.7 copy-start.32
  448.8 63.2 %collective-permute-start = (bf16[60,2304]{1,0:T(8,128)(2,1)S(1)}, bf16[60,2304]{1,0:T(8,128)(2,1)}, u32[]{:S(2)}, u32[]{:S(2)}) collective-permute-start(bf16[60,2304]{1,0:T(8,128)(2,1)S(1)} %bitcast.264), channel_id=1, source_target_pairs={{0,1},{1,2},{2,3},{3,0},{4,5},{5,6},{6,7},{7,4},{8,9},{9,10},{10,1... | collective-permute-start | bytes 829448 | tf_op jit(solution)/shard_map/ppermute | solution.py:1763
  452.9 59.1 %collective-permute-start.1 = (bf16[60,2304]{1,0:T(8,128)(2,1)S(1)}, bf16[60,2304]{1,0:T(8,128)(2,1)}, u32[]{:S(2)}, u32[]{:S(2)}) collective-permute-start(bf16[60,2304]{1,0:T(8,128)(2,1)S(1)} %bitcast.265), channel_id=1, source_target_pairs={{0,2},{1,3},{2,0},{3,1},{4,6},{5,7},{6,4},{7,5},{8,10},{9,11},{10,... | collective-permute-start | bytes 829448 | tf_op jit(solution)/shard_map/ppermute | solution.py:1763
  454.3 8.0 slice-start
  454.3 8.0 copy-start.30
  454.3 8.0 slice-start.1
  454.3 57.6 %collective-permute-start.2 = (bf16[60,2304]{1,0:T(8,128)(2,1)S(1)}, bf16[60,2304]{1,0:T(8,128)(2,1)}, u32[]{:S(2)}, u32[]{:S(2)}) collective-permute-start(bf16[60,2304]{1,0:T(8,128)(2,1)S(1)} %bitcast.266), channel_id=1, source_target_pairs={{0,3},{1,0},{2,1},{3,2},{4,7},{5,4},{6,5},{7,6},{8,11},{9,8},{10,9... | collective-permute-start | bytes 829448 | tf_op jit(solution)/shard_map/ppermute | solution.py:1763
  462.3 8.4 copy-start.19
  462.3 11.6 %slice-start.2 = ((s8[9437184]{0:T(1024)(128)(4,1)}), s8[1048576]{0:T(1024)(128)(4,1)S(1)}, s32[]{:S(2)}) async-start(s8[9437184]{0:T(1024)(128)(4,1)} %bitcast.279), calls=%async_computation.2 | async-start | bytes 2097152
  462.3 11.6 %slice-start.3 = ((s8[9437184]{0:T(1024)(128)(4,1)}), s8[4194304]{0:T(1024)(128)(4,1)S(1)}, s32[]{:S(2)}) async-start(s8[9437184]{0:T(1024)(128)(4,1)} %bitcast.279), calls=%async_computation.3 | async-start | bytes 8388608
  473.9 10.3 %copy-start.49 = (f32[2,1152]{1,0:T(2,128)S(1)}, f32[2,1152]{1,0:T(2,128)}, u32[]{:S(2)}) copy-start(f32[2,1152]{1,0:T(2,128)} %get-tuple-element.171) | copy-start | bytes 27652
  493.6 5.7 copy-start.16
  502.6 4.8 copy-start.50
  502.6 4.8 copy-start.51
  502.7 6.1 copy-start.62
  833.3 3.7 copy-start.38
  833.3 4.5 copy-start.37
  834.7 4.0 copy-start.22
  (45 other events, 95.9 us)
